TPU v7x, 512 devices: a whole 4x8x8 slice. The times are simulated.
512 devices in a mesh: tm: 4 (over x), lat: 8 (over y), lon: 16 (over z, core).
Axes of the slice: x: 4, y: 8, z: 8, core: 2. Of those that a mesh axis runs over, the one named last changes fastest.
Arguments:
- start: float32 [4, 48, 128, 2048], P('tm', None, 'lat', 'lon'), may hold values from -6 to 6
- wet: int32 [128, 2048], P('lat', 'lon'), may hold values 0 or 1
- kappa: float32 [128, 2048], P('lat', 'lon'), may hold values from 0.06 to 0.24
- mixing: float32 [48, 48], replicated, may hold values from -0.12 to 0.12
Outputs:
- corrected_end: float32 [4, 48, 128, 2048], P('tm', None, 'lat', 'lon')
- next_start: float32 [4, 48, 128, 2048], P('tm', None, 'lat', 'lon')
All inputs are finite; a program needn't handle non-finite values. No bound on the sum of `wet` on one device may be relied on, other than what follows from the above.
Results may differ from a plain program's by a relative error of at most 0.00018.
Values sent between devices are 32-bit elements; how exact they have to be, the bound alone decides.
No kernel may reach another device: no remote copies, remote signals or barrier semaphores. Data moves between devices by JAX's collectives and lax.ppermute only.
A program may use at most 64 MiB of HBM per device.

v0:
```python
import jax
import jax.numpy as jnp
from jax import lax
from jax.sharding import PartitionSpec as P


def with_halo(value, sides, width):
    for axis, dim in sides:
        devices, length = (lax.axis_size(axis), value.shape[dim])
        up = [(i, (i + 1) % devices) for i in range(devices)]
        down = [(j, i) for i, j in up]
        last = lax.slice_in_dim(value, length - width, length, axis=dim)
        leading = lax.slice_in_dim(value, 0, width, axis=dim)
        before = lax.ppermute(last, axis, up)
        after = lax.ppermute(leading, axis, down)
        value = jnp.concatenate([before, value, after], axis=dim)
    return value


def from_behind(value, axis, by):
    devices = lax.axis_size(axis)
    pairs = [(i, i + by) for i in range(devices) if 0 <= i + by < devices]
    return lax.ppermute(value, axis, pairs)


def mesh_spacing(
    bordered_field, mask_bordered, diffusivity_bordered, vertical_matrix, laplacian_scale
):
    middle_value = bordered_field[:, 1:-1, 1:-1]
    mask_mid = mask_bordered[1:-1, 1:-1]
    kap_mid = diffusivity_bordered[1:-1, 1:-1]
    parts = [
        (bordered_field[:, :-2, 1:-1], mask_bordered[:-2, 1:-1], diffusivity_bordered[:-2, 1:-1]),
        (bordered_field[:, 2:, 1:-1], mask_bordered[2:, 1:-1], diffusivity_bordered[2:, 1:-1]),
        (bordered_field[:, 1:-1, :-2], mask_bordered[1:-1, :-2], diffusivity_bordered[1:-1, :-2]),
        (bordered_field[:, 1:-1, 2:], mask_bordered[1:-1, 2:], diffusivity_bordered[1:-1, 2:]),
    ]
    lap = None
    for other, mask_other, kap_other in parts:
        term = 0.5 * (kap_mid + kap_other) * (mask_mid * mask_other) * (other - middle_value)
        lap = term if lap is None else lap + term
    depth_layers = middle_value.shape[0]
    vertical_term = jnp.dot(
        vertical_matrix, middle_value.reshape(depth_layers, -1), precision=lax.Precision.HIGHEST
    ).reshape(middle_value.shape)
    return mask_mid * (middle_value + laplacian_scale * lap + vertical_term)


def block_sum(field):
    rows, cols = (field.shape[-2], field.shape[-1])
    shaped = field.reshape(field.shape[:-2] + (rows // 2, 2, cols // 2, 2))
    return jnp.sum(shaped, axis=(-3, -1))


def prolong(field):
    return jnp.repeat(jnp.repeat(field, 2, axis=-2), 2, axis=-1)


def body(start, wet, kappa, mixing):
    first = start[0]
    rows_dev, cols_dev = wet.shape
    lat_pos = lax.axis_index("lat")
    lat_count = lax.axis_size("lat")
    slot = lax.axis_index("tm")
    slot_count = lax.axis_size("tm")
    mask = wet.astype(jnp.float32)
    stacked = jnp.stack([mask, kappa])
    coefs = with_halo(stacked, (("lat", 1), ("lon", 2)), 3)
    row_ids = lax.broadcasted_iota(jnp.int32, (rows_dev + 6, 1), 0)
    outside = (lat_pos == 0) & (row_ids < 3) | (lat_pos == lat_count - 1) & (
        row_ids >= rows_dev + 3
    )
    coefs = coefs * jnp.where(outside, 0.0, 1.0).astype(jnp.float32)
    mask_wide, kap_wide = (coefs[0], coefs[1])
    count_wide = block_sum(mask_wide[1:-1, 1:-1])
    cmask_pad = jnp.minimum(count_wide, 1.0)
    ckap_pad = block_sum(kap_wide[1:-1, 1:-1]) * 0.25
    divisor = jnp.maximum(count_wide[1:-1, 1:-1], 1.0)
    coarse_mix = 3.0 * mixing

    def restrict(field):
        return block_sum(mask * field) / divisor

    def coarse(field):
        bordered_field = with_halo(field, (("lat", 1), ("lon", 2)), 1)
        return mesh_spacing(bordered_field, cmask_pad, ckap_pad, coarse_mix, 0.75)

    field = first
    for step in range(3):
        bordered_field = with_halo(field, (("lat", 1), ("lon", 2)), 1)
        field = mesh_spacing(
            bordered_field, mask_wide[2:-2, 2:-2], kap_wide[2:-2, 2:-2], mixing, 1.0
        )
    coarse_end = restrict(field)
    jump = jnp.where(slot == 0, coarse_end, coarse_end - coarse(restrict(first)))
    every = lax.all_gather(jump[None], "tm", axis=0, tiled=True)
    state = every[0]
    mine = state
    for section in range(1, slot_count):
        state = coarse(state) + every[section]
        mine = jnp.where(slot == section, state, mine)
    corrected = field + mask * prolong(mine - coarse_end)
    shifted = from_behind(corrected, "tm", 1)
    following = jnp.where(slot == 0, first, shifted)
    return (corrected[None], following[None])


def solution(mesh):
    in_specs = (P("tm", None, "lat", "lon"), P("lat", "lon"), P("lat", "lon"), P())
    out_specs = (P("tm", None, "lat", "lon"), P("tm", None, "lat", "lon"))
    return jax.shard_map(body, mesh=mesh, in_specs=in_specs, out_specs=out_specs, check_vma=False)
```

profile of v0, /device:TPU:10, one launch (start us, length us, event | category | flops | bytes accessed | tf_op | source)
XLA Modules:
  0.0 168.6 jit_solution(17697303716429965197)
XLA Ops:
  1.4 3.5 %collective-permute-start = (f32[2,3,128]{2,1,0:T(4,128)S(1)}, f32[2,3,128]{2,1,0:T(4,128)S(1)}, u32[]{:S(2)}, u32[]{:S(2)}) collective-permute-start(f32[2,3,128]{2,1,0:T(4,128)S(1)} %get-tuple-element.51), channel_id=1, source_target_pairs={{0,16},{16,32},{32,48},{48,64},{64,80},{80,96},{96,112},{112,0},{1... | collective-permute-start | bytes 9224 | tf_op jit(solution)/shard_map/ppermute | solution.py:14
  8.5 3.5 %collective-permute-start.4 = (f32[48,1,128]{2,0,1:T(8,128)S(1)}, f32[48,1,128]{2,0,1:T(8,128)S(1)}, u32[]{:S(2)}, u32[]{:S(2)}) collective-permute-start(f32[48,1,128]{2,0,1:T(8,128)S(1)} %get-tuple-element.22), channel_id=1, source_target_pairs={{0,16},{16,32},{32,48},{48,64},{64,80},{80,96},{96,112},{112,0},{1... | collective-permute-start | bytes 73736 | tf_op jit(solution)/shard_map/ppermute | solution.py:14
  16.7 7.8 %collective-permute-start.3 = (f32[2,22,3]{2,1,0:T(8,128)S(1)}, f32[2,22,3]{2,1,0:T(8,128)S(1)}, u32[]{:S(2)}, u32[]{:S(2)}) collective-permute-start(f32[2,22,3]{2,1,0:T(8,128)S(1)} %get-tuple-element.46), channel_id=1, source_target_pairs={{1,0},{2,1},{3,2},{4,3},{5,4},{6,5},{7,6},{8,7},{9,8},{10,9},{11,1... | collective-permute-start | bytes 1592 | tf_op jit(solution)/shard_map/ppermute | solution.py:15
  27.7 4.9 %collective-permute-start.17 = (f32[48,1,64]{2,0,1:T(8,128)S(1)}, f32[48,1,64]{2,0,1:T(8,128)S(1)}, u32[]{:S(2)}, u32[]{:S(2)}) collective-permute-start(f32[48,1,64]{2,0,1:T(8,128)S(1)} %get-tuple-element.37), channel_id=1, source_target_pairs={{16,0},{32,16},{48,32},{64,48},{80,64},{96,80},{112,96},{0,112},{1... | collective-permute-start | bytes 36872 | tf_op jit(solution)/shard_map/ppermute | solution.py:15
  34.8 2.9 %collective-permute-start.7 = (f32[48,18,1]{2,0,1:T(8,128)S(1)}, f32[48,18,1]{2,0,1:T(8,128)}, u32[]{:S(2)}, u32[]{:S(2)}) collective-permute-start(f32[48,18,1]{2,0,1:T(8,128)S(1)} %get-tuple-element.17), channel_id=1, source_target_pairs={{1,0},{2,1},{3,2},{4,3},{5,4},{6,5},{7,6},{8,7},{9,8},{10,9},{11,1... | collective-permute-start | bytes 10376 | tf_op jit(solution)/shard_map/ppermute | solution.py:15
  38.5 5.2 %collective-permute-done.6 = f32[48,18,1]{2,0,1:T(8,128)S(1)} collective-permute-done((f32[48,18,1]{2,0,1:T(8,128)S(1)}, f32[48,18,1]{2,0,1:T(8,128)S(1)}, u32[]{:S(2)}, u32[]{:S(2)}) %collective-permute-start.6) | collective-permute-done | bytes 3488 | tf_op jit(solution)/shard_map/ppermute | solution.py:14
  45.4 3.9 %collective-permute-start.8 = (f32[48,1,128]{2,0,1:T(8,128)S(1)}, f32[48,1,128]{2,0,1:T(8,128)S(1)}, u32[]{:S(2)}, u32[]{:S(2)}) collective-permute-start(f32[48,1,128]{2,0,1:T(8,128)S(1)} %get-tuple-element.20), channel_id=1, source_target_pairs={{0,16},{16,32},{32,48},{48,64},{64,80},{80,96},{96,112},{112,0},{1... | collective-permute-start | bytes 73736 | tf_op jit(solution)/shard_map/ppermute | solution.py:14
  51.3 4.9 %collective-permute-done.9 = f32[48,1,128]{2,0,1:T(8,128)S(1)} collective-permute-done((f32[48,1,128]{2,0,1:T(8,128)S(1)}, f32[48,1,128]{2,0,1:T(8,128)S(1)}, u32[]{:S(2)}, u32[]{:S(2)}) %collective-permute-start.9) | collective-permute-done | bytes 24608 | tf_op jit(solution)/shard_map/ppermute | solution.py:15
  56.5 2.9 %collective-permute-start.11 = (f32[48,18,1]{2,0,1:T(8,128)S(1)}, f32[48,18,1]{2,0,1:T(8,128)S(1)}, u32[]{:S(2)}, u32[]{:S(2)}) collective-permute-start(f32[48,18,1]{2,0,1:T(8,128)S(1)} %get-tuple-element.15), channel_id=1, source_target_pairs={{1,0},{2,1},{3,2},{4,3},{5,4},{6,5},{7,6},{8,7},{9,8},{10,9},{11,1... | collective-permute-start | bytes 10376 | tf_op jit(solution)/shard_map/ppermute | solution.py:15
  59.9 5.5 %collective-permute-done.10 = f32[48,18,1]{2,0,1:T(8,128)S(1)} collective-permute-done((f32[48,18,1]{2,0,1:T(8,128)S(1)}, f32[48,18,1]{2,0,1:T(8,128)S(1)}, u32[]{:S(2)}, u32[]{:S(2)}) %collective-permute-start.10) | collective-permute-done | bytes 3488 | tf_op jit(solution)/shard_map/ppermute | solution.py:14
  65.9 3.9 %collective-permute-start.12 = (f32[48,1,128]{2,0,1:T(8,128)S(1)}, f32[48,1,128]{2,0,1:T(8,128)S(1)}, u32[]{:S(2)}, u32[]{:S(2)}) collective-permute-start(f32[48,1,128]{2,0,1:T(8,128)S(1)} %get-tuple-element.18), channel_id=1, source_target_pairs={{0,16},{16,32},{32,48},{48,64},{64,80},{80,96},{96,112},{112,0},{1... | collective-permute-start | bytes 73736 | tf_op jit(solution)/shard_map/ppermute | solution.py:14
  76.7 2.9 %collective-permute-start.15 = (f32[48,18,1]{2,0,1:T(8,128)S(1)}, f32[48,18,1]{2,0,1:T(8,128)S(1)}, u32[]{:S(2)}, u32[]{:S(2)}) collective-permute-start(f32[48,18,1]{2,0,1:T(8,128)S(1)} %get-tuple-element.13), channel_id=1, source_target_pairs={{1,0},{2,1},{3,2},{4,3},{5,4},{6,5},{7,6},{8,7},{9,8},{10,9},{11,1... | collective-permute-start | bytes 10376 | tf_op jit(solution)/shard_map/ppermute | solution.py:15
  80.1 5.5 %collective-permute-done.14 = f32[48,18,1]{2,0,1:T(8,128)S(1)} collective-permute-done((f32[48,18,1]{2,0,1:T(8,128)S(1)}, f32[48,18,1]{2,0,1:T(8,128)S(1)}, u32[]{:S(2)}, u32[]{:S(2)}) %collective-permute-start.14) | collective-permute-done | bytes 3488 | tf_op jit(solution)/shard_map/ppermute | solution.py:14
  89.5 13.4 %all-gather = f32[192,8,64]{2,0,1:T(8,128)S(1)} all-gather(f32[48,8,64]{2,0,1:T(8,128)S(1)} %fusion.10), channel_id=2, replica_groups=mesh['tm'=4,'lat'=8,'lon'=16] {'tm'}, dimensions={0}, use_global_device_ids=true | all-gather | bytes 491520 | tf_op jit(solution)/shard_map/all_gather | solution.py:96
  102.9 4.8 %collective-permute-start.20 = (f32[48,1,64]{2,0,1:T(8,128)S(1)}, f32[48,1,64]{2,0,1:T(8,128)S(1)}, u32[]{:S(2)}, u32[]{:S(2)}) collective-permute-start(f32[48,1,64]{2,0,1:T(8,128)S(1)} %get-tuple-element.10), channel_id=1, source_target_pairs={{0,16},{16,32},{32,48},{48,64},{64,80},{80,96},{96,112},{112,0},{1... | collective-permute-start | bytes 36872 | tf_op jit(solution)/shard_map/ppermute | solution.py:14
  109.7 3.8 %collective-permute-done.21 = f32[48,1,64]{2,0,1:T(8,128)S(1)} collective-permute-done((f32[48,1,64]{2,0,1:T(8,128)S(1)}, f32[48,1,64]{2,0,1:T(8,128)S(1)}, u32[]{:S(2)}, u32[]{:S(2)}) %collective-permute-start.21) | collective-permute-done | bytes 12320 | tf_op jit(solution)/shard_map/ppermute | solution.py:15
  113.6 2.9 %collective-permute-start.23 = (f32[48,10,1]{2,0,1:T(8,128)S(1)}, f32[48,10,1]{2,0,1:T(8,128)}, u32[]{:S(2)}, u32[]{:S(2)}) collective-permute-start(f32[48,10,1]{2,0,1:T(8,128)S(1)} %get-tuple-element.29), channel_id=1, source_target_pairs={{1,0},{2,1},{3,2},{4,3},{5,4},{6,5},{7,6},{8,7},{9,8},{10,9},{11,1... | collective-permute-start | bytes 5768 | tf_op jit(solution)/shard_map/ppermute | solution.py:15
  116.8 3.6 %collective-permute-done.22 = f32[48,10,1]{2,0,1:T(8,128)S(1)} collective-permute-done((f32[48,10,1]{2,0,1:T(8,128)S(1)}, f32[48,10,1]{2,0,1:T(8,128)S(1)}, u32[]{:S(2)}, u32[]{:S(2)}) %collective-permute-start.22) | collective-permute-done | bytes 1952 | tf_op jit(solution)/shard_map/ppermute | solution.py:14
  124.3 3.2 %collective-permute-start.25 = (f32[48,1,64]{2,0,1:T(8,128)S(1)}, f32[48,1,64]{2,0,1:T(8,128)S(1)}, u32[]{:S(2)}, u32[]{:S(2)}) collective-permute-start(f32[48,1,64]{2,0,1:T(8,128)S(1)} %get-tuple-element.35), channel_id=1, source_target_pairs={{16,0},{32,16},{48,32},{64,48},{80,64},{96,80},{112,96},{0,112},{1... | collective-permute-start | bytes 36872 | tf_op jit(solution)/shard_map/ppermute | solution.py:15
  133.8 3.6 %collective-permute-done.26 = f32[48,10,1]{2,0,1:T(8,128)S(1)} collective-permute-done((f32[48,10,1]{2,0,1:T(8,128)S(1)}, f32[48,10,1]{2,0,1:T(8,128)S(1)}, u32[]{:S(2)}, u32[]{:S(2)}) %collective-permute-start.26) | collective-permute-done | bytes 1952 | tf_op jit(solution)/shard_map/ppermute | solution.py:14
  138.8 3.9 %collective-permute-start.28 = (f32[48,1,64]{2,0,1:T(8,128)S(1)}, f32[48,1,64]{2,0,1:T(8,128)S(1)}, u32[]{:S(2)}, u32[]{:S(2)}) collective-permute-start(f32[48,1,64]{2,0,1:T(8,128)S(1)} %get-tuple-element.32), channel_id=1, source_target_pairs={{0,16},{16,32},{32,48},{48,64},{64,80},{80,96},{96,112},{112,0},{1... | collective-permute-start | bytes 36872 | tf_op jit(solution)/shard_map/ppermute | solution.py:14
  144.6 3.8 %collective-permute-done.29 = f32[48,1,64]{2,0,1:T(8,128)S(1)} collective-permute-done((f32[48,1,64]{2,0,1:T(8,128)S(1)}, f32[48,1,64]{2,0,1:T(8,128)S(1)}, u32[]{:S(2)}, u32[]{:S(2)}) %collective-permute-start.29) | collective-permute-done | bytes 12320 | tf_op jit(solution)/shard_map/ppermute | solution.py:15
  151.8 3.7 %collective-permute-done.30 = f32[48,10,1]{2,0,1:T(8,128)} collective-permute-done((f32[48,10,1]{2,0,1:T(8,128)S(1)}, f32[48,10,1]{2,0,1:T(8,128)}, u32[]{:S(2)}, u32[]{:S(2)}) %collective-permute-start.30) | collective-permute-done | bytes 1952 | tf_op jit(solution)/shard_map/ppermute | solution.py:14
  161.1 6.4 %collective-permute-done.32 = f32[48,16,128]{2,0,1:T(8,128)S(1)} collective-permute-done((f32[48,16,128]{2,0,1:T(8,128)S(1)}, f32[48,16,128]{2,0,1:T(8,128)S(1)}, u32[]{:S(2)}, u32[]{:S(2)}) %collective-permute-start.32) | collective-permute-done | bytes 393248 | tf_op jit(solution)/shard_map/ppermute | solution.py:23
  (131 shorter events, 56.5 us)
Async XLA Ops:
  1.4 15.3 %collective-permute-start = (f32[2,3,128]{2,1,0:T(4,128)S(1)}, f32[2,3,128]{2,1,0:T(4,128)S(1)}, u32[]{:S(2)}, u32[]{:S(2)}) collective-permute-start(f32[2,3,128]{2,1,0:T(4,128)S(1)} %get-tuple-element.51), channel_id=1, source_target_pairs={{0,16},{16,32},{32,48},{48,64},{64,80},{80,96},{96,112},{112,0},{1... | collective-permute-start | bytes 9224 | tf_op jit(solution)/shard_map/ppermute | solution.py:14
  4.9 11.8 %collective-permute-start.1 = (f32[2,3,128]{2,1,0:T(4,128)S(1)}, f32[2,3,128]{2,1,0:T(4,128)S(1)}, u32[]{:S(2)}, u32[]{:S(2)}) collective-permute-start(f32[2,3,128]{2,1,0:T(4,128)S(1)} %get-tuple-element.52), channel_id=1, source_target_pairs={{16,0},{32,16},{48,32},{64,48},{80,64},{96,80},{112,96},{0,112},{1... | collective-permute-start | bytes 9224 | tf_op jit(solution)/shard_map/ppermute | solution.py:15
  8.5 26.0 %collective-permute-start.4 = (f32[48,1,128]{2,0,1:T(8,128)S(1)}, f32[48,1,128]{2,0,1:T(8,128)S(1)}, u32[]{:S(2)}, u32[]{:S(2)}) collective-permute-start(f32[48,1,128]{2,0,1:T(8,128)S(1)} %get-tuple-element.22), channel_id=1, source_target_pairs={{0,16},{16,32},{32,48},{48,64},{64,80},{80,96},{96,112},{112,0},{1... | collective-permute-start | bytes 73736 | tf_op jit(solution)/shard_map/ppermute | solution.py:14
  12.0 22.5 %collective-permute-start.5 = (f32[48,1,128]{2,0,1:T(8,128)S(1)}, f32[48,1,128]{2,0,1:T(8,128)S(1)}, u32[]{:S(2)}, u32[]{:S(2)}) collective-permute-start(f32[48,1,128]{2,0,1:T(8,128)S(1)} %get-tuple-element.23), channel_id=1, source_target_pairs={{16,0},{32,16},{48,32},{64,48},{80,64},{96,80},{112,96},{0,112},{1... | collective-permute-start | bytes 73736 | tf_op jit(solution)/shard_map/ppermute | solution.py:15
  16.7 9.3 %collective-permute-start.2 = (f32[2,22,3]{2,1,0:T(8,128)S(1)}, f32[2,22,3]{2,1,0:T(8,128)S(1)}, u32[]{:S(2)}, u32[]{:S(2)}) collective-permute-start(f32[2,22,3]{2,1,0:T(8,128)S(1)} %get-tuple-element.45), channel_id=1, source_target_pairs={{0,1},{1,2},{2,3},{3,4},{4,5},{5,6},{6,7},{7,8},{8,9},{9,10},{10,1... | collective-permute-start | bytes 1592 | tf_op jit(solution)/shard_map/ppermute | solution.py:14
  16.7 9.3 %collective-permute-start.3 = (f32[2,22,3]{2,1,0:T(8,128)S(1)}, f32[2,22,3]{2,1,0:T(8,128)S(1)}, u32[]{:S(2)}, u32[]{:S(2)}) collective-permute-start(f32[2,22,3]{2,1,0:T(8,128)S(1)} %get-tuple-element.46), channel_id=1, source_target_pairs={{1,0},{2,1},{3,2},{4,3},{5,4},{6,5},{7,6},{8,7},{9,8},{10,9},{11,1... | collective-permute-start | bytes 1592 | tf_op jit(solution)/shard_map/ppermute | solution.py:15
  27.7 23.6 %collective-permute-start.17 = (f32[48,1,64]{2,0,1:T(8,128)S(1)}, f32[48,1,64]{2,0,1:T(8,128)S(1)}, u32[]{:S(2)}, u32[]{:S(2)}) collective-permute-start(f32[48,1,64]{2,0,1:T(8,128)S(1)} %get-tuple-element.37), channel_id=1, source_target_pairs={{16,0},{32,16},{48,32},{64,48},{80,64},{96,80},{112,96},{0,112},{1... | collective-permute-start | bytes 36872 | tf_op jit(solution)/shard_map/ppermute | solution.py:15
  32.6 18.7 %collective-permute-start.16 = (f32[48,1,64]{2,0,1:T(8,128)S(1)}, f32[48,1,64]{2,0,1:T(8,128)S(1)}, u32[]{:S(2)}, u32[]{:S(2)}) collective-permute-start(f32[48,1,64]{2,0,1:T(8,128)S(1)} %get-tuple-element.36), channel_id=1, source_target_pairs={{0,16},{16,32},{32,48},{48,64},{64,80},{80,96},{96,112},{112,0},{1... | collective-permute-start | bytes 36872 | tf_op jit(solution)/shard_map/ppermute | solution.py:14
  34.7 8.9 %collective-permute-start.6 = (f32[48,18,1]{2,0,1:T(8,128)S(1)}, f32[48,18,1]{2,0,1:T(8,128)S(1)}, u32[]{:S(2)}, u32[]{:S(2)}) collective-permute-start(f32[48,18,1]{2,0,1:T(8,128)S(1)} %get-tuple-element.16), channel_id=1, source_target_pairs={{0,1},{1,2},{2,3},{3,4},{4,5},{5,6},{6,7},{7,8},{8,9},{9,10},{10,1... | collective-permute-start | bytes 10376 | tf_op jit(solution)/shard_map/ppermute | solution.py:14
  34.8 8.9 %collective-permute-start.7 = (f32[48,18,1]{2,0,1:T(8,128)S(1)}, f32[48,18,1]{2,0,1:T(8,128)}, u32[]{:S(2)}, u32[]{:S(2)}) collective-permute-start(f32[48,18,1]{2,0,1:T(8,128)S(1)} %get-tuple-element.17), channel_id=1, source_target_pairs={{1,0},{2,1},{3,2},{4,3},{5,4},{6,5},{7,6},{8,7},{9,8},{10,9},{11,1... | collective-permute-start | bytes 10376 | tf_op jit(solution)/shard_map/ppermute | solution.py:15
  49.3 6.9 %collective-permute-start.9 = (f32[48,1,128]{2,0,1:T(8,128)S(1)}, f32[48,1,128]{2,0,1:T(8,128)S(1)}, u32[]{:S(2)}, u32[]{:S(2)}) collective-permute-start(f32[48,1,128]{2,0,1:T(8,128)S(1)} %get-tuple-element.21), channel_id=1, source_target_pairs={{16,0},{32,16},{48,32},{64,48},{80,64},{96,80},{112,96},{0,112},{1... | collective-permute-start | bytes 73736 | tf_op jit(solution)/shard_map/ppermute | solution.py:15
  56.5 8.9 %collective-permute-start.10 = (f32[48,18,1]{2,0,1:T(8,128)S(1)}, f32[48,18,1]{2,0,1:T(8,128)S(1)}, u32[]{:S(2)}, u32[]{:S(2)}) collective-permute-start(f32[48,18,1]{2,0,1:T(8,128)S(1)} %get-tuple-element.14), channel_id=1, source_target_pairs={{0,1},{1,2},{2,3},{3,4},{4,5},{5,6},{6,7},{7,8},{8,9},{9,10},{10,1... | collective-permute-start | bytes 10376 | tf_op jit(solution)/shard_map/ppermute | solution.py:14
  56.5 8.9 %collective-permute-start.11 = (f32[48,18,1]{2,0,1:T(8,128)S(1)}, f32[48,18,1]{2,0,1:T(8,128)S(1)}, u32[]{:S(2)}, u32[]{:S(2)}) collective-permute-start(f32[48,18,1]{2,0,1:T(8,128)S(1)} %get-tuple-element.15), channel_id=1, source_target_pairs={{1,0},{2,1},{3,2},{4,3},{5,4},{6,5},{7,6},{8,7},{9,8},{10,9},{11,1... | collective-permute-start | bytes 10376 | tf_op jit(solution)/shard_map/ppermute | solution.py:15
  65.9 9.0 %collective-permute-start.12 = (f32[48,1,128]{2,0,1:T(8,128)S(1)}, f32[48,1,128]{2,0,1:T(8,128)S(1)}, u32[]{:S(2)}, u32[]{:S(2)}) collective-permute-start(f32[48,1,128]{2,0,1:T(8,128)S(1)} %get-tuple-element.18), channel_id=1, source_target_pairs={{0,16},{16,32},{32,48},{48,64},{64,80},{80,96},{96,112},{112,0},{1... | collective-permute-start | bytes 73736 | tf_op jit(solution)/shard_map/ppermute | solution.py:14
  71.9 15.5 %collective-permute-start.18 = (f32[48,10,1]{2,0,1:T(8,128)S(1)}, f32[48,10,1]{2,0,1:T(8,128)}, u32[]{:S(2)}, u32[]{:S(2)}) collective-permute-start(f32[48,10,1]{2,0,1:T(8,128)S(1)} %get-tuple-element.30), channel_id=1, source_target_pairs={{0,1},{1,2},{2,3},{3,4},{4,5},{5,6},{6,7},{7,8},{8,9},{9,10},{10,1... | collective-permute-start | bytes 5768 | tf_op jit(solution)/shard_map/ppermute | solution.py:14
  71.9 15.5 %collective-permute-start.19 = (f32[48,10,1]{2,0,1:T(8,128)S(1)}, f32[48,10,1]{2,0,1:T(8,128)}, u32[]{:S(2)}, u32[]{:S(2)}) collective-permute-start(f32[48,10,1]{2,0,1:T(8,128)S(1)} %get-tuple-element.31), channel_id=1, source_target_pairs={{1,0},{2,1},{3,2},{4,3},{5,4},{6,5},{7,6},{8,7},{9,8},{10,9},{11,1... | collective-permute-start | bytes 5768 | tf_op jit(solution)/shard_map/ppermute | solution.py:15
  76.7 8.9 %collective-permute-start.14 = (f32[48,18,1]{2,0,1:T(8,128)S(1)}, f32[48,18,1]{2,0,1:T(8,128)S(1)}, u32[]{:S(2)}, u32[]{:S(2)}) collective-permute-start(f32[48,18,1]{2,0,1:T(8,128)S(1)} %get-tuple-element.12), channel_id=1, source_target_pairs={{0,1},{1,2},{2,3},{3,4},{4,5},{5,6},{6,7},{7,8},{8,9},{9,10},{10,1... | collective-permute-start | bytes 10376 | tf_op jit(solution)/shard_map/ppermute | solution.py:14
  76.7 8.9 %collective-permute-start.15 = (f32[48,18,1]{2,0,1:T(8,128)S(1)}, f32[48,18,1]{2,0,1:T(8,128)S(1)}, u32[]{:S(2)}, u32[]{:S(2)}) collective-permute-start(f32[48,18,1]{2,0,1:T(8,128)S(1)} %get-tuple-element.13), channel_id=1, source_target_pairs={{1,0},{2,1},{3,2},{4,3},{5,4},{6,5},{7,6},{8,7},{9,8},{10,9},{11,1... | collective-permute-start | bytes 10376 | tf_op jit(solution)/shard_map/ppermute | solution.py:15
  113.6 6.8 %collective-permute-start.22 = (f32[48,10,1]{2,0,1:T(8,128)S(1)}, f32[48,10,1]{2,0,1:T(8,128)S(1)}, u32[]{:S(2)}, u32[]{:S(2)}) collective-permute-start(f32[48,10,1]{2,0,1:T(8,128)S(1)} %get-tuple-element.28), channel_id=1, source_target_pairs={{0,1},{1,2},{2,3},{3,4},{4,5},{5,6},{6,7},{7,8},{8,9},{9,10},{10,1... | collective-permute-start | bytes 5768 | tf_op jit(solution)/shard_map/ppermute | solution.py:14
  113.6 6.8 %collective-permute-start.23 = (f32[48,10,1]{2,0,1:T(8,128)S(1)}, f32[48,10,1]{2,0,1:T(8,128)}, u32[]{:S(2)}, u32[]{:S(2)}) collective-permute-start(f32[48,10,1]{2,0,1:T(8,128)S(1)} %get-tuple-element.29), channel_id=1, source_target_pairs={{1,0},{2,1},{3,2},{4,3},{5,4},{6,5},{7,6},{8,7},{9,8},{10,9},{11,1... | collective-permute-start | bytes 5768 | tf_op jit(solution)/shard_map/ppermute | solution.py:15
  130.6 6.8 %collective-permute-start.26 = (f32[48,10,1]{2,0,1:T(8,128)S(1)}, f32[48,10,1]{2,0,1:T(8,128)S(1)}, u32[]{:S(2)}, u32[]{:S(2)}) collective-permute-start(f32[48,10,1]{2,0,1:T(8,128)S(1)} %get-tuple-element.26), channel_id=1, source_target_pairs={{0,1},{1,2},{2,3},{3,4},{4,5},{5,6},{6,7},{7,8},{8,9},{9,10},{10,1... | collective-permute-start | bytes 5768 | tf_op jit(solution)/shard_map/ppermute | solution.py:14
  148.6 7.0 %collective-permute-start.30 = (f32[48,10,1]{2,0,1:T(8,128)S(1)}, f32[48,10,1]{2,0,1:T(8,128)}, u32[]{:S(2)}, u32[]{:S(2)}) collective-permute-start(f32[48,10,1]{2,0,1:T(8,128)S(1)} %get-tuple-element.24), channel_id=1, source_target_pairs={{0,1},{1,2},{2,3},{3,4},{4,5},{5,6},{6,7},{7,8},{8,9},{9,10},{10,1... | collective-permute-start | bytes 5768 | tf_op jit(solution)/shard_map/ppermute | solution.py:14
  148.6 6.9 %collective-permute-start.31 = (f32[48,10,1]{2,0,1:T(8,128)S(1)}, f32[48,10,1]{2,0,1:T(8,128)}, u32[]{:S(2)}, u32[]{:S(2)}) collective-permute-start(f32[48,10,1]{2,0,1:T(8,128)S(1)} %get-tuple-element.25), channel_id=1, source_target_pairs={{1,0},{2,1},{3,2},{4,3},{5,4},{6,5},{7,6},{8,7},{9,8},{10,9},{11,1... | collective-permute-start | bytes 5768 | tf_op jit(solution)/shard_map/ppermute | solution.py:15
  157.9 9.7 %collective-permute-start.32 = (f32[48,16,128]{2,0,1:T(8,128)S(1)}, f32[48,16,128]{2,0,1:T(8,128)S(1)}, u32[]{:S(2)}, u32[]{:S(2)}) collective-permute-start(f32[48,16,128]{2,0,1:T(8,128)S(1)} %multiply_add_fusion), channel_id=1, source_target_pairs={{0,128},{128,256},{256,384},{1,129},{129,257},{257,385},{2,130},{1... | collective-permute-start | bytes 1179656 | tf_op jit(solution)/shard_map/ppermute | solution.py:23
  (14 other events, 72.4 us)
where the time goes:
time: 169 us
  starting transfers between devices  79.6 us (47%)
  waiting for transfers between devices  51.9 us (31%)
  blocking collectives  13.4 us (8%)
  local copies, waits for them, and re-layouts  8.73 us (5%)
  matrix products  7.95 us (5%)
  other arithmetic  5.66 us (3%)
    ppermute x16, starting transfers between devices, with_halo(): after = lax.ppermute(leading, axis, down)  49 us
    ppermute x16, waiting for transfers between devices, with_halo(): before = lax.ppermute(last, axis, up)  28.4 us
    ppermute x16, starting transfers between devices, with_halo(): before = lax.ppermute(last, axis, up)  28.2 us
    ppermute x16, waiting for transfers between devices, with_halo(): after = lax.ppermute(leading, axis, down)  17 us
    all_gather x1, blocking collectives, body(): every = lax.all_gather(jump[None], 'tm', axis=0, tiled=True)  13.4 us
    dot_general x7, matrix products, mesh_spacing(): jnp.dot(vertical_matrix, middle_value.reshape(depth_layers, -1), precisio...  7.95 us
    ppermute x1, waiting for transfers between devices, from_behind(): return lax.ppermute(value, axis, pairs)  6.45 us
    unnamed x14, local copies, waits for them, and re-layouts  3.91 us
  transfers between devices with their start and end apart: 33, of which 13 were waited for; matrix products, arithmetic and copies ran while one was open for 7% of the time, Pallas kernels for 0%

commit v1 on v0

v1 whole, which is shorter than its diff:
```python
import functools

import jax
import jax.numpy as jnp
from jax import lax
from jax.experimental import pallas as pl
from jax.experimental.pallas import tpu as pltpu
from jax.sharding import PartitionSpec as P

K = 48
R = 16
C = 128
H = 9
E = R + 2 * H
W = 2 * C
G = K // 8
SLOT = 2 * H
BASE = R - H
NC = 16
VMEM = pl.BlockSpec(memory_space=pltpu.VMEM)
SMEM = pl.BlockSpec(memory_space=pltpu.SMEM)
PARAMS = pltpu.CompilerParams(vmem_limit_bytes=40 * 1024 * 1024)


def lanes(shape):
    return lax.broadcasted_iota(jnp.int32, shape, len(shape) - 1)


def shift(x, by):
    return pltpu.roll(x, by % x.shape[-1], x.ndim - 1)


def own_row(x_ref, r):
    return x_ref[pl.ds(r, K, stride=R), :]


def halo_kernel(x_ref, wet_ref, kap_ref, top_ref, bot_ref):
    mask = wet_ref[...].astype(jnp.float32)
    for i in range(H):
        top_ref[pl.ds(i * K, K), :] = own_row(x_ref, i) * mask[i : i + 1]
        j = R - H + i
        bot_ref[pl.ds(i * K, K), :] = own_row(x_ref, j) * mask[j : j + 1]
    for ref in (top_ref, bot_ref):
        ref[pl.ds(H * K, R), :] = mask
        ref[pl.ds(H * K + R, R), :] = kap_ref[...]


def pack_row(row):
    lane = lanes((8, C))
    out = shift(row[0:8], H)
    for g in range(1, G):
        out = jnp.where(lane < SLOT * g, out, shift(row[8 * g : 8 * g + 8], SLOT * g + H))
    return out


def unpack_row(packed):
    return jnp.concatenate([shift(packed, C - H - SLOT * g) for g in range(G)], axis=0)


def core_row(x_ref, mask, up_ref, down_ref, r):
    if r < H:
        return up_ref[pl.ds(r * K, K), :]
    if r < H + R:
        return own_row(x_ref, r - H) * mask[r - H : r - H + 1]
    return down_ref[pl.ds((r - H - R) * K, K), :]


def coef_rows(up_ref, own, down_ref, offset):
    at = pl.ds(H * K + offset, R)
    return jnp.concatenate([up_ref[at, :], own, down_ref[at, :]], axis=0)


def edge_kernel(x_ref, wet_ref, kap_ref, up_ref, down_ref, left_ref, right_ref):
    mask = wet_ref[...].astype(jnp.float32)
    rows = [core_row(x_ref, mask, up_ref, down_ref, r) for r in range(E)]
    rows.append(coef_rows(up_ref, mask, down_ref, 0))
    rows.append(coef_rows(up_ref, kap_ref[...], down_ref, R))
    half = len(rows) // 2
    low = lanes((8, C)) % SLOT < H
    for p in range(half):
        a, b = pack_row(rows[p]), pack_row(rows[p + half])
        left_ref[pl.ds(8 * p, 8), :] = jnp.where(low, a, shift(b, H))
        right_ref[pl.ds(8 * p, 8), :] = jnp.where(low, shift(a, -H), b)


def split(x):
    high = x.astype(jnp.bfloat16)
    return high, (x - high.astype(jnp.float32)).astype(jnp.bfloat16)


def level_matrix(mix):
    high, low = split(mix)
    return jnp.concatenate([high, high, low], axis=1)


def levels(matrix, u):
    high, low = split(u)
    return jnp.dot(
        matrix, jnp.concatenate([high, low, high], axis=0), preferred_element_type=jnp.float32
    )


def coefficients(m, k, up, down, scale, by, out_ref):
    total = None
    for i, move in enumerate((up, down, lambda a: shift(a, by), lambda a: shift(a, -by))):
        c = (0.5 * scale) * (k + move(k)) * (m * move(m))
        out_ref[i + 1] = c
        total = c if total is None else total + c
    out_ref[0] = m * (1.0 - total)


def stencil(coef_ref, row, by, u, north, south, matrix):
    c = [coef_ref[i, pl.ds(row, 1), :] for i in range(5)]
    near = c[0] * u + c[1] * north + c[2] * south
    side = c[3] * shift(u, by) + c[4] * shift(u, -by)
    return (near + side) + levels(matrix, u)


def pair_sum(x):
    even = lanes(x.shape) % 2 == 0
    return x + jnp.where(even, shift(x, -1), shift(x, 1))


def put_q(q_ref, out_ref, first, count):
    even = lanes((K, W)) % 2 == 0
    for p in range(count // 2):
        both = jnp.where(even, q_ref[first + 2 * p], q_ref[first + 2 * p + 1])
        out_ref[pl.ds(p * K, K), :] = both[:, :C]
        out_ref[pl.ds((count // 2) * K + 8 * p, 8), :] = pack_row(both[:, C:])


def take_q(in_ref, count, write):
    even = lanes((K, W)) % 2 == 0
    for p in range(count // 2):
        core = in_ref[pl.ds(p * K, K), :]
        side = unpack_row(in_ref[pl.ds((count // 2) * K + 8 * p, 8), :])
        both = jnp.concatenate([core, side], axis=1)
        write(2 * p, jnp.where(even, both, shift(both, 1)))
        write(2 * p + 1, jnp.where(even, shift(both, -1), both))


def fine_kernel(
    later_ref, x_ref, wet_ref, kap_ref, mix_ref, up_ref, down_ref, rl_ref, rr_ref,
    q3_ref, q2_ref, q1_ref, q0_ref, rest_ref, cc_ref,
    ua, ub, mk, cf, rs, qs,
):
    mask = wet_ref[...].astype(jnp.float32)
    half = (E + 2) // 2
    low = lanes((8, C)) % SLOT < H
    sides = []
    for p in range(half):
        a, b = rl_ref[pl.ds(8 * p, 8), :], rr_ref[pl.ds(8 * p, 8), :]
        sides.append((jnp.where(low, a, shift(b, H)), jnp.where(low, shift(a, -H), b)))
    sides = [s[0] for s in sides] + [s[1] for s in sides]
    for r in range(E):
        ua[r, :, :C] = core_row(x_ref, mask, up_ref, down_ref, r)
        ua[r, :, C:] = unpack_row(sides[r])
    mk[0] = coef_rows(up_ref, mask, down_ref, 0)
    mk[1] = unpack_row(sides[E])
    mk[2] = coef_rows(up_ref, kap_ref[...], down_ref, R)
    mk[3] = unpack_row(sides[E + 1])
    north = lambda a: pltpu.roll(a, 1, 0)
    south = lambda a: pltpu.roll(a, a.shape[0] - 1, 0)
    m = jnp.concatenate([mk[0], mk[1]], axis=1)
    k = jnp.concatenate([mk[2], mk[3]], axis=1)
    coefficients(m, k, north, south, 1.0, 1, cf)

    at, after = pl.ds(8, NC, stride=2), pl.ds(9, NC, stride=2)

    def blocks(i):
        return pair_sum(jnp.concatenate([mk[j, at] + mk[j, after] for j in (i, i + 1)], axis=1))

    count = blocks(0)
    inverse = 1.0 / jnp.maximum(count, 1.0)
    coefficients(jnp.minimum(count, 1.0), 0.25 * blocks(2), north, south, 0.75, 2, cc_ref.at[pl.ds(0, 5)])
    cc_ref[5] = inverse
    mix = mix_ref[...]
    fine_mix = level_matrix(mix)
    coarse_mix = level_matrix(3.0 * mix)

    def restrict(src, i):
        return pair_sum(src[1 + 2 * i] + src[2 + 2 * i]) * cc_ref[5, pl.ds(i, 1), :]

    @pl.loop(0, NC)
    def _(i):
        rs[i] = restrict(ua, i)

    def step(src, dst, margin):
        @pl.loop(margin, E - margin)
        def _(r):
            dst[r] = stencil(cf, r + BASE, 1, src[r], src[r - 1], src[r + 1], fine_mix)

    step(ua, ub, 1)
    step(ub, ua, 2)
    step(ua, ub, 3)
    later = later_ref[0]

    @pl.loop(1, NC - 1)
    def _(i):
        fc = restrict(ub, i)
        qs[i] = fc - later * stencil(cc_ref, i, 2, rs[i], rs[i - 1], rs[i + 1], coarse_mix)
        rs[i - 1] = fc

    for i in range(R // 2):
        fc = rs[3 + i, :, :C]
        q0_ref[i] = qs[4 + i, :, :C]
        for r in (2 * i, 2 * i + 1):
            rest_ref[pl.ds(r * K, K), :] = ub[H + r, :, :C] - mask[r : r + 1] * fc
    put_q(qs, q3_ref, 1, 14)
    put_q(qs, q2_ref, 2, 12)
    put_q(qs, q1_ref, 3, 10)


def sweep_kernel(
    wet_ref, mix_ref, cc_ref, q3_ref, q2_ref, q1_ref, q0_ref, rest_ref, out_ref, y_ref, a, b
):
    coarse_mix = level_matrix(3.0 * mix_ref[...])
    mask = wet_ref[...].astype(jnp.float32)

    def put(ref, first):
        def write(i, value):
            ref[first + i] = value

        return write

    def step(src, dst, first, count):
        @pl.loop(first, first + count)
        def _(i):
            dst[i] = dst[i] + stencil(cc_ref, i, 2, src[i], src[i - 1], src[i + 1], coarse_mix)

    take_q(q3_ref, 14, put(a, 1))
    take_q(q2_ref, 12, put(b, 2))
    step(a, b, 2, 12)
    take_q(q1_ref, 10, put(a, 3))
    step(b, a, 3, 10)
    for i in range(8):
        y_ref[i] = a[4 + i, :, :C]
        z = q0_ref[i] + stencil(cc_ref, 4 + i, 2, a[4 + i], a[3 + i], a[5 + i], coarse_mix)[:, :C]
        for r in (2 * i, 2 * i + 1):
            value = rest_ref[pl.ds(r * K, K), :] + mask[r : r + 1] * z
            out_ref[pl.ds(r, K, stride=R), :] = value


def last_kernel(later_ref, wet_ref, x_ref, y_ref, rest_ref, out_ref):
    mask = wet_ref[...].astype(jnp.float32)
    first = later_ref[0] == 0.0

    @pl.when(first)
    def _():
        out_ref[...] = x_ref[...]

    @pl.when(jnp.logical_not(first))
    def _():
        for r in range(R):
            value = rest_ref[pl.ds(r * K, K), :] + mask[r : r + 1] * y_ref[r // 2]
            out_ref[pl.ds(r, K, stride=R), :] = value


def f32(*shape):
    return jax.ShapeDtypeStruct(shape, jnp.float32)


def call(kernel, n_in, outs, scratch=(), smem=0):
    return pl.pallas_call(
        kernel,
        out_shape=outs,
        in_specs=[SMEM] * smem + [VMEM] * (n_in - smem),
        out_specs=jax.tree.map(lambda _: VMEM, outs),
        scratch_shapes=list(scratch),
        compiler_params=PARAMS,
    )


def moved(value, axis, by, wrap=False):
    n = lax.axis_size(axis)
    pairs = [(i, (i + by) % n) for i in range(n) if wrap or 0 <= i + by < n]
    return lax.ppermute(value, axis, pairs)


def body(start, wet, kappa, mixing):
    x = start.reshape(K * R, C)
    later = (lax.axis_index("tm") > 0).astype(jnp.float32).reshape(1)
    send = H * K + 2 * R
    top, bottom = call(halo_kernel, 3, (f32(send, C), f32(send, C)))(x, wet, kappa)
    down = moved(top, "lat", -1)
    up = moved(bottom, "lat", 1)
    side = (E + 2) * 4
    left, right = call(edge_kernel, 5, (f32(side, C), f32(side, C)))(x, wet, kappa, up, down)
    from_left = moved(left, "lon", 1, True)
    from_right = moved(right, "lon", -1, True)
    q3, q2, q1, q0, rest, cc = call(
        fine_kernel,
        9,
        (f32(49 * 8, C), f32(42 * 8, C), f32(35 * 8, C), f32(8, K, C), f32(R * K, C), f32(6, NC, W)),
        [
            pltpu.VMEM((E, K, W), jnp.float32),
            pltpu.VMEM((E, K, W), jnp.float32),
            pltpu.VMEM((4, 48, C), jnp.float32),
            pltpu.VMEM((5, 48, W), jnp.float32),
            pltpu.VMEM((NC, K, W), jnp.float32),
            pltpu.VMEM((NC, K, W), jnp.float32),
        ],
        smem=1,
    )(later, x, wet, kappa, mixing, up, down, from_left, from_right)
    q3, q2, q1 = moved(q3, "tm", 3), moved(q2, "tm", 2), moved(q1, "tm", 1)
    rest_before = moved(rest, "tm", 1)
    out, y = call(
        sweep_kernel,
        8,
        (f32(K * R, C), f32(8, K, C)),
        [pltpu.VMEM((NC, K, W), jnp.float32), pltpu.VMEM((NC, K, W), jnp.float32)],
    )(wet, mixing, cc, q3, q2, q1, q0, rest)
    following = call(last_kernel, 5, f32(K * R, C), smem=1)(later, wet, x, y, rest_before)
    return out.reshape(1, K, R, C), following.reshape(1, K, R, C)


def solution(mesh):
    in_specs = (P("tm", None, "lat", "lon"), P("lat", "lon"), P("lat", "lon"), P())
    out_specs = (P("tm", None, "lat", "lon"), P("tm", None, "lat", "lon"))
    return jax.shard_map(body, mesh=mesh, in_specs=in_specs, out_specs=out_specs, check_vma=False)
```

time: 169 us -> 69.6 us (0.41)
  the two profiles are of different devices: /device:TPU:10 before, /device:TPU:26 now
where the time goes in v1:
time: 69.6 us; the launch traced here: 69.2 us
  Pallas kernels  25 us (36%)
  starting transfers between devices  22.6 us (32%)
  waiting for transfers between devices  18.5 us (27%)
  local copies, waits for them, and re-layouts  2.41 us (3%)
  between operations  0.76 us (1%)
    ppermute x8, starting transfers between devices, moved(): return lax.ppermute(value, axis, pairs)  22.6 us
    ppermute x8, waiting for transfers between devices, moved(): return lax.ppermute(value, axis, pairs)  18.5 us
    pallas_call x1, Pallas kernels, body(): call(fine_kernel, 9, (f32(49 * 8, C), f32(42 * 8, C), f32(35 * 8, C), f32...  17.3 us
    pallas_call x1, Pallas kernels, body(): call(sweep_kernel, 8, (f32(K * R, C), f32(8, K, C)), [pltpu.VMEM((NC, K,...  5.64 us
    unnamed x14, local copies, waits for them, and re-layouts  2.41 us
  transfers between devices with their start and end apart: 8, of which 4 were waited for; matrix products, arithmetic and copies ran while one was open for 0% of the time, Pallas kernels for 8%

profile of v1, /device:TPU:26, one launch (start us, length us, event | category | flops | bytes accessed | tf_op | source)
XLA Modules:
  0.0 69.2 jit_solution(3609035542536970906)
XLA Ops:
  0.6 0.0 copy-start
  0.6 1.0 %copy-done = f32[1,48,16,128]{3,2,1,0:T(8,128)S(1)} copy-done((f32[1,48,16,128]{3,2,1,0:T(8,128)S(1)}, f32[1,48,16,128]{3,2,1,0:T(8,128)}, u32[]{:S(2)}) %copy-start) | copy-done | bytes 393240
  1.6 0.7 %copy-done.2 = s32[16,128]{1,0:T(8,128)S(1)} copy-done((s32[16,128]{1,0:T(8,128)S(1)}, s32[16,128]{1,0:T(8,128)}, u32[]{:S(2)}) %copy-start.2) | copy-done | bytes 8216
  2.3 0.7 %copy-done.5 = f32[16,128]{1,0:T(8,128)S(1)} copy-done((f32[16,128]{1,0:T(8,128)S(1)}, f32[16,128]{1,0:T(8,128)}, u32[]{:S(2)}) %copy-start.5) | copy-done | bytes 8216
  3.0 0.1 shard_map.59
  3.2 4.7 %collective-permute-start = (f32[464,128]{1,0:T(8,128)S(1)}, f32[464,128]{1,0:T(8,128)S(1)}, u32[]{:S(2)}, u32[]{:S(2)}) collective-permute-start(f32[464,128]{1,0:T(8,128)S(1)} %get-tuple-element.14), channel_id=1, source_target_pairs={{0,16},{16,32},{32,48},{48,64},{64,80},{80,96},{96,112},{1,17},{17... | collective-permute-start | bytes 712712 | tf_op jit(solution)/shard_map/ppermute | solution.py:277
  7.9 0.0 copy-start.1
  7.9 2.1 %collective-permute-start.1 = (f32[464,128]{1,0:T(8,128)S(1)}, f32[464,128]{1,0:T(8,128)S(1)}, u32[]{:S(2)}, u32[]{:S(2)}) collective-permute-start(f32[464,128]{1,0:T(8,128)S(1)} %get-tuple-element.15), channel_id=1, source_target_pairs={{16,0},{32,16},{48,32},{64,48},{80,64},{96,80},{112,96},{17,1},{33... | collective-permute-start | bytes 712712 | tf_op jit(solution)/shard_map/ppermute | solution.py:277
  9.9 2.9 %collective-permute-done.up_ref = f32[464,128]{1,0:T(8,128)S(1)} collective-permute-done((f32[464,128]{1,0:T(8,128)S(1)}, f32[464,128]{1,0:T(8,128)S(1)}, u32[]{:S(2)}, u32[]{:S(2)}) %collective-permute-start) | collective-permute-done | bytes 237600 | tf_op jit(solution)/shard_map/ppermute | solution.py:277
  12.9 5.5 %collective-permute-done.1.down_ref = f32[464,128]{1,0:T(8,128)S(1)} collective-permute-done((f32[464,128]{1,0:T(8,128)S(1)}, f32[464,128]{1,0:T(8,128)S(1)}, u32[]{:S(2)}, u32[]{:S(2)}) %collective-permute-start.1) | collective-permute-done | bytes 237600 | tf_op jit(solution)/shard_map/ppermute | solution.py:277
  18.4 1.0 %shard_map.60 = (f32[144,128]{1,0:T(8,128)S(1)}, f32[144,128]{1,0:T(8,128)S(1)}) custom-call(f32[768,128]{1,0:T(8,128)S(1)} %bitcast.5, s32[16,128]{1,0:T(8,128)S(1)} %copy-done.2, f32[16,128]{1,0:T(8,128)S(1)} %copy-done.5, f32[464,128]{1,0:T(8,128)S(1)} %collective-permute-done.up_ref, f32[464,128]{1,0:T(8,128)S(1)} %collective-permute-done.1.down_ref), custom_call_target="tpu_custom_call" | custom-call | tf_op jit(solution)/shard_map/pallas_call | solution.py:288
  19.3 0.0 copy-start.6
  19.4 0.0 copy-start.3
  19.4 0.0 collective-permute-start.2
  19.4 7.3 %collective-permute-start.3 = (f32[144,128]{1,0:T(8,128)S(1)}, f32[144,128]{1,0:T(8,128)S(1)}, u32[]{:S(2)}, u32[]{:S(2)}) collective-permute-start(f32[144,128]{1,0:T(8,128)S(1)} %get-tuple-element.17), channel_id=1, source_target_pairs={{0,15},{1,0},{2,1},{3,2},{4,3},{5,4},{6,5},{7,6},{8,7},{9,8},{10,9... | collective-permute-start | bytes 221192 | tf_op jit(solution)/shard_map/ppermute | solution.py:277
  26.7 2.0 %collective-permute-done.2.rl_ref = f32[144,128]{1,0:T(8,128)S(1)} collective-permute-done((f32[144,128]{1,0:T(8,128)S(1)}, f32[144,128]{1,0:T(8,128)S(1)}, u32[]{:S(2)}, u32[]{:S(2)}) %collective-permute-start.2) | collective-permute-done | bytes 73760 | tf_op jit(solution)/shard_map/ppermute | solution.py:277
  28.7 17.3 %shard_map.61 = (f32[392,128]{1,0:T(8,128)S(1)}, f32[336,128]{1,0:T(8,128)S(1)}, f32[280,128]{1,0:T(8,128)S(1)}, f32[8,48,128]{2,1,0:T(8,128)S(1)}, f32[768,128]{1,0:T(8,128)S(1)}, /*index=5*/f32[6,16,256]{2,1,0:T(8,128)S(1)}) custom-call(f32[1]{0:T(128)} %bitcast.later_ref, f32[768,128]{1,0:T(8,128)S(1)} %bitcast.6, s32[16,128]{1,0:T(8,128)S(1)} %copy-done.3, ...), custom_call_target="tpu_custom_call" | custom-call | tf_op jit(solution)/shard_map/pallas_call | solution.py:291
  46.0 3.4 %collective-permute-start.7 = (f32[768,128]{1,0:T(8,128)S(1)}, f32[768,128]{1,0:T(8,128)S(1)}, u32[]{:S(2)}, u32[]{:S(2)}) collective-permute-start(f32[768,128]{1,0:T(8,128)S(1)} %get-tuple-element.23.rest_ref), channel_id=1, source_target_pairs={{0,128},{128,256},{256,384},{1,129},{129,257},{257,385},{2,130},{1... | collective-permute-start | bytes 1179656 | tf_op jit(solution)/shard_map/ppermute | solution.py:277
  49.4 0.7 collective-permute-start.4
  50.1 2.5 %collective-permute-start.5 = (f32[336,128]{1,0:T(8,128)S(1)}, f32[336,128]{1,0:T(8,128)S(1)}, u32[]{:S(2)}, u32[]{:S(2)}) collective-permute-start(f32[336,128]{1,0:T(8,128)S(1)} %get-tuple-element.20), channel_id=1, source_target_pairs={{0,256},{128,384},{1,257},{129,385},{2,258},{130,386},{3,259},{131... | collective-permute-start | bytes 516104 | tf_op jit(solution)/shard_map/ppermute | solution.py:277
  52.7 1.9 %collective-permute-start.6 = (f32[280,128]{1,0:T(8,128)S(1)}, f32[280,128]{1,0:T(8,128)S(1)}, u32[]{:S(2)}, u32[]{:S(2)}) collective-permute-start(f32[280,128]{1,0:T(8,128)S(1)} %get-tuple-element.21), channel_id=1, source_target_pairs={{0,128},{128,256},{256,384},{1,129},{129,257},{257,385},{2,130},{1... | collective-permute-start | bytes 430088 | tf_op jit(solution)/shard_map/ppermute | solution.py:277
  54.6 8.1 %collective-permute-done.6.q1_ref = f32[280,128]{1,0:T(8,128)S(1)} collective-permute-done((f32[280,128]{1,0:T(8,128)S(1)}, f32[280,128]{1,0:T(8,128)S(1)}, u32[]{:S(2)}, u32[]{:S(2)}) %collective-permute-start.6) | collective-permute-done | bytes 143392 | tf_op jit(solution)/shard_map/ppermute | solution.py:277
  62.7 5.6 %shard_map.62 = (f32[768,128]{1,0:T(8,128)}, f32[8,48,128]{2,1,0:T(8,128)S(1)}) custom-call(s32[16,128]{1,0:T(8,128)S(1)} %copy-done.3, f32[48,48]{1,0:T(8,128)S(1)} %copy-done.4, f32[6,16,256]{2,1,0:T(8,128)S(1)} %get-tuple-element.18.cc_ref, f32[392,128]{1,0:T(8,128)S(1)} %collective-permute-done.4.q3_ref, f32[336,128]{1,0:T(8,128)S(1)} %collective-permute-done.5.q2_ref, ...), custom_call_target="tpu_custom_call" | custom-call | tf_op jit(solution)/shard_map/pallas_call | solution.py:307
  68.3 0.9 %shard_map.63 = f32[768,128]{1,0:T(8,128)} custom-call(f32[1]{0:T(128)} %bitcast.later_ref, s32[16,128]{1,0:T(8,128)S(1)} %copy-done.3, f32[768,128]{1,0:T(8,128)S(1)} %bitcast.7, f32[8,48,128]{2,1,0:T(8,128)S(1)} %get-tuple-element.25.y_ref, f32[768,128]{1,0:T(8,128)S(1)} %collective-permute-done.7.rest_ref), custom_call_target="tpu_custom_call" | custom-call | tf_op jit(solution)/shard_map/pallas_call | solution.py:313
  (11 shorter events, 0.0 us)
Async XLA Ops:
  0.6 1.0 %copy-start = (f32[1,48,16,128]{3,2,1,0:T(8,128)S(1)}, f32[1,48,16,128]{3,2,1,0:T(8,128)}, u32[]{:S(2)}) copy-start(f32[1,48,16,128]{3,2,1,0:T(8,128)} %param.4) | copy-start | bytes 1179652
  1.6 0.7 %copy-start.2 = (s32[16,128]{1,0:T(8,128)S(1)}, s32[16,128]{1,0:T(8,128)}, u32[]{:S(2)}) copy-start(s32[16,128]{1,0:T(8,128)} %wet_ref.9) | copy-start | bytes 24580
  2.3 0.7 %copy-start.5 = (f32[16,128]{1,0:T(8,128)S(1)}, f32[16,128]{1,0:T(8,128)}, u32[]{:S(2)}) copy-start(f32[16,128]{1,0:T(8,128)} %kap_ref.5) | copy-start | bytes 24580
  3.2 9.7 %collective-permute-start = (f32[464,128]{1,0:T(8,128)S(1)}, f32[464,128]{1,0:T(8,128)S(1)}, u32[]{:S(2)}, u32[]{:S(2)}) collective-permute-start(f32[464,128]{1,0:T(8,128)S(1)} %get-tuple-element.14), channel_id=1, source_target_pairs={{0,16},{16,32},{32,48},{48,64},{64,80},{80,96},{96,112},{1,17},{17... | collective-permute-start | bytes 712712 | tf_op jit(solution)/shard_map/ppermute | solution.py:277
  7.9 20.8 %copy-start.1 = (f32[1,48,16,128]{3,2,1,0:T(8,128)S(1)}, f32[1,48,16,128]{3,2,1,0:T(8,128)}, u32[]{:S(2)}) copy-start(f32[1,48,16,128]{3,2,1,0:T(8,128)} %param.4) | copy-start | bytes 1179652
  7.9 10.5 %collective-permute-start.1 = (f32[464,128]{1,0:T(8,128)S(1)}, f32[464,128]{1,0:T(8,128)S(1)}, u32[]{:S(2)}, u32[]{:S(2)}) collective-permute-start(f32[464,128]{1,0:T(8,128)S(1)} %get-tuple-element.15), channel_id=1, source_target_pairs={{16,0},{32,16},{48,32},{64,48},{80,64},{96,80},{112,96},{17,1},{33... | collective-permute-start | bytes 712712 | tf_op jit(solution)/shard_map/ppermute | solution.py:277
  18.4 10.4 %copy-start.4 = (f32[48,48]{1,0:T(8,128)S(1)}, f32[48,48]{1,0:T(8,128)}, u32[]{:S(2)}) copy-start(f32[48,48]{1,0:T(8,128)} %mix_ref.3) | copy-start | bytes 27652
  19.3 9.4 %copy-start.6 = (f32[16,128]{1,0:T(8,128)S(1)}, f32[16,128]{1,0:T(8,128)}, u32[]{:S(2)}) copy-start(f32[16,128]{1,0:T(8,128)} %kap_ref.5) | copy-start | bytes 24580
  19.4 9.4 %copy-start.3 = (s32[16,128]{1,0:T(8,128)S(1)}, s32[16,128]{1,0:T(8,128)}, u32[]{:S(2)}) copy-start(s32[16,128]{1,0:T(8,128)} %wet_ref.9) | copy-start | bytes 24580
  19.4 9.3 %collective-permute-start.2 = (f32[144,128]{1,0:T(8,128)S(1)}, f32[144,128]{1,0:T(8,128)S(1)}, u32[]{:S(2)}, u32[]{:S(2)}) collective-permute-start(f32[144,128]{1,0:T(8,128)S(1)} %get-tuple-element.16), channel_id=1, source_target_pairs={{0,1},{1,2},{2,3},{3,4},{4,5},{5,6},{6,7},{7,8},{8,9},{9,10},{10,1... | collective-permute-start | bytes 221192 | tf_op jit(solution)/shard_map/ppermute | solution.py:277
  19.4 9.3 %collective-permute-start.3 = (f32[144,128]{1,0:T(8,128)S(1)}, f32[144,128]{1,0:T(8,128)S(1)}, u32[]{:S(2)}, u32[]{:S(2)}) collective-permute-start(f32[144,128]{1,0:T(8,128)S(1)} %get-tuple-element.17), channel_id=1, source_target_pairs={{0,15},{1,0},{2,1},{3,2},{4,3},{5,4},{6,5},{7,6},{8,7},{9,8},{10,9... | collective-permute-start | bytes 221192 | tf_op jit(solution)/shard_map/ppermute | solution.py:277
  46.0 22.3 %collective-permute-start.7 = (f32[768,128]{1,0:T(8,128)S(1)}, f32[768,128]{1,0:T(8,128)S(1)}, u32[]{:S(2)}, u32[]{:S(2)}) collective-permute-start(f32[768,128]{1,0:T(8,128)S(1)} %get-tuple-element.23.rest_ref), channel_id=1, source_target_pairs={{0,128},{128,256},{256,384},{1,129},{129,257},{257,385},{2,130},{1... | collective-permute-start | bytes 1179656 | tf_op jit(solution)/shard_map/ppermute | solution.py:277
  49.4 13.2 %collective-permute-start.4 = (f32[392,128]{1,0:T(8,128)S(1)}, f32[392,128]{1,0:T(8,128)S(1)}, u32[]{:S(2)}, u32[]{:S(2)}) collective-permute-start(f32[392,128]{1,0:T(8,128)S(1)} %get-tuple-element.19), channel_id=1, source_target_pairs={{0,384},{1,385},{2,386},{3,387},{4,388},{5,389},{6,390},{7,391},{8... | collective-permute-start | bytes 602120 | tf_op jit(solution)/shard_map/ppermute | solution.py:277
  50.1 12.6 %collective-permute-start.5 = (f32[336,128]{1,0:T(8,128)S(1)}, f32[336,128]{1,0:T(8,128)S(1)}, u32[]{:S(2)}, u32[]{:S(2)}) collective-permute-start(f32[336,128]{1,0:T(8,128)S(1)} %get-tuple-element.20), channel_id=1, source_target_pairs={{0,256},{128,384},{1,257},{129,385},{2,258},{130,386},{3,259},{131... | collective-permute-start | bytes 516104 | tf_op jit(solution)/shard_map/ppermute | solution.py:277
  52.7 10.0 %collective-permute-start.6 = (f32[280,128]{1,0:T(8,128)S(1)}, f32[280,128]{1,0:T(8,128)S(1)}, u32[]{:S(2)}, u32[]{:S(2)}) collective-permute-start(f32[280,128]{1,0:T(8,128)S(1)} %get-tuple-element.21), channel_id=1, source_target_pairs={{0,128},{128,256},{256,384},{1,129},{129,257},{257,385},{2,130},{1... | collective-permute-start | bytes 430088 | tf_op jit(solution)/shard_map/ppermute | solution.py:277

commit v2 on v1

v2 whole, which is shorter than its diff:
```python
import functools

import jax
import jax.numpy as jnp
from jax import lax
from jax.experimental import pallas as pl
from jax.experimental.pallas import tpu as pltpu
from jax.sharding import PartitionSpec as P

K = 48
R = 16
C = 128
H = 9
E = R + 2 * H
W = 2 * C
G = K // 8
SLOT = 2 * H
BASE = R - H
NC = 16
VMEM = pl.BlockSpec(memory_space=pltpu.VMEM)
SMEM = pl.BlockSpec(memory_space=pltpu.SMEM)
PARAMS = pltpu.CompilerParams(vmem_limit_bytes=40 * 1024 * 1024)


def lanes(shape):
    return lax.broadcasted_iota(jnp.int32, shape, len(shape) - 1)


def shift(x, by):
    return pltpu.roll(x, by % x.shape[-1], x.ndim - 1)


def halo_kernel(
    x_hbm, wet_hbm, kap_hbm, top_ref, bot_ref, core_ref, mk_ref, x_ref, wet_ref, kap_ref, sems
):
    copies = [
        pltpu.make_async_copy(src, dst, sems.at[i])
        for i, (src, dst) in enumerate(
            ((wet_hbm, wet_ref), (kap_hbm, kap_ref), (x_hbm, x_ref))
        )
    ]
    for copy in copies:
        copy.start()
    for copy in copies:
        copy.wait()
    mask = wet_ref[...].astype(jnp.float32)
    for r in range(R):
        row = x_ref[pl.ds(r, K, stride=R), :] * mask[r : r + 1]
        core_ref[pl.ds(r * K, K), :] = row
        if r < H:
            top_ref[pl.ds(r * K, K), :] = row
        if r >= R - H:
            bot_ref[pl.ds((r - R + H) * K, K), :] = row
    for ref, first in ((top_ref, H * K), (bot_ref, H * K), (mk_ref, 0)):
        ref[pl.ds(first, R), :] = mask
        ref[pl.ds(first + R, R), :] = kap_ref[...]


def pack_row(row):
    lane = lanes((8, C))
    out = shift(row[0:8], H)
    for g in range(1, G):
        out = jnp.where(lane < SLOT * g, out, shift(row[8 * g : 8 * g + 8], SLOT * g + H))
    return out


def unpack_row(packed):
    return jnp.concatenate([shift(packed, C - H - SLOT * g) for g in range(G)], axis=0)


def core_row(core_ref, up_ref, down_ref, r):
    for ref, first, count in ((up_ref, 0, H), (core_ref, H, R), (down_ref, H + R, H)):
        if first <= r < first + count:
            return ref[pl.ds((r - first) * K, K), :]


def coef_rows(up_ref, mk_ref, down_ref, i):
    at = pl.ds(H * K + i * R, R)
    return jnp.concatenate([up_ref[at, :], mk_ref[pl.ds(i * R, R), :], down_ref[at, :]], axis=0)


def edge_kernel(core_ref, mk_ref, up_ref, down_ref, left_ref, right_ref):
    rows = [core_row(core_ref, up_ref, down_ref, r) for r in range(E)]
    rows += [coef_rows(up_ref, mk_ref, down_ref, i) for i in range(2)]
    half = len(rows) // 2
    low = lanes((8, C)) % SLOT < H
    for p in range(half):
        a, b = pack_row(rows[p]), pack_row(rows[p + half])
        left_ref[pl.ds(8 * p, 8), :] = jnp.where(low, a, shift(b, H))
        right_ref[pl.ds(8 * p, 8), :] = jnp.where(low, shift(a, -H), b)


def split(x):
    high = x.astype(jnp.bfloat16)
    return high, (x - high.astype(jnp.float32)).astype(jnp.bfloat16)


def level_matrix(mix):
    high, low = split(mix)
    return jnp.concatenate([high, high, low], axis=1)


def levels(matrix, u):
    high, low = split(u)
    return jnp.dot(
        matrix, jnp.concatenate([high, low, high], axis=0), preferred_element_type=jnp.float32
    )


def coefficients(m, k, up, down, scale, by, out_ref):
    total = None
    for i, move in enumerate((up, down, lambda a: shift(a, by), lambda a: shift(a, -by))):
        c = (0.5 * scale) * (k + move(k)) * (m * move(m))
        out_ref[i + 1] = c
        total = c if total is None else total + c
    out_ref[0] = m * (1.0 - total)


def stencil(coef_ref, row, by, u, north, south, matrix):
    c = [coef_ref[i, pl.ds(row, 1), :] for i in range(5)]
    near = c[0] * u + c[1] * north + c[2] * south
    side = c[3] * shift(u, by) + c[4] * shift(u, -by)
    return (near + side) + levels(matrix, u)


def by_tile(fn, x):
    return jnp.concatenate([fn(x[:, :C]), fn(x[:, C:])], axis=1)


def pair_sum(x):
    return x + by_tile(lambda t: shift(t, -1), x)


def spread(x):
    return jnp.where(lanes(x.shape) % 2 == 0, x, shift(x, 1))


def put_q(q_ref, out_ref, first, count):
    even = lanes((K, W)) % 2 == 0
    for p in range(count // 2):
        odd = by_tile(lambda t: shift(t, 1), q_ref[first + 2 * p + 1])
        both = jnp.where(even, q_ref[first + 2 * p], odd)
        out_ref[pl.ds(p * K, K), :] = both[:, :C]
        out_ref[pl.ds((count // 2) * K + 8 * p, 8), :] = pack_row(both[:, C:])


def take_q(in_ref, count, write):
    for p in range(count // 2):
        core = in_ref[pl.ds(p * K, K), :]
        side = unpack_row(in_ref[pl.ds((count // 2) * K + 8 * p, 8), :])
        both = jnp.concatenate([core, side], axis=1)
        write(2 * p, both)
        write(2 * p + 1, by_tile(lambda t: shift(t, -1), both))


def fine_kernel(
    later_ref, core_ref, mk_ref, mix_ref, up_ref, down_ref, rl_ref, rr_ref,
    q3_ref, q2_ref, q1_ref, q0_ref, rest_ref, cc_ref,
    ua, ub, mk, cf, rs, qs,
):
    half = (E + 2) // 2
    low = lanes((8, C)) % SLOT < H
    sides = []
    for p in range(half):
        a, b = rl_ref[pl.ds(8 * p, 8), :], rr_ref[pl.ds(8 * p, 8), :]
        sides.append((jnp.where(low, a, shift(b, H)), jnp.where(low, shift(a, -H), b)))
    sides = [s[0] for s in sides] + [s[1] for s in sides]
    for r in range(E):
        ua[r, :, :C] = core_row(core_ref, up_ref, down_ref, r)
        ua[r, :, C:] = unpack_row(sides[r])
    mk[0] = coef_rows(up_ref, mk_ref, down_ref, 0)
    mk[1] = unpack_row(sides[E])
    mk[2] = coef_rows(up_ref, mk_ref, down_ref, 1)
    mk[3] = unpack_row(sides[E + 1])
    north = lambda a: pltpu.roll(a, 1, 0)
    south = lambda a: pltpu.roll(a, a.shape[0] - 1, 0)
    m = jnp.concatenate([mk[0], mk[1]], axis=1)
    k = jnp.concatenate([mk[2], mk[3]], axis=1)
    coefficients(m, k, north, south, 1.0, 1, cf)

    at, after = pl.ds(8, NC, stride=2), pl.ds(9, NC, stride=2)

    def blocks(i):
        return pair_sum(jnp.concatenate([mk[j, at] + mk[j, after] for j in (i, i + 1)], axis=1))

    count = blocks(0)
    inverse = 1.0 / jnp.maximum(count, 1.0)
    coefficients(jnp.minimum(count, 1.0), 0.25 * blocks(2), north, south, 0.75, 2, cc_ref.at[pl.ds(0, 5)])
    cc_ref[5] = inverse
    mix = mix_ref[...]
    fine_mix = level_matrix(mix)
    coarse_mix = level_matrix(3.0 * mix)

    def restrict(src, i):
        return pair_sum(src[1 + 2 * i] + src[2 + 2 * i]) * cc_ref[5, pl.ds(i, 1), :]

    @pl.loop(0, NC, unroll=8)
    def _(i):
        rs[i] = restrict(ua, i)

    def step(src, dst, margin):
        @pl.loop(margin, E - margin, unroll=8)
        def _(r):
            dst[r] = stencil(cf, r + BASE, 1, src[r], src[r - 1], src[r + 1], fine_mix)

    step(ua, ub, 1)
    step(ub, ua, 2)
    step(ua, ub, 3)
    later = later_ref[0]

    @pl.loop(1, NC - 1, unroll=7)
    def _(i):
        fc = restrict(ub, i)
        qs[i] = fc - later * stencil(cc_ref, i, 2, rs[i], rs[i - 1], rs[i + 1], coarse_mix)
        rs[i - 1] = fc

    for i in range(R // 2):
        fc = spread(rs[3 + i, :, :C])
        q0_ref[i] = qs[4 + i, :, :C]
        for r in (2 * i, 2 * i + 1):
            rest_ref[pl.ds(r * K, K), :] = ub[H + r, :, :C] - mk_ref[pl.ds(r, 1), :] * fc
    put_q(qs, q3_ref, 1, 14)
    put_q(qs, q2_ref, 2, 12)
    put_q(qs, q1_ref, 3, 10)


def sweep_kernel(
    mk_ref, mix_ref, cc_ref, q3_ref, q2_ref, q1_ref, q0_ref, rest_ref, out_ref, y_ref, a, b
):
    coarse_mix = level_matrix(3.0 * mix_ref[...])

    def put(ref, first):
        def write(i, value):
            ref[first + i] = value

        return write

    def step(src, dst, first, count):
        @pl.loop(first, first + count, unroll=count // 2)
        def _(i):
            dst[i] = dst[i] + stencil(cc_ref, i, 2, src[i], src[i - 1], src[i + 1], coarse_mix)

    take_q(q3_ref, 14, put(a, 1))
    take_q(q2_ref, 12, put(b, 2))
    step(a, b, 2, 12)
    take_q(q1_ref, 10, put(a, 3))
    step(b, a, 3, 10)
    for i in range(8):
        y_ref[i] = spread(a[4 + i, :, :C])
        z = q0_ref[i] + stencil(cc_ref, 4 + i, 2, a[4 + i], a[3 + i], a[5 + i], coarse_mix)[:, :C]
        z = spread(z)
        for r in (2 * i, 2 * i + 1):
            value = rest_ref[pl.ds(r * K, K), :] + mk_ref[pl.ds(r, 1), :] * z
            out_ref[pl.ds(r, K, stride=R), :] = value


def last_kernel(later_ref, mk_ref, x_ref, y_ref, rest_ref, out_ref):
    first = later_ref[0] == 0.0

    @pl.when(first)
    def _():
        out_ref[...] = x_ref[...]

    @pl.when(jnp.logical_not(first))
    def _():
        for r in range(R):
            value = rest_ref[pl.ds(r * K, K), :] + mk_ref[pl.ds(r, 1), :] * y_ref[r // 2]
            out_ref[pl.ds(r, K, stride=R), :] = value


def f32(*shape):
    return jax.ShapeDtypeStruct(shape, jnp.float32)


def call(kernel, n_in, outs, scratch=(), smem=0, spec=VMEM):
    return pl.pallas_call(
        kernel,
        out_shape=outs,
        in_specs=[SMEM] * smem + [spec] * (n_in - smem),
        out_specs=jax.tree.map(lambda _: VMEM, outs),
        scratch_shapes=list(scratch),
        compiler_params=PARAMS,
    )


def fine_call():
    return call(
        fine_kernel,
        8,
        (f32(49 * 8, C), f32(42 * 8, C), f32(35 * 8, C), f32(8, K, C), f32(R * K, C), f32(6, NC, W)),
        [
            pltpu.VMEM((E, K, W), jnp.float32),
            pltpu.VMEM((E, K, W), jnp.float32),
            pltpu.VMEM((4, 48, C), jnp.float32),
            pltpu.VMEM((5, 48, W), jnp.float32),
            pltpu.VMEM((NC, K, W), jnp.float32),
            pltpu.VMEM((NC, K, W), jnp.float32),
        ],
        smem=1,
    )


def moved(value, axis, by, wrap=False):
    n = lax.axis_size(axis)
    pairs = [(i, (i + by) % n) for i in range(n) if wrap or 0 <= i + by < n]
    return lax.ppermute(value, axis, pairs)


def body(start, wet, kappa, mixing):
    x = start.reshape(K * R, C)
    later = (lax.axis_index("tm") > 0).astype(jnp.float32).reshape(1)
    send = H * K + 2 * R
    top, bottom, core, mk = call(
        halo_kernel,
        3,
        (f32(send, C), f32(send, C), f32(R * K, C), f32(2 * R, C)),
        [
            pltpu.VMEM((K * R, C), jnp.float32),
            pltpu.VMEM((R, C), jnp.int32),
            pltpu.VMEM((R, C), jnp.float32),
            pltpu.SemaphoreType.DMA((3,)),
        ],
        spec=pl.BlockSpec(memory_space=pl.ANY),
    )(x, wet, kappa)
    down = moved(top, "lat", -1)
    up = moved(bottom, "lat", 1)
    side = (E + 2) * 4
    left, right = call(edge_kernel, 4, (f32(side, C), f32(side, C)))(core, mk, up, down)
    from_left = moved(left, "lon", 1, True)
    from_right = moved(right, "lon", -1, True)
    q3, q2, q1, q0, rest, cc = fine_call()(
        later, core, mk, mixing, up, down, from_left, from_right
    )
    q3, q2, q1 = moved(q3, "tm", 3), moved(q2, "tm", 2), moved(q1, "tm", 1)
    rest_before = moved(rest, "tm", 1)
    out, y = call(
        sweep_kernel,
        8,
        (f32(K * R, C), f32(8, K, C)),
        [pltpu.VMEM((NC, K, W), jnp.float32), pltpu.VMEM((NC, K, W), jnp.float32)],
    )(mk, mixing, cc, q3, q2, q1, q0, rest)
    following = call(last_kernel, 5, f32(K * R, C), smem=1)(later, mk, x, y, rest_before)
    return out.reshape(1, K, R, C), following.reshape(1, K, R, C)


def solution(mesh):
    in_specs = (P("tm", None, "lat", "lon"), P("lat", "lon"), P("lat", "lon"), P())
    out_specs = (P("tm", None, "lat", "lon"), P("tm", None, "lat", "lon"))
    return jax.shard_map(body, mesh=mesh, in_specs=in_specs, out_specs=out_specs, check_vma=False)
```

time: 69.6 us -> 57.6 us (0.83)
  the two profiles are of different devices: /device:TPU:26 before, /device:TPU:28 now
where the time goes in v2:
time: 57.6 us; the launch traced here: 57.2 us
  starting transfers between devices  20.9 us (36%)
  waiting for transfers between devices  20 us (35%)
  Pallas kernels  13.1 us (23%)
  local copies, waits for them, and re-layouts  2.39 us (4%)
  between operations  0.73 us (1%)
    ppermute x8, starting transfers between devices, moved(): return lax.ppermute(value, axis, pairs)  20.9 us
    ppermute x8, waiting for transfers between devices, moved(): return lax.ppermute(value, axis, pairs)  20 us
    pallas_call x1, Pallas kernels, body(): fine_call()(later, core, mk, mixing, up, down, from_left, from_right)  7.6 us
    pallas_call x1, Pallas kernels, body(): call(sweep_kernel, 8, (f32(K * R, C), f32(8, K, C)), [pltpu.VMEM((NC, K,...  3.24 us
    unnamed x10, local copies, waits for them, and re-layouts  2.39 us
  transfers between devices with their start and end apart: 8, of which 4 were waited for; matrix products, arithmetic and copies ran while one was open for 0% of the time, Pallas kernels for 6%

profile of v2, /device:TPU:28, one launch (start us, length us, event | category | flops | bytes accessed | tf_op | source)
XLA Modules:
  0.0 57.2 jit_solution(10274727443194399845)
XLA Ops:
  0.6 0.0 copy-start
  0.6 1.0 %copy-done = f32[1,48,16,128]{3,2,1,0:T(8,128)S(1)} copy-done((f32[1,48,16,128]{3,2,1,0:T(8,128)S(1)}, f32[1,48,16,128]{3,2,1,0:T(8,128)}, u32[]{:S(2)}) %copy-start) | copy-done | bytes 393240
  1.6 0.7 %copy-done.3 = s32[16,128]{1,0:T(8,128)S(1)} copy-done((s32[16,128]{1,0:T(8,128)S(1)}, s32[16,128]{1,0:T(8,128)}, u32[]{:S(2)}) %copy-start.3) | copy-done | bytes 8216
  2.3 0.7 %copy-done.4 = f32[16,128]{1,0:T(8,128)S(1)} copy-done((f32[16,128]{1,0:T(8,128)S(1)}, f32[16,128]{1,0:T(8,128)}, u32[]{:S(2)}) %copy-start.4) | copy-done | bytes 8216
  3.0 0.4 shard_map.59
  3.4 4.7 %collective-permute-start = (f32[464,128]{1,0:T(8,128)S(1)}, f32[464,128]{1,0:T(8,128)S(1)}, u32[]{:S(2)}, u32[]{:S(2)}) collective-permute-start(f32[464,128]{1,0:T(8,128)S(1)} %get-tuple-element.18), channel_id=1, source_target_pairs={{0,16},{16,32},{32,48},{48,64},{64,80},{80,96},{96,112},{1,17},{17... | collective-permute-start | bytes 712712 | tf_op jit(solution)/shard_map/ppermute | solution.py:306
  8.1 1.9 %collective-permute-start.1 = (f32[464,128]{1,0:T(8,128)S(1)}, f32[464,128]{1,0:T(8,128)S(1)}, u32[]{:S(2)}, u32[]{:S(2)}) collective-permute-start(f32[464,128]{1,0:T(8,128)S(1)} %get-tuple-element.19), channel_id=1, source_target_pairs={{16,0},{32,16},{48,32},{64,48},{80,64},{96,80},{112,96},{17,1},{33... | collective-permute-start | bytes 712712 | tf_op jit(solution)/shard_map/ppermute | solution.py:306
  10.0 3.1 %collective-permute-done.up_ref = f32[464,128]{1,0:T(8,128)S(1)} collective-permute-done((f32[464,128]{1,0:T(8,128)S(1)}, f32[464,128]{1,0:T(8,128)S(1)}, u32[]{:S(2)}, u32[]{:S(2)}) %collective-permute-start) | collective-permute-done | bytes 237600 | tf_op jit(solution)/shard_map/ppermute | solution.py:306
  13.1 5.3 %collective-permute-done.1.down_ref = f32[464,128]{1,0:T(8,128)S(1)} collective-permute-done((f32[464,128]{1,0:T(8,128)S(1)}, f32[464,128]{1,0:T(8,128)S(1)}, u32[]{:S(2)}, u32[]{:S(2)}) %collective-permute-start.1) | collective-permute-done | bytes 237600 | tf_op jit(solution)/shard_map/ppermute | solution.py:306
  18.4 1.0 %shard_map.60 = (f32[144,128]{1,0:T(8,128)S(1)}, f32[144,128]{1,0:T(8,128)S(1)}) custom-call(f32[768,128]{1,0:T(8,128)S(1)} %get-tuple-element.17.core_ref, f32[32,128]{1,0:T(8,128)S(1)} %get-tuple-element.16.mk_ref, f32[464,128]{1,0:T(8,128)S(1)} %collective-permute-done.up_ref, f32[464,128]{1,0:T(8,128)S(1)} %collective-permute-done.1.down_ref), custom_call_target="tpu_custom_call" | custom-call | tf_op jit(solution)/shard_map/pallas_call | solution.py:328
  19.4 0.0 collective-permute-start.2
  19.4 7.3 %collective-permute-start.3 = (f32[144,128]{1,0:T(8,128)S(1)}, f32[144,128]{1,0:T(8,128)S(1)}, u32[]{:S(2)}, u32[]{:S(2)}) collective-permute-start(f32[144,128]{1,0:T(8,128)S(1)} %get-tuple-element.21), channel_id=1, source_target_pairs={{0,15},{1,0},{2,1},{3,2},{4,3},{5,4},{6,5},{7,6},{8,7},{9,8},{10,9... | collective-permute-start | bytes 221192 | tf_op jit(solution)/shard_map/ppermute | solution.py:306
  26.7 2.0 %collective-permute-done.2.rl_ref = f32[144,128]{1,0:T(8,128)S(1)} collective-permute-done((f32[144,128]{1,0:T(8,128)S(1)}, f32[144,128]{1,0:T(8,128)S(1)}, u32[]{:S(2)}, u32[]{:S(2)}) %collective-permute-start.2) | collective-permute-done | bytes 73760 | tf_op jit(solution)/shard_map/ppermute | solution.py:306
  28.8 0.0 collective-permute-done.3.rr_ref
  28.8 7.6 %shard_map.61 = (f32[392,128]{1,0:T(8,128)S(1)}, f32[336,128]{1,0:T(8,128)S(1)}, f32[280,128]{1,0:T(8,128)S(1)}, f32[8,48,128]{2,1,0:T(8,128)S(1)}, f32[768,128]{1,0:T(8,128)S(1)}, /*index=5*/f32[6,16,256]{2,1,0:T(8,128)S(1)}) custom-call(f32[1]{0:T(128)} %bitcast.1.later_ref, f32[768,128]{1,0:T(8,128)S(1)} %get-tuple-element.17.core_ref, ...), custom_call_target="tpu_custom_call" | custom-call | tf_op jit(solution)/shard_map/pallas_call | solution.py:331
  36.4 3.1 %collective-permute-start.7 = (f32[768,128]{1,0:T(8,128)S(1)}, f32[768,128]{1,0:T(8,128)S(1)}, u32[]{:S(2)}, u32[]{:S(2)}) collective-permute-start(f32[768,128]{1,0:T(8,128)S(1)} %get-tuple-element.27.rest_ref), channel_id=1, source_target_pairs={{0,128},{128,256},{256,384},{1,129},{129,257},{257,385},{2,130},{1... | collective-permute-start | bytes 1179656 | tf_op jit(solution)/shard_map/ppermute | solution.py:306
  39.5 0.7 %collective-permute-start.4 = (f32[392,128]{1,0:T(8,128)S(1)}, f32[392,128]{1,0:T(8,128)S(1)}, u32[]{:S(2)}, u32[]{:S(2)}) collective-permute-start(f32[392,128]{1,0:T(8,128)S(1)} %get-tuple-element.23), channel_id=1, source_target_pairs={{0,384},{1,385},{2,386},{3,387},{4,388},{5,389},{6,390},{7,391},{8... | collective-permute-start | bytes 602120 | tf_op jit(solution)/shard_map/ppermute | solution.py:306
  40.2 1.3 %collective-permute-start.5 = (f32[336,128]{1,0:T(8,128)S(1)}, f32[336,128]{1,0:T(8,128)S(1)}, u32[]{:S(2)}, u32[]{:S(2)}) collective-permute-start(f32[336,128]{1,0:T(8,128)S(1)} %get-tuple-element.24), channel_id=1, source_target_pairs={{0,256},{128,384},{1,257},{129,385},{2,258},{130,386},{3,259},{131... | collective-permute-start | bytes 516104 | tf_op jit(solution)/shard_map/ppermute | solution.py:306
  41.5 1.9 %collective-permute-start.6 = (f32[280,128]{1,0:T(8,128)S(1)}, f32[280,128]{1,0:T(8,128)S(1)}, u32[]{:S(2)}, u32[]{:S(2)}) collective-permute-start(f32[280,128]{1,0:T(8,128)S(1)} %get-tuple-element.25), channel_id=1, source_target_pairs={{0,128},{128,256},{256,384},{1,129},{129,257},{257,385},{2,130},{1... | collective-permute-start | bytes 430088 | tf_op jit(solution)/shard_map/ppermute | solution.py:306
  43.4 9.6 %collective-permute-done.6.q1_ref = f32[280,128]{1,0:T(8,128)S(1)} collective-permute-done((f32[280,128]{1,0:T(8,128)S(1)}, f32[280,128]{1,0:T(8,128)S(1)}, u32[]{:S(2)}, u32[]{:S(2)}) %collective-permute-start.6) | collective-permute-done | bytes 143392 | tf_op jit(solution)/shard_map/ppermute | solution.py:306
  53.0 0.0 collective-permute-done.5.q2_ref
  53.0 0.0 collective-permute-done.4.q3_ref
  53.0 3.2 %shard_map.62 = (f32[768,128]{1,0:T(8,128)}, f32[8,48,128]{2,1,0:T(8,128)S(1)}) custom-call(f32[32,128]{1,0:T(8,128)S(1)} %get-tuple-element.16.mk_ref, f32[48,48]{1,0:T(8,128)S(1)} %copy-done.2, f32[6,16,256]{2,1,0:T(8,128)S(1)} %get-tuple-element.22.cc_ref, f32[392,128]{1,0:T(8,128)S(1)} %collective-permute-done.4.q3_ref, ...), custom_call_target="tpu_custom_call" | custom-call | tf_op jit(solution)/shard_map/pallas_call | solution.py:336
  56.2 0.9 %shard_map.63 = f32[768,128]{1,0:T(8,128)} custom-call(f32[1]{0:T(128)} %bitcast.1.later_ref, f32[32,128]{1,0:T(8,128)S(1)} %get-tuple-element.16.mk_ref, f32[768,128]{1,0:T(8,128)S(1)} %bitcast.5, f32[8,48,128]{2,1,0:T(8,128)S(1)} %get-tuple-element.29.y_ref, f32[768,128]{1,0:T(8,128)S(1)} %collective-permute-done.7.rest_ref), custom_call_target="tpu_custom_call" | custom-call | tf_op jit(solution)/shard_map/pallas_call | solution.py:342
  (7 shorter events, 0.0 us)
Async XLA Ops:
  0.6 1.0 %copy-start = (f32[1,48,16,128]{3,2,1,0:T(8,128)S(1)}, f32[1,48,16,128]{3,2,1,0:T(8,128)}, u32[]{:S(2)}) copy-start(f32[1,48,16,128]{3,2,1,0:T(8,128)} %param.4) | copy-start | bytes 1179652
  1.6 0.7 %copy-start.3 = (s32[16,128]{1,0:T(8,128)S(1)}, s32[16,128]{1,0:T(8,128)}, u32[]{:S(2)}) copy-start(s32[16,128]{1,0:T(8,128)} %wet_hbm.1) | copy-start | bytes 24580
  2.3 0.7 %copy-start.4 = (f32[16,128]{1,0:T(8,128)S(1)}, f32[16,128]{1,0:T(8,128)}, u32[]{:S(2)}) copy-start(f32[16,128]{1,0:T(8,128)} %kap_hbm.1) | copy-start | bytes 24580
  3.4 9.7 %collective-permute-start = (f32[464,128]{1,0:T(8,128)S(1)}, f32[464,128]{1,0:T(8,128)S(1)}, u32[]{:S(2)}, u32[]{:S(2)}) collective-permute-start(f32[464,128]{1,0:T(8,128)S(1)} %get-tuple-element.18), channel_id=1, source_target_pairs={{0,16},{16,32},{32,48},{48,64},{64,80},{80,96},{96,112},{1,17},{17... | collective-permute-start | bytes 712712 | tf_op jit(solution)/shard_map/ppermute | solution.py:306
  8.1 10.3 %collective-permute-start.1 = (f32[464,128]{1,0:T(8,128)S(1)}, f32[464,128]{1,0:T(8,128)S(1)}, u32[]{:S(2)}, u32[]{:S(2)}) collective-permute-start(f32[464,128]{1,0:T(8,128)S(1)} %get-tuple-element.19), channel_id=1, source_target_pairs={{16,0},{32,16},{48,32},{64,48},{80,64},{96,80},{112,96},{17,1},{33... | collective-permute-start | bytes 712712 | tf_op jit(solution)/shard_map/ppermute | solution.py:306
  18.4 10.3 %copy-start.2 = (f32[48,48]{1,0:T(8,128)S(1)}, f32[48,48]{1,0:T(8,128)}, u32[]{:S(2)}) copy-start(f32[48,48]{1,0:T(8,128)} %mix_ref.3) | copy-start | bytes 27652
  19.4 9.3 %collective-permute-start.2 = (f32[144,128]{1,0:T(8,128)S(1)}, f32[144,128]{1,0:T(8,128)S(1)}, u32[]{:S(2)}, u32[]{:S(2)}) collective-permute-start(f32[144,128]{1,0:T(8,128)S(1)} %get-tuple-element.20), channel_id=1, source_target_pairs={{0,1},{1,2},{2,3},{3,4},{4,5},{5,6},{6,7},{7,8},{8,9},{9,10},{10,1... | collective-permute-start | bytes 221192 | tf_op jit(solution)/shard_map/ppermute | solution.py:306
  19.4 9.3 %collective-permute-start.3 = (f32[144,128]{1,0:T(8,128)S(1)}, f32[144,128]{1,0:T(8,128)S(1)}, u32[]{:S(2)}, u32[]{:S(2)}) collective-permute-start(f32[144,128]{1,0:T(8,128)S(1)} %get-tuple-element.21), channel_id=1, source_target_pairs={{0,15},{1,0},{2,1},{3,2},{4,3},{5,4},{6,5},{7,6},{8,7},{9,8},{10,9... | collective-permute-start | bytes 221192 | tf_op jit(solution)/shard_map/ppermute | solution.py:306
  36.4 19.9 %collective-permute-start.7 = (f32[768,128]{1,0:T(8,128)S(1)}, f32[768,128]{1,0:T(8,128)S(1)}, u32[]{:S(2)}, u32[]{:S(2)}) collective-permute-start(f32[768,128]{1,0:T(8,128)S(1)} %get-tuple-element.27.rest_ref), channel_id=1, source_target_pairs={{0,128},{128,256},{256,384},{1,129},{129,257},{257,385},{2,130},{1... | collective-permute-start | bytes 1179656 | tf_op jit(solution)/shard_map/ppermute | solution.py:306
  39.5 13.5 %collective-permute-start.4 = (f32[392,128]{1,0:T(8,128)S(1)}, f32[392,128]{1,0:T(8,128)S(1)}, u32[]{:S(2)}, u32[]{:S(2)}) collective-permute-start(f32[392,128]{1,0:T(8,128)S(1)} %get-tuple-element.23), channel_id=1, source_target_pairs={{0,384},{1,385},{2,386},{3,387},{4,388},{5,389},{6,390},{7,391},{8... | collective-permute-start | bytes 602120 | tf_op jit(solution)/shard_map/ppermute | solution.py:306
  40.2 12.8 %collective-permute-start.5 = (f32[336,128]{1,0:T(8,128)S(1)}, f32[336,128]{1,0:T(8,128)S(1)}, u32[]{:S(2)}, u32[]{:S(2)}) collective-permute-start(f32[336,128]{1,0:T(8,128)S(1)} %get-tuple-element.24), channel_id=1, source_target_pairs={{0,256},{128,384},{1,257},{129,385},{2,258},{130,386},{3,259},{131... | collective-permute-start | bytes 516104 | tf_op jit(solution)/shard_map/ppermute | solution.py:306
  41.5 11.5 %collective-permute-start.6 = (f32[280,128]{1,0:T(8,128)S(1)}, f32[280,128]{1,0:T(8,128)S(1)}, u32[]{:S(2)}, u32[]{:S(2)}) collective-permute-start(f32[280,128]{1,0:T(8,128)S(1)} %get-tuple-element.25), channel_id=1, source_target_pairs={{0,128},{128,256},{256,384},{1,129},{129,257},{257,385},{2,130},{1... | collective-permute-start | bytes 430088 | tf_op jit(solution)/shard_map/ppermute | solution.py:306
  53.0 3.2 %copy-start.1 = (f32[1,48,16,128]{3,2,1,0:T(8,128)S(1)}, f32[1,48,16,128]{3,2,1,0:T(8,128)}, u32[]{:S(2)}) copy-start(f32[1,48,16,128]{3,2,1,0:T(8,128)} %param.4) | copy-start | bytes 1179652

commit v3 on v2

--- a/solution.py
+++ b/solution.py
@@ -13,6 +13,7 @@
 H = 9
 E = R + 2 * H
 W = 2 * C
+REACH = 3
 G = K // 8
 SLOT = 2 * H
 BASE = R - H
@@ -30,30 +31,16 @@
     return pltpu.roll(x, by % x.shape[-1], x.ndim - 1)
 
 
-def halo_kernel(
-    x_hbm, wet_hbm, kap_hbm, top_ref, bot_ref, core_ref, mk_ref, x_ref, wet_ref, kap_ref, sems
-):
-    copies = [
-        pltpu.make_async_copy(src, dst, sems.at[i])
-        for i, (src, dst) in enumerate(
-            ((wet_hbm, wet_ref), (kap_hbm, kap_ref), (x_hbm, x_ref))
-        )
-    ]
-    for copy in copies:
-        copy.start()
-    for copy in copies:
-        copy.wait()
-    mask = wet_ref[...].astype(jnp.float32)
+def halo_kernel(x_ref, mk_ref, top_ref, bot_ref, core_ref):
     for r in range(R):
-        row = x_ref[pl.ds(r, K, stride=R), :] * mask[r : r + 1]
+        row = x_ref[pl.ds(r, K, stride=R), :] * mk_ref[r : r + 1]
         core_ref[pl.ds(r * K, K), :] = row
         if r < H:
             top_ref[pl.ds(r * K, K), :] = row
         if r >= R - H:
             bot_ref[pl.ds((r - R + H) * K, K), :] = row
-    for ref, first in ((top_ref, H * K), (bot_ref, H * K), (mk_ref, 0)):
-        ref[pl.ds(first, R), :] = mask
-        ref[pl.ds(first + R, R), :] = kap_ref[...]
+    for ref in (top_ref, bot_ref):
+        ref[pl.ds(H * K, 2 * R), :] = mk_ref[...]
 
 
 def pack_row(row):
@@ -153,9 +140,52 @@
         write(2 * p + 1, by_tile(lambda t: shift(t, -1), both))
 
 
+RING = [*range(REACH), *range(R - REACH, R)]
+SIDE = range(2, 6)
+
+
+def put_ring(src, out_ref):
+    for i, r in enumerate(RING):
+        out_ref[pl.ds(i * K, K), :] = src[H + r, :, :C]
+    at = lanes((8, C)) % SLOT
+    for i, r in enumerate(SIDE):
+        a, b, c = (pack_row(src[H + r + d, :, :C]) for d in (0, 4, 8))
+        both = jnp.where(at < 2 * REACH, shift(a, -2 * REACH), b)
+        both = jnp.where(at < 4 * REACH, both, shift(c, 2 * REACH))
+        out_ref[pl.ds(len(RING) * K + 8 * i, 8), :] = both
+
+
+def take_ring(in_ref, inner_ref):
+    rows = {r: in_ref[pl.ds(i * K, K), :] for i, r in enumerate(RING)}
+    lane = lanes((K, C))
+    inside = (lane >= REACH) & (lane < C - REACH)
+    for i, r in enumerate(SIDE):
+        packed = in_ref[pl.ds(len(RING) * K + 8 * i, 8), :]
+        for d, by in ((0, 2 * REACH), (4, 0), (8, -2 * REACH)):
+            if r + d not in rows:
+                ends = unpack_row(shift(packed, by))
+                rows[r + d] = jnp.where(inside, inner_ref[pl.ds((r + d) * K, K), :], ends)
+    return [rows[r] for r in range(R)]
+
+
+def inner_kernel(core_ref, mix_ref, cf_ref, out_ref, ua, ub):
+    mix = level_matrix(mix_ref[...])
+    for r in range(R):
+        ua[r] = core_ref[pl.ds(r * K, K), :]
+    for margin, src, dst in ((1, ua, ub), (2, ub, ua), (3, ua, None)):
+        for r in range(margin, R - margin):
+            value = stencil(cf_ref, r, 1, src[r], src[r - 1], src[r + 1], mix)
+            if dst is None:
+                out_ref[pl.ds(r * K, K), :] = value
+            else:
+                dst[r] = value
+    for r in RING:
+        out_ref[pl.ds(r * K, K), :] = jnp.zeros((K, C), jnp.float32)
+
+
 def fine_kernel(
     later_ref, core_ref, mk_ref, mix_ref, up_ref, down_ref, rl_ref, rr_ref,
-    q3_ref, q2_ref, q1_ref, q0_ref, rest_ref, cc_ref,
+    q3_ref, q2_ref, q1_ref, q0_ref, ring_ref, rest_ref, cc_ref, fc_ref,
     ua, ub, mk, cf, rs, qs,
 ):
     half = (E + 2) // 2
@@ -219,6 +249,9 @@
         q0_ref[i] = qs[4 + i, :, :C]
         for r in (2 * i, 2 * i + 1):
             rest_ref[pl.ds(r * K, K), :] = ub[H + r, :, :C] - mk_ref[pl.ds(r, 1), :] * fc
+    put_ring(ub, ring_ref)
+    for i in range(5):
+        fc_ref[i] = cf[i, pl.ds(R, R), :C]
     put_q(qs, q3_ref, 1, 14)
     put_q(qs, q2_ref, 2, 12)
     put_q(qs, q1_ref, 3, 10)
@@ -246,7 +279,7 @@
     take_q(q1_ref, 10, put(a, 3))
     step(b, a, 3, 10)
     for i in range(8):
-        y_ref[i] = spread(a[4 + i, :, :C])
+        y_ref[i] = a[4 + i, :, :C]
         z = q0_ref[i] + stencil(cc_ref, 4 + i, 2, a[4 + i], a[3 + i], a[5 + i], coarse_mix)[:, :C]
         z = spread(z)
         for r in (2 * i, 2 * i + 1):
@@ -254,7 +287,7 @@
             out_ref[pl.ds(r, K, stride=R), :] = value
 
 
-def last_kernel(later_ref, mk_ref, x_ref, y_ref, rest_ref, out_ref):
+def last_kernel(later_ref, mk_ref, cc_ref, x_ref, y_ref, ring_ref, inner_ref, out_ref):
     first = later_ref[0] == 0.0
 
     @pl.when(first)
@@ -263,20 +296,25 @@
 
     @pl.when(jnp.logical_not(first))
     def _():
-        for r in range(R):
-            value = rest_ref[pl.ds(r * K, K), :] + mk_ref[pl.ds(r, 1), :] * y_ref[r // 2]
-            out_ref[pl.ds(r, K, stride=R), :] = value
+        rows = take_ring(ring_ref, inner_ref)
+        for i in range(R // 2):
+            above, below = rows[2 * i], rows[2 * i + 1]
+            total = above + below
+            fc = (total + shift(total, -1)) * cc_ref[5, 4 + i : 5 + i, :C]
+            jump = spread(y_ref[i] - fc)
+            for r, value in ((2 * i, above), (2 * i + 1, below)):
+                out_ref[pl.ds(r, K, stride=R), :] = value + mk_ref[pl.ds(r, 1), :] * jump
 
 
 def f32(*shape):
     return jax.ShapeDtypeStruct(shape, jnp.float32)
 
 
-def call(kernel, n_in, outs, scratch=(), smem=0, spec=VMEM):
+def call(kernel, n_in, outs, scratch=(), smem=0):
     return pl.pallas_call(
         kernel,
         out_shape=outs,
-        in_specs=[SMEM] * smem + [spec] * (n_in - smem),
+        in_specs=[SMEM] * smem + [VMEM] * (n_in - smem),
         out_specs=jax.tree.map(lambda _: VMEM, outs),
         scratch_shapes=list(scratch),
         compiler_params=PARAMS,
@@ -287,7 +325,7 @@
     return call(
         fine_kernel,
         8,
-        (f32(49 * 8, C), f32(42 * 8, C), f32(35 * 8, C), f32(8, K, C), f32(R * K, C), f32(6, NC, W)),
+        (f32(49 * 8, C), f32(42 * 8, C), f32(35 * 8, C), f32(8, K, C), f32(40 * 8, C), f32(R * K, C), f32(6, NC, W), f32(5, R, C)),
         [
             pltpu.VMEM((E, K, W), jnp.float32),
             pltpu.VMEM((E, K, W), jnp.float32),
@@ -310,36 +348,35 @@
     x = start.reshape(K * R, C)
     later = (lax.axis_index("tm") > 0).astype(jnp.float32).reshape(1)
     send = H * K + 2 * R
-    top, bottom, core, mk = call(
-        halo_kernel,
-        3,
-        (f32(send, C), f32(send, C), f32(R * K, C), f32(2 * R, C)),
-        [
-            pltpu.VMEM((K * R, C), jnp.float32),
-            pltpu.VMEM((R, C), jnp.int32),
-            pltpu.VMEM((R, C), jnp.float32),
-            pltpu.SemaphoreType.DMA((3,)),
-        ],
-        spec=pl.BlockSpec(memory_space=pl.ANY),
-    )(x, wet, kappa)
+    mk = jnp.concatenate([wet.astype(jnp.float32), kappa], axis=0)
+    top, bottom, core = call(halo_kernel, 2, (f32(send, C), f32(send, C), f32(R * K, C)))(x, mk)
     down = moved(top, "lat", -1)
     up = moved(bottom, "lat", 1)
     side = (E + 2) * 4
     left, right = call(edge_kernel, 4, (f32(side, C), f32(side, C)))(core, mk, up, down)
     from_left = moved(left, "lon", 1, True)
     from_right = moved(right, "lon", -1, True)
-    q3, q2, q1, q0, rest, cc = fine_call()(
+    before = moved(core, "tm", 1)
+    q3, q2, q1, q0, ring, rest, cc, cf = fine_call()(
         later, core, mk, mixing, up, down, from_left, from_right
     )
     q3, q2, q1 = moved(q3, "tm", 3), moved(q2, "tm", 2), moved(q1, "tm", 1)
-    rest_before = moved(rest, "tm", 1)
+    ring_before = moved(ring, "tm", 1)
+    inner = call(
+        inner_kernel,
+        3,
+        f32(R * K, C),
+        [pltpu.VMEM((R, K, C), jnp.float32), pltpu.VMEM((R, K, C), jnp.float32)],
+    )(before, mixing, cf)
     out, y = call(
         sweep_kernel,
         8,
         (f32(K * R, C), f32(8, K, C)),
         [pltpu.VMEM((NC, K, W), jnp.float32), pltpu.VMEM((NC, K, W), jnp.float32)],
     )(mk, mixing, cc, q3, q2, q1, q0, rest)
-    following = call(last_kernel, 5, f32(K * R, C), smem=1)(later, mk, x, y, rest_before)
+    following = call(last_kernel, 7, f32(K * R, C), smem=1)(
+        later, mk, cc, x, y, ring_before, inner
+    )
     return out.reshape(1, K, R, C), following.reshape(1, K, R, C)
 
 

time: 57.6 us -> 55.3 us (0.960)
  the two profiles are of different devices: /device:TPU:28 before, /device:TPU:26 now
where the time goes in v3:
time: 55.3 us; the launch traced here: 55 us
  starting transfers between devices  26.5 us (48%)
  Pallas kernels  14 us (25%)
  waiting for transfers between devices  12 us (22%)
  local copies, waits for them, and re-layouts  1.01 us (2%)
  between operations  0.75 us (1%)
  other arithmetic  0.71 us (1%)
    ppermute x9, starting transfers between devices, moved(): return lax.ppermute(value, axis, pairs)  26.5 us
    ppermute x9, waiting for transfers between devices, moved(): return lax.ppermute(value, axis, pairs)  12 us
    pallas_call x1, Pallas kernels, body(): fine_call()(later, core, mk, mixing, up, down, from_left, from_right)  7.93 us
    pallas_call x1, Pallas kernels, body(): call(sweep_kernel, 8, (f32(K * R, C), f32(8, K, C)), [pltpu.VMEM((NC, K,...  3.04 us
    pallas_call x1, Pallas kernels, body(): call(last_kernel, 7, f32(K * R, C), smem=1)  1.24 us
  transfers between devices with their start and end apart: 9, of which 3 were waited for; matrix products, arithmetic and copies ran while one was open for 0% of the time, Pallas kernels for 23%

profile of v3, /device:TPU:26, one launch (start us, length us, event | category | flops | bytes accessed | tf_op | source)
XLA Modules:
  0.0 55.0 jit_solution(5450707682524042857)
XLA Ops:
  0.6 0.7 %convert_element_type.4 = f32[16,128]{1,0:T(8,128)S(1)} convert(s32[16,128]{1,0:T(8,128)} %param.5) | non-fusion elementwise | flops 2048 | bytes 16384 | tf_op jit(solution)/shard_map/convert_element_type | solution.py:351
  1.4 1.0 %copy-done = f32[1,48,16,128]{3,2,1,0:T(8,128)S(1)} copy-done((f32[1,48,16,128]{3,2,1,0:T(8,128)S(1)}, f32[1,48,16,128]{3,2,1,0:T(8,128)}, u32[]{:S(2)}) %copy-start) | copy-done | bytes 393240
  2.3 0.1 shard_map.59
  2.5 4.7 %collective-permute-start = (f32[464,128]{1,0:T(8,128)S(1)}, f32[464,128]{1,0:T(8,128)S(1)}, u32[]{:S(2)}, u32[]{:S(2)}) collective-permute-start(f32[464,128]{1,0:T(8,128)S(1)} %get-tuple-element.18), channel_id=1, source_target_pairs={{0,16},{16,32},{32,48},{48,64},{64,80},{80,96},{96,112},{1,17},{17... | collective-permute-start | bytes 712712 | tf_op jit(solution)/shard_map/ppermute | solution.py:344
  7.2 1.9 %collective-permute-start.1 = (f32[464,128]{1,0:T(8,128)S(1)}, f32[464,128]{1,0:T(8,128)S(1)}, u32[]{:S(2)}, u32[]{:S(2)}) collective-permute-start(f32[464,128]{1,0:T(8,128)S(1)} %get-tuple-element.19), channel_id=1, source_target_pairs={{16,0},{32,16},{48,32},{64,48},{80,64},{96,80},{112,96},{17,1},{33... | collective-permute-start | bytes 712712 | tf_op jit(solution)/shard_map/ppermute | solution.py:344
  9.1 3.4 %collective-permute-start.8 = (f32[768,128]{1,0:T(8,128)S(1)}, f32[768,128]{1,0:T(8,128)S(1)}, u32[]{:S(2)}, u32[]{:S(2)}) collective-permute-start(f32[768,128]{1,0:T(8,128)S(1)} %get-tuple-element.17.core_ref), channel_id=1, source_target_pairs={{0,128},{128,256},{256,384},{1,129},{129,257},{257,385},{2,130},{1... | collective-permute-start | bytes 1179656 | tf_op jit(solution)/shard_map/ppermute | solution.py:344
  12.5 0.0 collective-permute-done.up_ref
  12.5 5.0 %collective-permute-done.1.down_ref = f32[464,128]{1,0:T(8,128)S(1)} collective-permute-done((f32[464,128]{1,0:T(8,128)S(1)}, f32[464,128]{1,0:T(8,128)S(1)}, u32[]{:S(2)}, u32[]{:S(2)}) %collective-permute-start.1) | collective-permute-done | bytes 237600 | tf_op jit(solution)/shard_map/ppermute | solution.py:344
  17.5 1.0 %shard_map.60 = (f32[144,128]{1,0:T(8,128)S(1)}, f32[144,128]{1,0:T(8,128)S(1)}) custom-call(f32[768,128]{1,0:T(8,128)S(1)} %get-tuple-element.17.core_ref, f32[32,128]{1,0:T(8,128)S(1)} %pad_maximum_fusion.mk_ref, f32[464,128]{1,0:T(8,128)S(1)} %collective-permute-done.up_ref, f32[464,128]{1,0:T(8,128)S(1)} %collective-permute-done.1.down_ref), custom_call_target="tpu_custom_call" | custom-call | tf_op jit(solution)/shard_map/pallas_call | solution.py:356
  18.5 0.0 collective-permute-start.2
  18.5 7.3 %collective-permute-start.3 = (f32[144,128]{1,0:T(8,128)S(1)}, f32[144,128]{1,0:T(8,128)S(1)}, u32[]{:S(2)}, u32[]{:S(2)}) collective-permute-start(f32[144,128]{1,0:T(8,128)S(1)} %get-tuple-element.21), channel_id=1, source_target_pairs={{0,15},{1,0},{2,1},{3,2},{4,3},{5,4},{6,5},{7,6},{8,7},{9,8},{10,9... | collective-permute-start | bytes 221192 | tf_op jit(solution)/shard_map/ppermute | solution.py:344
  25.8 2.0 %collective-permute-done.2.rl_ref = f32[144,128]{1,0:T(8,128)S(1)} collective-permute-done((f32[144,128]{1,0:T(8,128)S(1)}, f32[144,128]{1,0:T(8,128)S(1)}, u32[]{:S(2)}, u32[]{:S(2)}) %collective-permute-start.2) | collective-permute-done | bytes 73760 | tf_op jit(solution)/shard_map/ppermute | solution.py:344
  27.9 0.0 collective-permute-done.3.rr_ref
  27.9 7.9 %shard_map.61 = (f32[392,128]{1,0:T(8,128)S(1)}, f32[336,128]{1,0:T(8,128)S(1)}, f32[280,128]{1,0:T(8,128)S(1)}, f32[8,48,128]{2,1,0:T(8,128)S(1)}, f32[320,128]...) custom-call(f32[1]{0:T(128)} %bitcast.later_ref, ...), custom_call_target="tpu_custom_call" | custom-call | tf_op jit(solution)/shard_map/pallas_call | solution.py:360
  35.8 0.7 %collective-permute-start.4 = (f32[392,128]{1,0:T(8,128)S(1)}, f32[392,128]{1,0:T(8,128)S(1)}, u32[]{:S(2)}, u32[]{:S(2)}) collective-permute-start(f32[392,128]{1,0:T(8,128)S(1)} %get-tuple-element.23), channel_id=1, source_target_pairs={{0,384},{1,385},{2,386},{3,387},{4,388},{5,389},{6,390},{7,391},{8... | collective-permute-start | bytes 602120 | tf_op jit(solution)/shard_map/ppermute | solution.py:344
  36.5 4.7 %collective-permute-start.5 = (f32[336,128]{1,0:T(8,128)S(1)}, f32[336,128]{1,0:T(8,128)S(1)}, u32[]{:S(2)}, u32[]{:S(2)}) collective-permute-start(f32[336,128]{1,0:T(8,128)S(1)} %get-tuple-element.24), channel_id=1, source_target_pairs={{0,256},{128,384},{1,257},{129,385},{2,258},{130,386},{3,259},{131... | collective-permute-start | bytes 516104 | tf_op jit(solution)/shard_map/ppermute | solution.py:344
  41.1 1.9 %collective-permute-start.7 = (f32[320,128]{1,0:T(8,128)S(1)}, f32[320,128]{1,0:T(8,128)S(1)}, u32[]{:S(2)}, u32[]{:S(2)}) collective-permute-start(f32[320,128]{1,0:T(8,128)S(1)} %get-tuple-element.30), channel_id=1, source_target_pairs={{0,128},{128,256},{256,384},{1,129},{129,257},{257,385},{2,130},{1... | collective-permute-start | bytes 491528 | tf_op jit(solution)/shard_map/ppermute | solution.py:344
  43.1 1.9 %collective-permute-start.6 = (f32[280,128]{1,0:T(8,128)S(1)}, f32[280,128]{1,0:T(8,128)S(1)}, u32[]{:S(2)}, u32[]{:S(2)}) collective-permute-start(f32[280,128]{1,0:T(8,128)S(1)} %get-tuple-element.25), channel_id=1, source_target_pairs={{0,128},{128,256},{256,384},{1,129},{129,257},{257,385},{2,130},{1... | collective-permute-start | bytes 430088 | tf_op jit(solution)/shard_map/ppermute | solution.py:344
  45.0 0.0 collective-permute-done.8.core_ref
  45.0 0.7 %shard_map.63.inner_ref = f32[768,128]{1,0:T(8,128)S(1)} custom-call(f32[768,128]{1,0:T(8,128)S(1)} %collective-permute-done.8.core_ref, f32[48,48]{1,0:T(8,128)S(1)} %copy-done.2, f32[5,16,128]{2,1,0:T(8,128)S(1)} %get-tuple-element.31.cf_ref), custom_call_target="tpu_custom_call" | custom-call | tf_op jit(solution)/shard_map/pallas_call | solution.py:365
  45.7 5.0 %collective-permute-done.6.q1_ref = f32[280,128]{1,0:T(8,128)S(1)} collective-permute-done((f32[280,128]{1,0:T(8,128)S(1)}, f32[280,128]{1,0:T(8,128)S(1)}, u32[]{:S(2)}, u32[]{:S(2)}) %collective-permute-start.6) | collective-permute-done | bytes 143392 | tf_op jit(solution)/shard_map/ppermute | solution.py:344
  50.7 0.0 collective-permute-done.5.q2_ref
  50.7 3.0 %shard_map.62 = (f32[768,128]{1,0:T(8,128)}, f32[8,48,128]{2,1,0:T(8,128)S(1)}) custom-call(f32[32,128]{1,0:T(8,128)S(1)} %pad_maximum_fusion.mk_ref, f32[48,48]{1,0:T(8,128)S(1)} %copy-done.2, f32[6,16,256]{2,1,0:T(8,128)S(1)} %get-tuple-element.22.cc_ref, f32[392,128]{1,0:T(8,128)S(1)} %collective-permute-done.4.q3_ref, ...), custom_call_target="tpu_custom_call" | custom-call | tf_op jit(solution)/shard_map/pallas_call | solution.py:371
  53.8 1.2 %shard_map.64 = f32[768,128]{1,0:T(8,128)} custom-call(f32[1]{0:T(128)} %bitcast.later_ref, f32[32,128]{1,0:T(8,128)S(1)} %pad_maximum_fusion.mk_ref, f32[6,16,256]{2,1,0:T(8,128)S(1)} %get-tuple-element.22.cc_ref, f32[768,128]{1,0:T(8,128)S(1)} %bitcast.5, f32[8,48,128]{2,1,0:T(8,128)S(1)} %get-tuple-element.29.y_ref, ...), custom_call_target="tpu_custom_call" | custom-call | tf_op jit(solution)/shard_map/pallas_call | solution.py:377
  (10 shorter events, 0.0 us)
Async XLA Ops:
  0.6 0.7 %copy-start.3 = (f32[16,128]{1,0:T(8,128)S(1)}, f32[16,128]{1,0:T(8,128)}, u32[]{:S(2)}) copy-start(f32[16,128]{1,0:T(8,128)} %param.6) | copy-start | bytes 24580
  1.4 1.0 %copy-start = (f32[1,48,16,128]{3,2,1,0:T(8,128)S(1)}, f32[1,48,16,128]{3,2,1,0:T(8,128)}, u32[]{:S(2)}) copy-start(f32[1,48,16,128]{3,2,1,0:T(8,128)} %param.4) | copy-start | bytes 1179652
  2.5 10.0 %collective-permute-start = (f32[464,128]{1,0:T(8,128)S(1)}, f32[464,128]{1,0:T(8,128)S(1)}, u32[]{:S(2)}, u32[]{:S(2)}) collective-permute-start(f32[464,128]{1,0:T(8,128)S(1)} %get-tuple-element.18), channel_id=1, source_target_pairs={{0,16},{16,32},{32,48},{48,64},{64,80},{80,96},{96,112},{1,17},{17... | collective-permute-start | bytes 712712 | tf_op jit(solution)/shard_map/ppermute | solution.py:344
  7.2 10.3 %collective-permute-start.1 = (f32[464,128]{1,0:T(8,128)S(1)}, f32[464,128]{1,0:T(8,128)S(1)}, u32[]{:S(2)}, u32[]{:S(2)}) collective-permute-start(f32[464,128]{1,0:T(8,128)S(1)} %get-tuple-element.19), channel_id=1, source_target_pairs={{16,0},{32,16},{48,32},{64,48},{80,64},{96,80},{112,96},{17,1},{33... | collective-permute-start | bytes 712712 | tf_op jit(solution)/shard_map/ppermute | solution.py:344
  9.1 35.9 %collective-permute-start.8 = (f32[768,128]{1,0:T(8,128)S(1)}, f32[768,128]{1,0:T(8,128)S(1)}, u32[]{:S(2)}, u32[]{:S(2)}) collective-permute-start(f32[768,128]{1,0:T(8,128)S(1)} %get-tuple-element.17.core_ref), channel_id=1, source_target_pairs={{0,128},{128,256},{256,384},{1,129},{129,257},{257,385},{2,130},{1... | collective-permute-start | bytes 1179656 | tf_op jit(solution)/shard_map/ppermute | solution.py:344
  17.5 10.3 %copy-start.2 = (f32[48,48]{1,0:T(8,128)S(1)}, f32[48,48]{1,0:T(8,128)}, u32[]{:S(2)}) copy-start(f32[48,48]{1,0:T(8,128)} %mix_ref.5) | copy-start | bytes 27652
  18.5 9.3 %collective-permute-start.2 = (f32[144,128]{1,0:T(8,128)S(1)}, f32[144,128]{1,0:T(8,128)S(1)}, u32[]{:S(2)}, u32[]{:S(2)}) collective-permute-start(f32[144,128]{1,0:T(8,128)S(1)} %get-tuple-element.20), channel_id=1, source_target_pairs={{0,1},{1,2},{2,3},{3,4},{4,5},{5,6},{6,7},{7,8},{8,9},{9,10},{10,1... | collective-permute-start | bytes 221192 | tf_op jit(solution)/shard_map/ppermute | solution.py:344
  18.5 9.3 %collective-permute-start.3 = (f32[144,128]{1,0:T(8,128)S(1)}, f32[144,128]{1,0:T(8,128)S(1)}, u32[]{:S(2)}, u32[]{:S(2)}) collective-permute-start(f32[144,128]{1,0:T(8,128)S(1)} %get-tuple-element.21), channel_id=1, source_target_pairs={{0,15},{1,0},{2,1},{3,2},{4,3},{5,4},{6,5},{7,6},{8,7},{9,8},{10,9... | collective-permute-start | bytes 221192 | tf_op jit(solution)/shard_map/ppermute | solution.py:344
  35.8 14.9 %collective-permute-start.4 = (f32[392,128]{1,0:T(8,128)S(1)}, f32[392,128]{1,0:T(8,128)S(1)}, u32[]{:S(2)}, u32[]{:S(2)}) collective-permute-start(f32[392,128]{1,0:T(8,128)S(1)} %get-tuple-element.23), channel_id=1, source_target_pairs={{0,384},{1,385},{2,386},{3,387},{4,388},{5,389},{6,390},{7,391},{8... | collective-permute-start | bytes 602120 | tf_op jit(solution)/shard_map/ppermute | solution.py:344
  36.5 14.2 %collective-permute-start.5 = (f32[336,128]{1,0:T(8,128)S(1)}, f32[336,128]{1,0:T(8,128)S(1)}, u32[]{:S(2)}, u32[]{:S(2)}) collective-permute-start(f32[336,128]{1,0:T(8,128)S(1)} %get-tuple-element.24), channel_id=1, source_target_pairs={{0,256},{128,384},{1,257},{129,385},{2,258},{130,386},{3,259},{131... | collective-permute-start | bytes 516104 | tf_op jit(solution)/shard_map/ppermute | solution.py:344
  41.1 12.6 %collective-permute-start.7 = (f32[320,128]{1,0:T(8,128)S(1)}, f32[320,128]{1,0:T(8,128)S(1)}, u32[]{:S(2)}, u32[]{:S(2)}) collective-permute-start(f32[320,128]{1,0:T(8,128)S(1)} %get-tuple-element.30), channel_id=1, source_target_pairs={{0,128},{128,256},{256,384},{1,129},{129,257},{257,385},{2,130},{1... | collective-permute-start | bytes 491528 | tf_op jit(solution)/shard_map/ppermute | solution.py:344
  43.1 7.6 %collective-permute-start.6 = (f32[280,128]{1,0:T(8,128)S(1)}, f32[280,128]{1,0:T(8,128)S(1)}, u32[]{:S(2)}, u32[]{:S(2)}) collective-permute-start(f32[280,128]{1,0:T(8,128)S(1)} %get-tuple-element.25), channel_id=1, source_target_pairs={{0,128},{128,256},{256,384},{1,129},{129,257},{257,385},{2,130},{1... | collective-permute-start | bytes 430088 | tf_op jit(solution)/shard_map/ppermute | solution.py:344
  50.7 3.1 %copy-start.1 = (f32[1,48,16,128]{3,2,1,0:T(8,128)S(1)}, f32[1,48,16,128]{3,2,1,0:T(8,128)}, u32[]{:S(2)}) copy-start(f32[1,48,16,128]{3,2,1,0:T(8,128)} %param.4) | copy-start | bytes 1179652

commit v4 on v1

v4 whole, which is shorter than its diff:
```python
import jax
import jax.numpy as jnp
from jax import lax
from jax.experimental import pallas as pl
from jax.experimental.pallas import tpu as pltpu
from jax.sharding import PartitionSpec as P

K = 48
R = 16
C = 128
H = 9
E = R + 2 * H
W = 2 * C
G = K // 8
SLOT = 2 * H
BASE = R - H
NC = 16
REACH = 3
RING = [*range(REACH), *range(R - REACH, R)]
SIDE = range(2, 6)
Q3, Q2, Q1, RG = 49 * 8, 42 * 8, 35 * 8, 40 * 8
LAT = H * K + 8 * H + 2 * R + 8
VMEM = pl.BlockSpec(memory_space=pltpu.VMEM)
SMEM = pl.BlockSpec(memory_space=pltpu.SMEM)
ANY = pl.BlockSpec(memory_space=pl.ANY)


def lanes(shape):
    return lax.broadcasted_iota(jnp.int32, shape, len(shape) - 1)


def shift(x, by):
    return pltpu.roll(x, by % x.shape[-1], x.ndim - 1)


def by_tile(fn, x):
    return jnp.concatenate([fn(x[:, :C]), fn(x[:, C:])], axis=1)


def pair_sum(x):
    return x + by_tile(lambda t: shift(t, -1), x)


def spread(x):
    return jnp.where(lanes(x.shape) % 2 == 0, x, shift(x, 1))


def pack_row(row):
    lane = lanes((8, C))
    out = shift(row[0:8], H)
    for g in range(1, G):
        out = jnp.where(lane < SLOT * g, out, shift(row[8 * g : 8 * g + 8], SLOT * g + H))
    return out


def unpack_row(packed):
    return jnp.concatenate([shift(packed, C - H - SLOT * g) for g in range(G)], axis=0)


def edge_kernel(x_ref, mk_ref, left_ref, right_ref, core_ref):
    rows = []
    for r in range(R):
        row = x_ref[pl.ds(r, K, stride=R), :] * mk_ref[r : r + 1]
        core_ref[pl.ds(r * K, K), :] = row
        rows.append(pack_row(row))
    coefs = pack_row(jnp.concatenate([mk_ref[...], jnp.zeros((R, C), jnp.float32)], axis=0))
    rows += [coefs, coefs]
    half = len(rows) // 2
    low = lanes((8, C)) % SLOT < H
    for p in range(half):
        a, b = rows[p], rows[p + half]
        left_ref[pl.ds(8 * p, 8), :] = jnp.where(low, a, shift(b, H))
        right_ref[pl.ds(8 * p, 8), :] = jnp.where(low, shift(a, -H), b)


def halo_kernel(core_in, mk_ref, rl_ref, rr_ref, core_ref, top_ref, bot_ref, side_ref):
    half = (R + 2) // 2
    low = lanes((8, C)) % SLOT < H
    for p in range(half):
        a, b = rl_ref[pl.ds(8 * p, 8), :], rr_ref[pl.ds(8 * p, 8), :]
        side_ref[pl.ds(8 * p, 8), :] = jnp.where(low, a, shift(b, H))
        side_ref[pl.ds(8 * (p + half), 8), :] = jnp.where(low, shift(a, -H), b)
    for ref, first in ((top_ref, 0), (bot_ref, R - H)):
        ref[pl.ds(0, H * K), :] = core_in[pl.ds(first * K, H * K), :]
        ref[pl.ds(H * K, 8 * H), :] = side_ref[pl.ds(8 * first, 8 * H), :]
        ref[pl.ds(H * K + 8 * H, 2 * R), :] = mk_ref[...]
        ref[pl.ds(H * K + 8 * H + 2 * R, 8), :] = side_ref[pl.ds(8 * R, 8), :]


def split(x):
    high = x.astype(jnp.bfloat16)
    return high, (x - high.astype(jnp.float32)).astype(jnp.bfloat16)


def level_matrix(mix):
    high, low = split(mix)
    return jnp.concatenate([high, high, low], axis=1)


def levels(matrix, u):
    high, low = split(u)
    return jnp.dot(
        matrix, jnp.concatenate([high, low, high], axis=0), preferred_element_type=jnp.float32
    )


def coefficients(m, k, scale, by, out_ref):
    moves = (
        lambda a: pltpu.roll(a, 1, 0),
        lambda a: pltpu.roll(a, a.shape[0] - 1, 0),
        lambda a: shift(a, by),
        lambda a: shift(a, -by),
    )
    total = None
    for i, move in enumerate(moves):
        c = (0.5 * scale) * (k + move(k)) * (m * move(m))
        out_ref[i + 1] = c
        total = c if total is None else total + c
    out_ref[0] = m * (1.0 - total)


def fine_coarse_coefficients(mk, first, count, cf_ref, cc_ref):
    wide = lambda i: jnp.concatenate([mk[i], mk[i + 1]], axis=1)
    coefficients(wide(0), wide(2), 1.0, 1, cf_ref)
    at, after = pl.ds(first, count, stride=2), pl.ds(first + 1, count, stride=2)

    def blocks(i):
        return pair_sum(jnp.concatenate([mk[j, at] + mk[j, after] for j in (i, i + 1)], axis=1))

    wet = blocks(0)
    coefficients(
        jnp.minimum(wet, 1.0), 0.25 * blocks(2), 0.75, 2, cc_ref.at[pl.ds(0, 5)]
    )
    cc_ref[5] = 1.0 / jnp.maximum(wet, 1.0)


def stencil(coef_ref, row, by, u, north, south, matrix):
    c = [coef_ref[i, pl.ds(row, 1), :] for i in range(5)]
    near = c[0] * u + c[1] * north + c[2] * south
    side = c[3] * shift(u, by) + c[4] * shift(u, -by)
    return (near + side) + levels(matrix, u)


def step_row(src, r, coef_ref, row, by, matrix):
    return stencil(coef_ref, row, by, src[r], src[r - 1], src[r + 1], matrix)


def restrict(src, i, cc_ref, row):
    return pair_sum(src[1 + 2 * i] + src[2 + 2 * i]) * cc_ref[5, pl.ds(row, 1), :]


def own_kernel(
    later_ref, core_ref, side_ref, mk_ref, mix_ref, u0, u1, u2, u3, rs, gs, qs, mk, cf, cc
):
    for r in range(R):
        u0[H + r, :, :C] = core_ref[pl.ds(r * K, K), :]
        u0[H + r, :, C:] = unpack_row(side_ref[pl.ds(8 * r, 8), :])
    coefs = unpack_row(side_ref[pl.ds(8 * R, 8), :])
    for i in range(2):
        mk[2 * i] = mk_ref[pl.ds(i * R, R), :]
        mk[2 * i + 1] = coefs[i * R : i * R + R]
    fine_coarse_coefficients(mk, 0, R // 2, cf, cc)
    mix = mix_ref[...]
    fine_mix = level_matrix(mix)
    coarse_mix = level_matrix(3.0 * mix)
    for margin, src, dst in ((1, u0, u1), (2, u1, u2), (3, u2, u3)):

        @pl.loop(margin, R - margin, unroll=R - 2 * margin)
        def _(r):
            dst[H + r] = step_row(src, H + r, cf, r, 1, fine_mix)

    for i in range(4, 12):
        rs[i] = restrict(u0, i, cc, i - 4)
    for i in range(5, 11):
        gs[i] = step_row(rs, i, cc, i - 4, 2, coarse_mix)
    for i in range(6, 10):
        qs[i] = restrict(u3, i, cc, i - 4) - later_ref[0] * gs[i]


def put_q(q_ref, out_ref, first, count):
    even = lanes((K, W)) % 2 == 0
    for p in range(count // 2):
        odd = by_tile(lambda t: shift(t, 1), q_ref[first + 2 * p + 1])
        both = jnp.where(even, q_ref[first + 2 * p], odd)
        out_ref[pl.ds(p * K, K), :] = both[:, :C]
        out_ref[pl.ds((count // 2) * K + 8 * p, 8), :] = pack_row(both[:, C:])


def take_q(in_ref, count, write):
    for p in range(count // 2):
        core = in_ref[pl.ds(p * K, K), :]
        side = unpack_row(in_ref[pl.ds((count // 2) * K + 8 * p, 8), :])
        both = jnp.concatenate([core, side], axis=1)
        write(2 * p, both)
        write(2 * p + 1, by_tile(lambda t: shift(t, -1), both))


def put_ring(src, out_ref):
    for i, r in enumerate(RING):
        out_ref[pl.ds(Q1 + i * K, K), :] = src[H + r, :, :C]
    at = lanes((8, C)) % SLOT
    for i, r in enumerate(SIDE):
        a, b, c = (pack_row(src[H + r + d, :, :C]) for d in (0, 4, 8))
        both = jnp.where(at < 2 * REACH, shift(a, -2 * REACH), b)
        both = jnp.where(at < 4 * REACH, both, shift(c, 2 * REACH))
        out_ref[pl.ds(Q1 + len(RING) * K + 8 * i, 8), :] = both


def take_ring(in_ref, inner_ref):
    rows = {r: in_ref[pl.ds(Q1 + i * K, K), :] for i, r in enumerate(RING)}
    lane = lanes((K, C))
    inside = (lane >= REACH) & (lane < C - REACH)
    for i, r in enumerate(SIDE):
        packed = in_ref[pl.ds(Q1 + len(RING) * K + 8 * i, 8), :]
        for d, by in ((0, 2 * REACH), (4, 0), (8, -2 * REACH)):
            if r + d not in rows:
                ends = unpack_row(shift(packed, by))
                rows[r + d] = jnp.where(inside, inner_ref[pl.ds((r + d) * K, K), :], ends)
    return [rows[r] for r in range(R)]


def outer_kernel(
    later_ref, mk_ref, side_ref, mix_ref, up_ref, down_ref,
    _u0, _u1, _u2, _u3, _rs, _gs, _qs,
    u0, u1, u2, u3, rs, gs, qs, q3_ref, q2_ref, q1_ref, cc, core_cf, mk, cf,
):
    for ref, first in ((up_ref, 0), (down_ref, H + R)):
        for i in range(H):
            u0[first + i, :, :C] = ref[pl.ds(i * K, K), :]
            u0[first + i, :, C:] = unpack_row(ref[pl.ds(H * K + 8 * i, 8), :])
    for j, (ref, at, side, side_at) in enumerate(
        (
            (up_ref, H * K + 8 * H, up_ref, H * K + 8 * H + 2 * R),
            (mk_ref, 0, side_ref, 8 * R),
            (down_ref, H * K + 8 * H, down_ref, H * K + 8 * H + 2 * R),
        )
    ):
        coefs = unpack_row(side[pl.ds(side_at, 8), :])
        for i in range(2):
            mk[2 * i, pl.ds(j * R, R), :] = ref[pl.ds(at + i * R, R), :]
            mk[2 * i + 1, pl.ds(j * R, R), :] = coefs[i * R : i * R + R]
    fine_coarse_coefficients(mk, R - 8, NC, cf, cc)
    mix = mix_ref[...]
    fine_mix = level_matrix(mix)
    coarse_mix = level_matrix(3.0 * mix)
    for margin, src, dst in ((1, u0, u1), (2, u1, u2), (3, u2, u3)):

        @pl.loop(0, H, unroll=H)
        def _(i):
            for r in (margin + i, E - 1 - margin - i):
                dst[r] = step_row(src, r, cf, r + BASE, 1, fine_mix)

    for i in (0, 1, 2, 3, 12, 13, 14, 15):
        rs[i] = restrict(u0, i, cc, i)
    for i in (1, 2, 3, 4, 11, 12, 13, 14):
        gs[i] = step_row(rs, i, cc, i, 2, coarse_mix)
    for i in (1, 2, 3, 4, 5, 10, 11, 12, 13, 14):
        qs[i] = restrict(u3, i, cc, i) - later_ref[0] * gs[i]
    put_q(qs, q3_ref, 1, 14)
    put_q(qs, q2_ref, 2, 12)
    put_q(qs, q1_ref, 3, 10)
    put_ring(u3, q1_ref)
    for i in range(5):
        core_cf[i] = cf[i, pl.ds(R, R), :C]


def before_kernel(core_ref, mix_ref, cf_ref, u3, cc_ref, mk_ref, inner_ref, rest_ref, ua, ub):
    mix = level_matrix(mix_ref[...])
    for r in range(R):
        ua[r] = core_ref[pl.ds(r * K, K), :]
    for margin, src, dst in ((1, ua, ub), (2, ub, ua), (3, ua, None)):
        for r in range(margin, R - margin):
            value = step_row(src, r, cf_ref, r, 1, mix)
            if dst is None:
                inner_ref[pl.ds(r * K, K), :] = value
            else:
                dst[r] = value
    for r in RING:
        inner_ref[pl.ds(r * K, K), :] = jnp.zeros((K, C), jnp.float32)
    for i in range(R // 2):
        pair = [u3[H + r, :, :C] for r in (2 * i, 2 * i + 1)]
        fc = spread(block_mean(pair, cc_ref, i))
        for r, value in zip((2 * i, 2 * i + 1), pair):
            rest_ref[pl.ds(r * K, K), :] = value - mk_ref[pl.ds(r, 1), :] * fc


def block_mean(pair, cc_ref, i):
    total = pair[0] + pair[1]
    return (total + shift(total, -1)) * cc_ref[5, 4 + i : 5 + i, :C]


def sweep_kernel(mix_ref, cc_ref, q3_ref, q2_ref, b, a):
    coarse_mix = level_matrix(3.0 * mix_ref[...])
    take_q(q3_ref, 14, lambda i, value: a.__setitem__(1 + i, value))
    take_q(q2_ref, 12, lambda i, value: b.__setitem__(2 + i, value))
    for i in range(2, 14):
        b[i] = b[i] + step_row(a, i, cc_ref, i, 2, coarse_mix)


def last_kernel(
    later_ref, mk_ref, mix_ref, cc_ref, x_ref, b, q1_ref, qs, rest_ref, inner_ref,
    out_hbm, next_hbm, a, out_ref, next_ref, sems,
):
    coarse_mix = level_matrix(3.0 * mix_ref[...])
    take_q(q1_ref, 10, lambda i, value: a.__setitem__(3 + i, value))
    for i in range(3, 13):
        a[i] = a[i] + step_row(b, i, cc_ref, i, 2, coarse_mix)
    first = later_ref[0] == 0.0

    @pl.when(first)
    def _():
        next_ref[...] = x_ref[...]

    @pl.when(jnp.logical_not(first))
    def _():
        rows = take_ring(q1_ref, inner_ref)
        for i in range(R // 2):
            pair = rows[2 * i], rows[2 * i + 1]
            jump = spread(a[4 + i, :, :C] - block_mean(pair, cc_ref, i))
            for r, value in zip((2 * i, 2 * i + 1), pair):
                next_ref[pl.ds(r, K, stride=R), :] = value + mk_ref[pl.ds(r, 1), :] * jump

    next_copy = pltpu.make_async_copy(next_ref, next_hbm, sems.at[0])
    next_copy.start()
    for i in range(R // 2):
        z = qs[4 + i] + step_row(a, 4 + i, cc_ref, 4 + i, 2, coarse_mix)
        z = spread(z[:, :C])
        for r in (2 * i, 2 * i + 1):
            value = rest_ref[pl.ds(r * K, K), :] + mk_ref[pl.ds(r, 1), :] * z
            out_ref[pl.ds(r, K, stride=R), :] = value
    out_copy = pltpu.make_async_copy(out_ref, out_hbm, sems.at[1])
    out_copy.start()
    next_copy.wait()
    out_copy.wait()


def f32(*shape):
    return jax.ShapeDtypeStruct(shape, jnp.float32)


def scratch(*shape):
    return pltpu.VMEM(shape, jnp.float32)


def call(kernel, n_in, outs, scratches=(), smem=0, aliases=None, out_spec=VMEM):
    return pl.pallas_call(
        kernel,
        out_shape=outs,
        in_specs=[SMEM] * smem + [VMEM] * (n_in - smem),
        out_specs=jax.tree.map(lambda _: out_spec, outs),
        scratch_shapes=list(scratches),
        input_output_aliases=aliases or {},
        compiler_params=pltpu.CompilerParams(vmem_limit_bytes=40 * 1024 * 1024),
    )


def moved(value, axis, by, wrap=False):
    n = lax.axis_size(axis)
    pairs = [(i, (i + by) % n) for i in range(n) if wrap or 0 <= i + by < n]
    return lax.ppermute(value, axis, pairs)


def body(start, wet, kappa, mixing):
    x = start.reshape(K * R, C)
    later = (lax.axis_index("tm") > 0).astype(jnp.float32).reshape(1)
    mk = jnp.concatenate([wet.astype(jnp.float32), kappa], axis=0)
    lon = (R + 2) * 4
    left, right, core = call(edge_kernel, 2, (f32(lon, C), f32(lon, C), f32(R * K, C)))(x, mk)
    from_left = moved(left, "lon", 1, True)
    from_right = moved(right, "lon", -1, True)
    core, top, bottom, side = call(
        halo_kernel,
        4,
        (f32(R * K, C), f32(LAT, C), f32(LAT, C), f32(8 * (R + 2), C)),
        aliases={0: 0},
    )(core, mk, from_left, from_right)
    down = moved(top, "lat", -1)
    up = moved(bottom, "lat", 1)
    before = moved(core, "tm", 1)
    fine, coarse = f32(E, K, W), f32(NC, K, W)
    states = call(
        own_kernel,
        5,
        (fine,) * 4 + (coarse,) * 3,
        [scratch(4, R, C), scratch(5, R, W), scratch(6, R // 2, W)],
        smem=1,
    )(later, core, side, mk, mixing)
    *states, q3, q2, q1, cc, cf = call(
        outer_kernel,
        13,
        (fine,) * 4 + (coarse,) * 3 + (f32(Q3, C), f32(Q2, C), f32(Q1 + RG, C))
        + (f32(6, NC, W), f32(5, R, C)),
        [scratch(4, 48, C), scratch(5, 48, W)],
        smem=1,
        aliases={6 + i: i for i in range(7)},
    )(later, mk, side, mixing, up, down, *states)
    u3, qs = states[3], states[6]
    q3, q2, q1 = moved(q3, "tm", 3), moved(q2, "tm", 2), moved(q1, "tm", 1)
    inner, rest = call(
        before_kernel, 6, (f32(R * K, C), f32(R * K, C)), [scratch(R, K, C), scratch(R, K, C)]
    )(before, mixing, cf, u3, cc, mk)
    state = call(sweep_kernel, 4, coarse, [scratch(NC, K, W)])(mixing, cc, q3, q2)
    out, following = call(
        last_kernel,
        10,
        (f32(K * R, C), f32(K * R, C)),
        [scratch(NC, K, W), scratch(K * R, C), scratch(K * R, C), pltpu.SemaphoreType.DMA((2,))],
        smem=1,
        out_spec=ANY,
    )(later, mk, mixing, cc, x, state, q1, qs, rest, inner)
    return out.reshape(1, K, R, C), following.reshape(1, K, R, C)


def solution(mesh):
    in_specs = (P("tm", None, "lat", "lon"), P("lat", "lon"), P("lat", "lon"), P())
    out_specs = (P("tm", None, "lat", "lon"), P("tm", None, "lat", "lon"))
    return jax.shard_map(body, mesh=mesh, in_specs=in_specs, out_specs=out_specs, check_vma=False)
```

time: 69.6 us -> 48.8 us (0.70)
  the two profiles are of different devices: /device:TPU:26 before, /device:TPU:28 now
where the time goes in v4:
time: 48.8 us; the launch traced here: 48.4 us
  starting transfers between devices  23.3 us (48%)
  Pallas kernels  11.1 us (23%)
  waiting for transfers between devices  10.1 us (21%)
  local copies, waits for them, and re-layouts  1.74 us (4%)
  other arithmetic  1.4 us (3%)
  between operations  0.78 us (2%)
    ppermute x8, starting transfers between devices, moved(): return lax.ppermute(value, axis, pairs)  23.3 us
    ppermute x8, waiting for transfers between devices, moved(): return lax.ppermute(value, axis, pairs)  10.1 us
    pallas_call x1, Pallas kernels, body(): call(outer_kernel, 13, (fine,) * 4 + (coarse,) * 3 + (f32(Q3, C), f32(Q2,...  4.34 us
    pallas_call x1, Pallas kernels, body(): call(last_kernel, 10, (f32(K * R, C), f32(K * R, C)), [scratch(NC, K, W),...  2.3 us
    pallas_call x1, Pallas kernels, body(): call(own_kernel, 5, (fine,) * 4 + (coarse,) * 3, [scratch(4, R, C), scrat...  1.87 us
    unnamed x8, local copies, waits for them, and re-layouts  1.74 us
    pallas_call x1, Pallas kernels, body(): call(sweep_kernel, 4, coarse, [scratch(NC, K, W)])(mixing, cc, q3, q2)  1.2 us
    pallas_call x1, Pallas kernels, body(): call(before_kernel, 6, (f32(R * K, C), f32(R * K, C)), [scratch(R, K, C),...  0.98 us
  transfers between devices with their start and end apart: 8, of which 3 were waited for; matrix products, arithmetic and copies ran while one was open for 0% of the time, Pallas kernels for 17%

profile of v4, /device:TPU:28, one launch (start us, length us, event | category | flops | bytes accessed | tf_op | source)
XLA Modules:
  0.0 48.4 jit_solution(11897790310229182279)
XLA Ops:
  0.6 0.7 %convert_element_type.4 = f32[16,128]{1,0:T(8,128)S(1)} convert(s32[16,128]{1,0:T(8,128)} %param.5) | non-fusion elementwise | flops 2048 | bytes 16384 | tf_op jit(solution)/shard_map/convert_element_type | solution.py:366
  1.3 0.7 %pad_maximum_fusion.mk_ref = f32[32,128]{1,0:T(8,128)S(1)} fusion(f32[16,128]{1,0:T(8,128)} %param.6, f32[16,128]{1,0:T(8,128)S(1)} %convert_element_type.4), kind=kLoop, calls=%fused_computation | loop fusion | flops 4096 | bytes 32768 | tf_op jit(solution)/shard_map/concatenate | solution.py:366
  2.0 1.0 %copy-done = f32[1,48,16,128]{3,2,1,0:T(8,128)S(1)} copy-done((f32[1,48,16,128]{3,2,1,0:T(8,128)S(1)}, f32[1,48,16,128]{3,2,1,0:T(8,128)}, u32[]{:S(2)}) %copy-start) | copy-done | bytes 393240
  3.0 0.3 shard_map.59
  3.3 0.0 collective-permute-start
  3.3 8.5 %collective-permute-start.1 = (f32[72,128]{1,0:T(8,128)S(1)}, f32[72,128]{1,0:T(8,128)S(1)}, u32[]{:S(2)}, u32[]{:S(2)}) collective-permute-start(f32[72,128]{1,0:T(8,128)S(1)} %get-tuple-element.29), channel_id=1, source_target_pairs={{0,15},{1,0},{2,1},{3,2},{4,3},{5,4},{6,5},{7,6},{8,7},{9,8},{10,9... | collective-permute-start | bytes 110600 | tf_op jit(solution)/shard_map/ppermute | solution.py:360
  11.8 1.6 %collective-permute-done.rl_ref = f32[72,128]{1,0:T(8,128)S(1)} collective-permute-done((f32[72,128]{1,0:T(8,128)S(1)}, f32[72,128]{1,0:T(8,128)S(1)}, u32[]{:S(2)}, u32[]{:S(2)}) %collective-permute-start) | collective-permute-done | bytes 36896 | tf_op jit(solution)/shard_map/ppermute | solution.py:360
  13.4 0.0 collective-permute-done.1.rr_ref
  13.5 0.1 shard_map.60
  13.6 4.7 %collective-permute-start.2 = (f32[544,128]{1,0:T(8,128)S(1)}, f32[544,128]{1,0:T(8,128)S(1)}, u32[]{:S(2)}, u32[]{:S(2)}) collective-permute-start(f32[544,128]{1,0:T(8,128)S(1)} %get-tuple-element.31), channel_id=1, source_target_pairs={{0,16},{16,32},{32,48},{48,64},{64,80},{80,96},{96,112},{1,17},{17... | collective-permute-start | bytes 835592 | tf_op jit(solution)/shard_map/ppermute | solution.py:360
  18.3 1.9 %collective-permute-start.3 = (f32[544,128]{1,0:T(8,128)S(1)}, f32[544,128]{1,0:T(8,128)S(1)}, u32[]{:S(2)}, u32[]{:S(2)}) collective-permute-start(f32[544,128]{1,0:T(8,128)S(1)} %get-tuple-element.32), channel_id=1, source_target_pairs={{16,0},{32,16},{48,32},{64,48},{80,64},{96,80},{112,96},{17,1},{33... | collective-permute-start | bytes 835592 | tf_op jit(solution)/shard_map/ppermute | solution.py:360
  20.2 3.1 %collective-permute-start.7 = (f32[768,128]{1,0:T(8,128)S(1)}, f32[768,128]{1,0:T(8,128)S(1)}, u32[]{:S(2)}, u32[]{:S(2)}) collective-permute-start(f32[768,128]{1,0:T(8,128)S(1)} %get-tuple-element.33.core_ref), channel_id=1, source_target_pairs={{0,128},{128,256},{256,384},{1,129},{129,257},{257,385},{2,130},{1... | collective-permute-start | bytes 1179656 | tf_op jit(solution)/shard_map/ppermute | solution.py:360
  23.3 0.0 copy-start.2
  23.3 0.7 %copy-done.2 = f32[48,48]{1,0:T(8,128)S(1)} copy-done((f32[48,48]{1,0:T(8,128)S(1)}, f32[48,48]{1,0:T(8,128)}, u32[]{:S(2)}) %copy-start.2) | copy-done | bytes 9240
  24.0 1.9 %shard_map.61 = (f32[34,48,256]{2,1,0:T(8,128)S(1)}, f32[34,48,256]{2,1,0:T(8,128)S(1)}, f32[34,48,256]{2,1,0:T(8,128)S(1)}, f32[34,48,256]{2,1,0:T(8,128)S(1)},...) custom-call(f32[1]{0:T(128)} %bitcast.later_ref, ...), custom_call_target="tpu_custom_call" | custom-call | tf_op jit(solution)/shard_map/pallas_call | solution.py:381
  25.9 2.0 %collective-permute-done.3.down_ref = f32[544,128]{1,0:T(8,128)S(1)} collective-permute-done((f32[544,128]{1,0:T(8,128)S(1)}, f32[544,128]{1,0:T(8,128)S(1)}, u32[]{:S(2)}, u32[]{:S(2)}) %collective-permute-start.3) | collective-permute-done | bytes 278560 | tf_op jit(solution)/shard_map/ppermute | solution.py:360
  27.9 4.3 %shard_map.62 = (f32[34,48,256]{2,1,0:T(8,128)S(1)}, f32[34,48,256]{2,1,0:T(8,128)S(1)}, f32[34,48,256]{2,1,0:T(8,128)S(1)}, f32[34,48,256]{2,1,0:T(8,128)S(1)},...) custom-call(f32[1]{0:T(128)} %bitcast.later_ref, ...), custom_call_target="tpu_custom_call", output_to_operand_aliasing={{0}: (6, {}), {1}: (7, {}), {2}: (8, {}), {3}: (9, {}), {4}... | custom-call | tf_op jit(solution)/shard_map/pallas_call | solution.py:388
  32.2 3.1 %collective-permute-start.6 = (f32[600,128]{1,0:T(8,128)S(1)}, f32[600,128]{1,0:T(8,128)S(1)}, u32[]{:S(2)}, u32[]{:S(2)}) collective-permute-start(f32[600,128]{1,0:T(8,128)S(1)} %get-tuple-element.44), channel_id=1, source_target_pairs={{0,128},{128,256},{256,384},{1,129},{129,257},{257,385},{2,130},{1... | collective-permute-start | bytes 921608 | tf_op jit(solution)/shard_map/ppermute | solution.py:360
  35.4 0.7 %collective-permute-start.4 = (f32[392,128]{1,0:T(8,128)S(1)}, f32[392,128]{1,0:T(8,128)S(1)}, u32[]{:S(2)}, u32[]{:S(2)}) collective-permute-start(f32[392,128]{1,0:T(8,128)S(1)} %get-tuple-element.42), channel_id=1, source_target_pairs={{0,384},{1,385},{2,386},{3,387},{4,388},{5,389},{6,390},{7,391},{8... | collective-permute-start | bytes 602120 | tf_op jit(solution)/shard_map/ppermute | solution.py:360
  36.0 1.3 %collective-permute-start.5 = (f32[336,128]{1,0:T(8,128)S(1)}, f32[336,128]{1,0:T(8,128)S(1)}, u32[]{:S(2)}, u32[]{:S(2)}) collective-permute-start(f32[336,128]{1,0:T(8,128)S(1)} %get-tuple-element.43), channel_id=1, source_target_pairs={{0,256},{128,384},{1,257},{129,385},{2,258},{130,386},{3,259},{131... | collective-permute-start | bytes 516104 | tf_op jit(solution)/shard_map/ppermute | solution.py:360
  37.4 1.0 %shard_map.64 = (f32[768,128]{1,0:T(8,128)S(1)}, f32[768,128]{1,0:T(8,128)S(1)}) custom-call(f32[768,128]{1,0:T(8,128)S(1)} %collective-permute-done.7.core_ref, f32[48,48]{1,0:T(8,128)S(1)} %copy-done.3, f32[5,16,128]{2,1,0:T(8,128)S(1)} %get-tuple-element.46.cf_ref, f32[34,48,256]{2,1,0:T(8,128)S(1)} %get-tuple-element.47.u3, ...), custom_call_target="tpu_custom_call" | custom-call | tf_op jit(solution)/shard_map/pallas_call | solution.py:399
  38.4 6.5 %collective-permute-done.5.q2_ref = f32[336,128]{1,0:T(8,128)S(1)} collective-permute-done((f32[336,128]{1,0:T(8,128)S(1)}, f32[336,128]{1,0:T(8,128)S(1)}, u32[]{:S(2)}, u32[]{:S(2)}) %collective-permute-start.5) | collective-permute-done | bytes 172064 | tf_op jit(solution)/shard_map/ppermute | solution.py:360
  44.9 1.2 %shard_map.63.b = f32[16,48,256]{2,1,0:T(8,128)S(1)} custom-call(f32[48,48]{1,0:T(8,128)S(1)} %copy-done.3, f32[6,16,256]{2,1,0:T(8,128)S(1)} %get-tuple-element.41.cc_ref, f32[392,128]{1,0:T(8,128)S(1)} %collective-permute-done.4.q3_ref, f32[336,128]{1,0:T(8,128)S(1)} %collective-permute-done.5.q2_ref), custom_call_target="tpu_custom_call" | custom-call | tf_op jit(solution)/shard_map/pallas_call | solution.py:402
  46.1 2.3 %shard_map.65 = (f32[768,128]{1,0:T(8,128)}, f32[768,128]{1,0:T(8,128)}) custom-call(f32[1]{0:T(128)} %bitcast.later_ref, f32[32,128]{1,0:T(8,128)S(1)} %pad_maximum_fusion.mk_ref, f32[48,48]{1,0:T(8,128)S(1)} %copy-done.3, f32[6,16,256]{2,1,0:T(8,128)S(1)} %get-tuple-element.41.cc_ref, f32[768,128]{1,0:T(8,128)S(1)} %bitcast.5, ...), custom_call_target="tpu_custom_call" | custom-call | tf_op jit(solution)/shard_map/pallas_call | solution.py:403
  (9 shorter events, 0.0 us)
Async XLA Ops:
  2.0 1.0 %copy-start = (f32[1,48,16,128]{3,2,1,0:T(8,128)S(1)}, f32[1,48,16,128]{3,2,1,0:T(8,128)}, u32[]{:S(2)}) copy-start(f32[1,48,16,128]{3,2,1,0:T(8,128)} %param.4) | copy-start | bytes 1179652
  3.3 10.1 %collective-permute-start = (f32[72,128]{1,0:T(8,128)S(1)}, f32[72,128]{1,0:T(8,128)S(1)}, u32[]{:S(2)}, u32[]{:S(2)}) collective-permute-start(f32[72,128]{1,0:T(8,128)S(1)} %get-tuple-element.28), channel_id=1, source_target_pairs={{0,1},{1,2},{2,3},{3,4},{4,5},{5,6},{6,7},{7,8},{8,9},{9,10},{10,1... | collective-permute-start | bytes 110600 | tf_op jit(solution)/shard_map/ppermute | solution.py:360
  3.3 10.1 %collective-permute-start.1 = (f32[72,128]{1,0:T(8,128)S(1)}, f32[72,128]{1,0:T(8,128)S(1)}, u32[]{:S(2)}, u32[]{:S(2)}) collective-permute-start(f32[72,128]{1,0:T(8,128)S(1)} %get-tuple-element.29), channel_id=1, source_target_pairs={{0,15},{1,0},{2,1},{3,2},{4,3},{5,4},{6,5},{7,6},{8,7},{9,8},{10,9... | collective-permute-start | bytes 110600 | tf_op jit(solution)/shard_map/ppermute | solution.py:360
  13.6 12.4 %collective-permute-start.2 = (f32[544,128]{1,0:T(8,128)S(1)}, f32[544,128]{1,0:T(8,128)S(1)}, u32[]{:S(2)}, u32[]{:S(2)}) collective-permute-start(f32[544,128]{1,0:T(8,128)S(1)} %get-tuple-element.31), channel_id=1, source_target_pairs={{0,16},{16,32},{32,48},{48,64},{64,80},{80,96},{96,112},{1,17},{17... | collective-permute-start | bytes 835592 | tf_op jit(solution)/shard_map/ppermute | solution.py:360
  18.3 9.7 %collective-permute-start.3 = (f32[544,128]{1,0:T(8,128)S(1)}, f32[544,128]{1,0:T(8,128)S(1)}, u32[]{:S(2)}, u32[]{:S(2)}) collective-permute-start(f32[544,128]{1,0:T(8,128)S(1)} %get-tuple-element.32), channel_id=1, source_target_pairs={{16,0},{32,16},{48,32},{64,48},{80,64},{96,80},{112,96},{17,1},{33... | collective-permute-start | bytes 835592 | tf_op jit(solution)/shard_map/ppermute | solution.py:360
  20.2 17.2 %collective-permute-start.7 = (f32[768,128]{1,0:T(8,128)S(1)}, f32[768,128]{1,0:T(8,128)S(1)}, u32[]{:S(2)}, u32[]{:S(2)}) collective-permute-start(f32[768,128]{1,0:T(8,128)S(1)} %get-tuple-element.33.core_ref), channel_id=1, source_target_pairs={{0,128},{128,256},{256,384},{1,129},{129,257},{257,385},{2,130},{1... | collective-permute-start | bytes 1179656 | tf_op jit(solution)/shard_map/ppermute | solution.py:360
  23.3 0.7 %copy-start.2 = (f32[48,48]{1,0:T(8,128)S(1)}, f32[48,48]{1,0:T(8,128)}, u32[]{:S(2)}) copy-start(f32[48,48]{1,0:T(8,128)} %mix_ref.9) | copy-start | bytes 27652
  27.9 9.4 %copy-start.3 = (f32[48,48]{1,0:T(8,128)S(1)}, f32[48,48]{1,0:T(8,128)}, u32[]{:S(2)}) copy-start(f32[48,48]{1,0:T(8,128)} %mix_ref.9) | copy-start | bytes 27652
  32.2 13.8 %collective-permute-start.6 = (f32[600,128]{1,0:T(8,128)S(1)}, f32[600,128]{1,0:T(8,128)S(1)}, u32[]{:S(2)}, u32[]{:S(2)}) collective-permute-start(f32[600,128]{1,0:T(8,128)S(1)} %get-tuple-element.44), channel_id=1, source_target_pairs={{0,128},{128,256},{256,384},{1,129},{129,257},{257,385},{2,130},{1... | collective-permute-start | bytes 921608 | tf_op jit(solution)/shard_map/ppermute | solution.py:360
  35.4 9.5 %collective-permute-start.4 = (f32[392,128]{1,0:T(8,128)S(1)}, f32[392,128]{1,0:T(8,128)S(1)}, u32[]{:S(2)}, u32[]{:S(2)}) collective-permute-start(f32[392,128]{1,0:T(8,128)S(1)} %get-tuple-element.42), channel_id=1, source_target_pairs={{0,384},{1,385},{2,386},{3,387},{4,388},{5,389},{6,390},{7,391},{8... | collective-permute-start | bytes 602120 | tf_op jit(solution)/shard_map/ppermute | solution.py:360
  36.0 8.8 %collective-permute-start.5 = (f32[336,128]{1,0:T(8,128)S(1)}, f32[336,128]{1,0:T(8,128)S(1)}, u32[]{:S(2)}, u32[]{:S(2)}) collective-permute-start(f32[336,128]{1,0:T(8,128)S(1)} %get-tuple-element.43), channel_id=1, source_target_pairs={{0,256},{128,384},{1,257},{129,385},{2,258},{130,386},{3,259},{131... | collective-permute-start | bytes 516104 | tf_op jit(solution)/shard_map/ppermute | solution.py:360
  37.4 8.7 %copy-start.1 = (f32[1,48,16,128]{3,2,1,0:T(8,128)S(1)}, f32[1,48,16,128]{3,2,1,0:T(8,128)}, u32[]{:S(2)}) copy-start(f32[1,48,16,128]{3,2,1,0:T(8,128)} %param.4) | copy-start | bytes 1179652

commit v5 on v4

--- a/solution.py
+++ b/solution.py
@@ -57,10 +57,14 @@
     return jnp.concatenate([shift(packed, C - H - SLOT * g) for g in range(G)], axis=0)
 
 
-def edge_kernel(x_ref, mk_ref, left_ref, right_ref, core_ref):
+def edge_kernel(x_ref, signed_ref, left_ref, right_ref, core_ref, mk_ref):
+    signed = signed_ref[...]
+    mask = jnp.where(signed > 0.0, 1.0, 0.0)
+    mk_ref[pl.ds(0, R), :] = mask
+    mk_ref[pl.ds(R, R), :] = jnp.abs(signed)
     rows = []
     for r in range(R):
-        row = x_ref[pl.ds(r, K, stride=R), :] * mk_ref[r : r + 1]
+        row = x_ref[pl.ds(r, K, stride=R), :] * mask[r : r + 1]
         core_ref[pl.ds(r * K, K), :] = row
         rows.append(pack_row(row))
     coefs = pack_row(jnp.concatenate([mk_ref[...], jnp.zeros((R, C), jnp.float32)], axis=0))
@@ -73,7 +77,12 @@
         right_ref[pl.ds(8 * p, 8), :] = jnp.where(low, shift(a, -H), b)
 
 
-def halo_kernel(core_in, mk_ref, rl_ref, rr_ref, core_ref, top_ref, bot_ref, side_ref):
+def halo_kernel(
+    core_in, mk_ref, rl_ref, rr_ref, mix_ref,
+    core_ref, top_ref, bot_ref, side_ref, fine_ref, coarse_ref,
+):
+    fine_ref[...] = level_matrix(mix_ref[0])
+    coarse_ref[...] = level_matrix(mix_ref[1])
     half = (R + 2) // 2
     low = lanes((8, C)) % SLOT < H
     for p in range(half):
@@ -150,7 +159,7 @@
 
 
 def own_kernel(
-    later_ref, core_ref, side_ref, mk_ref, mix_ref, u0, u1, u2, u3, rs, gs, qs, mk, cf, cc
+    later_ref, core_ref, side_ref, mk_ref, fine_mix, coarse_mix, u0, u1, u2, u3, rs, gs, qs, core_cf, mk, cf, cc
 ):
     for r in range(R):
         u0[H + r, :, :C] = core_ref[pl.ds(r * K, K), :]
@@ -160,21 +169,20 @@
         mk[2 * i] = mk_ref[pl.ds(i * R, R), :]
         mk[2 * i + 1] = coefs[i * R : i * R + R]
     fine_coarse_coefficients(mk, 0, R // 2, cf, cc)
-    mix = mix_ref[...]
-    fine_mix = level_matrix(mix)
-    coarse_mix = level_matrix(3.0 * mix)
     for margin, src, dst in ((1, u0, u1), (2, u1, u2), (3, u2, u3)):
 
         @pl.loop(margin, R - margin, unroll=R - 2 * margin)
         def _(r):
-            dst[H + r] = step_row(src, H + r, cf, r, 1, fine_mix)
+            dst[H + r] = step_row(src, H + r, cf, r, 1, fine_mix[...])
 
     for i in range(4, 12):
         rs[i] = restrict(u0, i, cc, i - 4)
     for i in range(5, 11):
-        gs[i] = step_row(rs, i, cc, i - 4, 2, coarse_mix)
+        gs[i] = step_row(rs, i, cc, i - 4, 2, coarse_mix[...])
     for i in range(6, 10):
         qs[i] = restrict(u3, i, cc, i - 4) - later_ref[0] * gs[i]
+    for i in range(5):
+        core_cf[i] = cf[i, :, :C]
 
 
 def put_q(q_ref, out_ref, first, count):
@@ -219,58 +227,66 @@
     return [rows[r] for r in range(R)]
 
 
-def outer_kernel(
-    later_ref, mk_ref, side_ref, mix_ref, up_ref, down_ref,
-    _u0, _u1, _u2, _u3, _rs, _gs, _qs,
-    u0, u1, u2, u3, rs, gs, qs, q3_ref, q2_ref, q1_ref, cc, core_cf, mk, cf,
+def outer_rows(
+    upper, later_ref, mk_ref, side_ref, fine_mix, coarse_mix, halo_ref, states, cc_out, mk, cf, cc
 ):
-    for ref, first in ((up_ref, 0), (down_ref, H + R)):
-        for i in range(H):
-            u0[first + i, :, :C] = ref[pl.ds(i * K, K), :]
-            u0[first + i, :, C:] = unpack_row(ref[pl.ds(H * K + 8 * i, 8), :])
-    for j, (ref, at, side, side_at) in enumerate(
-        (
-            (up_ref, H * K + 8 * H, up_ref, H * K + 8 * H + 2 * R),
-            (mk_ref, 0, side_ref, 8 * R),
-            (down_ref, H * K + 8 * H, down_ref, H * K + 8 * H + 2 * R),
-        )
+    u0, u1, u2, u3, rs, gs, qs = states
+    mk[...] = jnp.zeros_like(mk)
+    first = 0 if upper else H + R
+    for i in range(H):
+        u0[first + i, :, :C] = halo_ref[pl.ds(i * K, K), :]
+        u0[first + i, :, C:] = unpack_row(halo_ref[pl.ds(H * K + 8 * i, 8), :])
+    at = H * K + 8 * H
+    for j, ref, at, side, side_at in (
+        (0 if upper else 2, halo_ref, at, halo_ref, at + 2 * R),
+        (1, mk_ref, 0, side_ref, 8 * R),
     ):
         coefs = unpack_row(side[pl.ds(side_at, 8), :])
         for i in range(2):
             mk[2 * i, pl.ds(j * R, R), :] = ref[pl.ds(at + i * R, R), :]
             mk[2 * i + 1, pl.ds(j * R, R), :] = coefs[i * R : i * R + R]
     fine_coarse_coefficients(mk, R - 8, NC, cf, cc)
-    mix = mix_ref[...]
-    fine_mix = level_matrix(mix)
-    coarse_mix = level_matrix(3.0 * mix)
     for margin, src, dst in ((1, u0, u1), (2, u1, u2), (3, u2, u3)):
 
         @pl.loop(0, H, unroll=H)
         def _(i):
-            for r in (margin + i, E - 1 - margin - i):
-                dst[r] = step_row(src, r, cf, r + BASE, 1, fine_mix)
-
-    for i in (0, 1, 2, 3, 12, 13, 14, 15):
+            r = margin + i if upper else E - 1 - margin - i
+            dst[r] = step_row(src, r, cf, r + BASE, 1, fine_mix[...])
+
+    mirror = lambda rows: rows if upper else [NC - 1 - i for i in rows]
+    for i in mirror([0, 1, 2, 3]):
         rs[i] = restrict(u0, i, cc, i)
-    for i in (1, 2, 3, 4, 11, 12, 13, 14):
-        gs[i] = step_row(rs, i, cc, i, 2, coarse_mix)
-    for i in (1, 2, 3, 4, 5, 10, 11, 12, 13, 14):
+    for i in mirror([1, 2, 3, 4]):
+        gs[i] = step_row(rs, i, cc, i, 2, coarse_mix[...])
+    for i in mirror([1, 2, 3, 4, 5]):
         qs[i] = restrict(u3, i, cc, i) - later_ref[0] * gs[i]
+    half = pl.ds(0 if upper else NC // 2, NC // 2)
+    for i in range(6):
+        cc_out[i, half, :] = cc[i, half, :]
+
+
+def upper_kernel(*refs):
+    *ins, mk, cf, cc = refs
+    outer_rows(True, *ins[:6], ins[13:20], ins[20], mk, cf, cc)
+
+
+def lower_kernel(*refs):
+    *ins, q3_ref, q2_ref, q1_ref, mk, cf, cc = refs
+    states = ins[14:21]
+    outer_rows(False, *ins[:6], states, ins[21], mk, cf, cc)
+    u3, qs = states[3], states[6]
     put_q(qs, q3_ref, 1, 14)
     put_q(qs, q2_ref, 2, 12)
     put_q(qs, q1_ref, 3, 10)
     put_ring(u3, q1_ref)
-    for i in range(5):
-        core_cf[i] = cf[i, pl.ds(R, R), :C]
-
-
-def before_kernel(core_ref, mix_ref, cf_ref, u3, cc_ref, mk_ref, inner_ref, rest_ref, ua, ub):
-    mix = level_matrix(mix_ref[...])
+
+
+def before_kernel(core_ref, fine_mix, cf_ref, u3, cc_ref, mk_ref, inner_ref, rest_ref, ua, ub):
     for r in range(R):
         ua[r] = core_ref[pl.ds(r * K, K), :]
     for margin, src, dst in ((1, ua, ub), (2, ub, ua), (3, ua, None)):
         for r in range(margin, R - margin):
-            value = step_row(src, r, cf_ref, r, 1, mix)
+            value = step_row(src, r, cf_ref, r, 1, fine_mix[...])
             if dst is None:
                 inner_ref[pl.ds(r * K, K), :] = value
             else:
@@ -289,23 +305,36 @@
     return (total + shift(total, -1)) * cc_ref[5, 4 + i : 5 + i, :C]
 
 
-def sweep_kernel(mix_ref, cc_ref, q3_ref, q2_ref, b, a):
-    coarse_mix = level_matrix(3.0 * mix_ref[...])
+def near_kernel(q1_ref, inner_ref, cc_ref, mk_ref, a, base_ref):
+    take_q(q1_ref, 10, lambda i, value: a.__setitem__(3 + i, value))
+    rows = take_ring(q1_ref, inner_ref)
+    for i in range(R // 2):
+        pair = rows[2 * i], rows[2 * i + 1]
+        fc = spread(block_mean(pair, cc_ref, i))
+        for r, value in zip((2 * i, 2 * i + 1), pair):
+            base_ref[pl.ds(r * K, K), :] = value - mk_ref[pl.ds(r, 1), :] * fc
+
+
+def far_kernel(coarse_mix, cc_ref, q3_ref, b, a):
     take_q(q3_ref, 14, lambda i, value: a.__setitem__(1 + i, value))
-    take_q(q2_ref, 12, lambda i, value: b.__setitem__(2 + i, value))
     for i in range(2, 14):
-        b[i] = b[i] + step_row(a, i, cc_ref, i, 2, coarse_mix)
+        b[i] = step_row(a, i, cc_ref, i, 2, coarse_mix[...])
 
 
 def last_kernel(
-    later_ref, mk_ref, mix_ref, cc_ref, x_ref, b, q1_ref, qs, rest_ref, inner_ref,
-    out_hbm, next_hbm, a, out_ref, next_ref, sems,
+    later_ref, mk_ref, coarse_mix, cc_ref, x_ref, far, near, q2_ref, qs, rest_ref, base_ref,
+    out_hbm, next_hbm, a, b, out_ref, next_ref, sems,
 ):
-    coarse_mix = level_matrix(3.0 * mix_ref[...])
-    take_q(q1_ref, 10, lambda i, value: a.__setitem__(3 + i, value))
+    take_q(q2_ref, 12, lambda i, value: b.__setitem__(2 + i, far[2 + i] + value))
     for i in range(3, 13):
-        a[i] = a[i] + step_row(b, i, cc_ref, i, 2, coarse_mix)
+        a[i] = near[i] + step_row(b, i, cc_ref, i, 2, coarse_mix[...])
     first = later_ref[0] == 0.0
+
+    def put(ref, from_ref, i, value):
+        value = spread(value)
+        for r in (2 * i, 2 * i + 1):
+            total = from_ref[pl.ds(r * K, K), :] + mk_ref[pl.ds(r, 1), :] * value
+            ref[pl.ds(r, K, stride=R), :] = total
 
     @pl.when(first)
     def _():
@@ -313,21 +342,14 @@
 
     @pl.when(jnp.logical_not(first))
     def _():
-        rows = take_ring(q1_ref, inner_ref)
         for i in range(R // 2):
-            pair = rows[2 * i], rows[2 * i + 1]
-            jump = spread(a[4 + i, :, :C] - block_mean(pair, cc_ref, i))
-            for r, value in zip((2 * i, 2 * i + 1), pair):
-                next_ref[pl.ds(r, K, stride=R), :] = value + mk_ref[pl.ds(r, 1), :] * jump
+            put(next_ref, base_ref, i, a[4 + i, :, :C])
 
     next_copy = pltpu.make_async_copy(next_ref, next_hbm, sems.at[0])
     next_copy.start()
     for i in range(R // 2):
-        z = qs[4 + i] + step_row(a, 4 + i, cc_ref, 4 + i, 2, coarse_mix)
-        z = spread(z[:, :C])
-        for r in (2 * i, 2 * i + 1):
-            value = rest_ref[pl.ds(r * K, K), :] + mk_ref[pl.ds(r, 1), :] * z
-            out_ref[pl.ds(r, K, stride=R), :] = value
+        z = qs[4 + i] + step_row(a, 4 + i, cc_ref, 4 + i, 2, coarse_mix[...])
+        put(out_ref, rest_ref, i, z[:, :C])
     out_copy = pltpu.make_async_copy(out_ref, out_hbm, sems.at[1])
     out_copy.start()
     next_copy.wait()
@@ -363,51 +385,60 @@
 def body(start, wet, kappa, mixing):
     x = start.reshape(K * R, C)
     later = (lax.axis_index("tm") > 0).astype(jnp.float32).reshape(1)
-    mk = jnp.concatenate([wet.astype(jnp.float32), kappa], axis=0)
+    mixing = mixing[None] * jnp.array([1.0, 3.0], jnp.float32)[:, None, None]
     lon = (R + 2) * 4
-    left, right, core = call(edge_kernel, 2, (f32(lon, C), f32(lon, C), f32(R * K, C)))(x, mk)
+    left, right, core, mk = call(
+        edge_kernel, 2, (f32(lon, C), f32(lon, C), f32(R * K, C), f32(2 * R, C))
+    )(x, jnp.where(wet > 0, kappa, -kappa))
     from_left = moved(left, "lon", 1, True)
     from_right = moved(right, "lon", -1, True)
-    core, top, bottom, side = call(
+    matrix = jax.ShapeDtypeStruct((K, 3 * K), jnp.bfloat16)
+    core, top, bottom, side, fine_mix, coarse_mix = call(
         halo_kernel,
-        4,
-        (f32(R * K, C), f32(LAT, C), f32(LAT, C), f32(8 * (R + 2), C)),
+        5,
+        (f32(R * K, C), f32(LAT, C), f32(LAT, C), f32(8 * (R + 2), C), matrix, matrix),
         aliases={0: 0},
-    )(core, mk, from_left, from_right)
+    )(core, mk, from_left, from_right, mixing)
     down = moved(top, "lat", -1)
     up = moved(bottom, "lat", 1)
     before = moved(core, "tm", 1)
     fine, coarse = f32(E, K, W), f32(NC, K, W)
-    states = call(
+    shapes = (fine,) * 4 + (coarse,) * 3
+    *states, cf = call(
         own_kernel,
-        5,
-        (fine,) * 4 + (coarse,) * 3,
+        6,
+        shapes + (f32(5, R, C),),
         [scratch(4, R, C), scratch(5, R, W), scratch(6, R // 2, W)],
         smem=1,
-    )(later, core, side, mk, mixing)
-    *states, q3, q2, q1, cc, cf = call(
-        outer_kernel,
-        13,
-        (fine,) * 4 + (coarse,) * 3 + (f32(Q3, C), f32(Q2, C), f32(Q1 + RG, C))
-        + (f32(6, NC, W), f32(5, R, C)),
-        [scratch(4, 48, C), scratch(5, 48, W)],
+    )(later, core, side, mk, fine_mix, coarse_mix)
+    parts = [scratch(4, 48, C), scratch(5, 48, W), scratch(6, NC, W)]
+    coefs = f32(6, NC, W)
+    states = call(
+        upper_kernel, 13, shapes + (coefs,), parts, smem=1, aliases={6 + i: i for i in range(7)}
+    )(later, mk, side, fine_mix, coarse_mix, up, *states)
+    *states, cc, q3, q2, q1 = call(
+        lower_kernel,
+        14,
+        shapes + (coefs, f32(Q3, C), f32(Q2, C), f32(Q1 + RG, C)),
+        parts,
         smem=1,
-        aliases={6 + i: i for i in range(7)},
-    )(later, mk, side, mixing, up, down, *states)
+        aliases={6 + i: i for i in range(8)},
+    )(later, mk, side, fine_mix, coarse_mix, down, *states)
     u3, qs = states[3], states[6]
     q3, q2, q1 = moved(q3, "tm", 3), moved(q2, "tm", 2), moved(q1, "tm", 1)
     inner, rest = call(
         before_kernel, 6, (f32(R * K, C), f32(R * K, C)), [scratch(R, K, C), scratch(R, K, C)]
-    )(before, mixing, cf, u3, cc, mk)
-    state = call(sweep_kernel, 4, coarse, [scratch(NC, K, W)])(mixing, cc, q3, q2)
+    )(before, fine_mix, cf, u3, cc, mk)
+    near, base = call(near_kernel, 4, (coarse, f32(R * K, C)))(q1, inner, cc, mk)
+    far = call(far_kernel, 3, coarse, [scratch(NC, K, W)])(coarse_mix, cc, q3)
     out, following = call(
         last_kernel,
-        10,
+        11,
         (f32(K * R, C), f32(K * R, C)),
-        [scratch(NC, K, W), scratch(K * R, C), scratch(K * R, C), pltpu.SemaphoreType.DMA((2,))],
+        [scratch(NC, K, W)] * 2 + [scratch(K * R, C)] * 2 + [pltpu.SemaphoreType.DMA((2,))],
         smem=1,
         out_spec=ANY,
-    )(later, mk, mixing, cc, x, state, q1, qs, rest, inner)
+    )(later, mk, coarse_mix, cc, x, far, near, q2, qs, rest, base)
     return out.reshape(1, K, R, C), following.reshape(1, K, R, C)
 
 

time: 48.8 us -> 46.2 us (0.947)
  the two profiles are of different devices: /device:TPU:28 before, /device:TPU:30 now
where the time goes in v5:
time: 46.2 us; the launch traced here: 45.9 us
  starting transfers between devices  20.3 us (44%)
  Pallas kernels  11.2 us (24%)
  waiting for transfers between devices  11.1 us (24%)
  other arithmetic  1.54 us (3%)
  local copies, waits for them, and re-layouts  1 us (2%)
  between operations  0.78 us (2%)
    ppermute x8, starting transfers between devices, moved(): return lax.ppermute(value, axis, pairs)  20.3 us
    ppermute x8, waiting for transfers between devices, moved(): return lax.ppermute(value, axis, pairs)  11.1 us
    pallas_call x1, Pallas kernels, body(): call(lower_kernel, 14, shapes + (coefs, f32(Q3, C), f32(Q2, C), f32(Q1 +...  3.08 us
    pallas_call x1, Pallas kernels, body(): call(last_kernel, 11, (f32(K * R, C), f32(K * R, C)), [scratch(NC, K, W)]...  2.05 us
    pallas_call x1, Pallas kernels, body(): call(own_kernel, 6, shapes + (f32(5, R, C),), [scratch(4, R, C), scratch(...  1.83 us
    pallas_call x1, Pallas kernels, body(): call(upper_kernel, 13, shapes + (coefs,), parts, smem=1, aliases={6 + i:...  1.5 us
    unnamed x4, local copies, waits for them, and re-layouts  1 us
  transfers between devices with their start and end apart: 8, of which 3 were waited for; matrix products, arithmetic and copies ran while one was open for 2% of the time, Pallas kernels for 19%

profile of v5, /device:TPU:30, one launch (start us, length us, event | category | flops | bytes accessed | tf_op | source)
XLA Modules:
  0.0 45.9 jit_solution(1284612021962788047)
XLA Ops:
  0.6 0.7 %negate_select_fusion.signed_ref = f32[16,128]{1,0:T(8,128)S(1)} fusion(f32[16,128]{1,0:T(8,128)} %param.7, s32[16,128]{1,0:T(8,128)} %param.6), kind=kLoop, calls=%fused_computation.1 | loop fusion | flops 6144 | bytes 24576 | tf_op jit(solution)/shard_map/jit(_where)/select_n | solution.py:392
  1.4 1.0 %copy-done = f32[1,48,16,128]{3,2,1,0:T(8,128)S(1)} copy-done((f32[1,48,16,128]{3,2,1,0:T(8,128)S(1)}, f32[1,48,16,128]{3,2,1,0:T(8,128)}, u32[]{:S(2)}) %copy-start) | copy-done | bytes 393240
  2.3 0.3 shard_map.68
  2.6 0.0 collective-permute-start
  2.6 8.5 %collective-permute-start.1 = (f32[72,128]{1,0:T(8,128)S(1)}, f32[72,128]{1,0:T(8,128)S(1)}, u32[]{:S(2)}, u32[]{:S(2)}) collective-permute-start(f32[72,128]{1,0:T(8,128)S(1)} %get-tuple-element.43), channel_id=1, source_target_pairs={{0,15},{1,0},{2,1},{3,2},{4,3},{5,4},{6,5},{7,6},{8,7},{9,8},{10,9... | collective-permute-start | bytes 110600 | tf_op jit(solution)/shard_map/ppermute | solution.py:382
  11.1 0.8 %broadcast_multiply_fusion.mix_ref = f32[2,48,48]{2,1,0:T(8,128)S(1)} fusion(f32[2]{0:T(128)} %constant.11.clone, f32[48,48]{1,0:T(8,128)} %param.8), kind=kLoop, calls=%fused_computation | loop fusion | flops 4608 | bytes 27656 | tf_op jit(solution)/shard_map/mul | solution.py:388
  12.0 0.8 %collective-permute-done.rl_ref = f32[72,128]{1,0:T(8,128)S(1)} collective-permute-done((f32[72,128]{1,0:T(8,128)S(1)}, f32[72,128]{1,0:T(8,128)S(1)}, u32[]{:S(2)}, u32[]{:S(2)}) %collective-permute-start) | collective-permute-done | bytes 36896 | tf_op jit(solution)/shard_map/ppermute | solution.py:382
  12.8 0.0 collective-permute-done.1.rr_ref
  12.8 0.1 shard_map.69
  12.9 4.7 %collective-permute-start.3 = (f32[544,128]{1,0:T(8,128)S(1)}, f32[544,128]{1,0:T(8,128)S(1)}, u32[]{:S(2)}, u32[]{:S(2)}) collective-permute-start(f32[544,128]{1,0:T(8,128)S(1)} %get-tuple-element.48), channel_id=1, source_target_pairs={{0,16},{16,32},{32,48},{48,64},{64,80},{80,96},{96,112},{1,17},{17... | collective-permute-start | bytes 835592 | tf_op jit(solution)/shard_map/ppermute | solution.py:382
  17.6 1.9 %collective-permute-start.2 = (f32[544,128]{1,0:T(8,128)S(1)}, f32[544,128]{1,0:T(8,128)S(1)}, u32[]{:S(2)}, u32[]{:S(2)}) collective-permute-start(f32[544,128]{1,0:T(8,128)S(1)} %get-tuple-element.47), channel_id=1, source_target_pairs={{16,0},{32,16},{48,32},{64,48},{80,64},{96,80},{112,96},{17,1},{33... | collective-permute-start | bytes 835592 | tf_op jit(solution)/shard_map/ppermute | solution.py:382
  19.5 1.3 %collective-permute-start.6 = (f32[768,128]{1,0:T(8,128)S(1)}, f32[768,128]{1,0:T(8,128)S(1)}, u32[]{:S(2)}, u32[]{:S(2)}) collective-permute-start(f32[768,128]{1,0:T(8,128)S(1)} %get-tuple-element.49.core_ref), channel_id=1, source_target_pairs={{0,128},{128,256},{256,384},{1,129},{129,257},{257,385},{2,130},{1... | collective-permute-start | bytes 1179656 | tf_op jit(solution)/shard_map/ppermute | solution.py:382
  20.8 1.8 %shard_map.70 = (f32[34,48,256]{2,1,0:T(8,128)S(1)}, f32[34,48,256]{2,1,0:T(8,128)S(1)}, f32[34,48,256]{2,1,0:T(8,128)S(1)}, f32[34,48,256]{2,1,0:T(8,128)S(1)},...) custom-call(f32[1]{0:T(128)} %bitcast.later_ref.refs_0_, ...), custom_call_target="tpu_custom_call" | custom-call | tf_op jit(solution)/shard_map/pallas_call | solution.py:407
  22.7 1.5 %shard_map.71 = (f32[34,48,256]{2,1,0:T(8,128)S(1)}, f32[34,48,256]{2,1,0:T(8,128)S(1)}, f32[34,48,256]{2,1,0:T(8,128)S(1)}, f32[34,48,256]{2,1,0:T(8,128)S(1)},...) custom-call(f32[1]{0:T(128)} %bitcast.later_ref.refs_0_, ...), custom_call_target="tpu_custom_call", output_to_operand_aliasing={{0}: (6, {}), {1}: (7, {}), {2}: (8, {}), {3}: (9, {}), {4}... | custom-call | tf_op jit(solution)/shard_map/pallas_call | solution.py:416
  24.2 3.1 %collective-permute-done.2.refs_5_ = f32[544,128]{1,0:T(8,128)S(1)} collective-permute-done((f32[544,128]{1,0:T(8,128)S(1)}, f32[544,128]{1,0:T(8,128)S(1)}, u32[]{:S(2)}, u32[]{:S(2)}) %collective-permute-start.2) | collective-permute-done | bytes 278560 | tf_op jit(solution)/shard_map/ppermute | solution.py:382
  27.2 3.1 %shard_map.72 = (f32[34,48,256]{2,1,0:T(8,128)S(1)}, f32[34,48,256]{2,1,0:T(8,128)S(1)}, f32[34,48,256]{2,1,0:T(8,128)S(1)}, f32[34,48,256]{2,1,0:T(8,128)S(1)},...) custom-call(f32[1]{0:T(128)} %bitcast.later_ref.refs_0_, ...), custom_call_target="tpu_custom_call", output_to_operand_aliasing={{0}: (6, {}), {1}: (7, {}), {2}: (8, {}), {3}: (9, {}), {4}... | custom-call | tf_op jit(solution)/shard_map/pallas_call | solution.py:419
  30.3 1.3 %collective-permute-start.5 = (f32[600,128]{1,0:T(8,128)S(1)}, f32[600,128]{1,0:T(8,128)S(1)}, u32[]{:S(2)}, u32[]{:S(2)}) collective-permute-start(f32[600,128]{1,0:T(8,128)S(1)} %get-tuple-element.67), channel_id=1, source_target_pairs={{0,128},{128,256},{256,384},{1,129},{129,257},{257,385},{2,130},{1... | collective-permute-start | bytes 921608 | tf_op jit(solution)/shard_map/ppermute | solution.py:382
  31.6 1.3 %collective-permute-start.4 = (f32[392,128]{1,0:T(8,128)S(1)}, f32[392,128]{1,0:T(8,128)S(1)}, u32[]{:S(2)}, u32[]{:S(2)}) collective-permute-start(f32[392,128]{1,0:T(8,128)S(1)} %get-tuple-element.66), channel_id=1, source_target_pairs={{0,384},{1,385},{2,386},{3,387},{4,388},{5,389},{6,390},{7,391},{8... | collective-permute-start | bytes 602120 | tf_op jit(solution)/shard_map/ppermute | solution.py:382
  32.9 1.3 %collective-permute-start.7 = (f32[336,128]{1,0:T(8,128)S(1)}, f32[336,128]{1,0:T(8,128)S(1)}, u32[]{:S(2)}, u32[]{:S(2)}) collective-permute-start(f32[336,128]{1,0:T(8,128)S(1)} %get-tuple-element.72), channel_id=1, source_target_pairs={{0,256},{128,384},{1,257},{129,385},{2,258},{130,386},{3,259},{131... | collective-permute-start | bytes 516104 | tf_op jit(solution)/shard_map/ppermute | solution.py:382
  34.2 0.9 %shard_map.74 = (f32[768,128]{1,0:T(8,128)S(1)}, f32[768,128]{1,0:T(8,128)S(1)}) custom-call(f32[768,128]{1,0:T(8,128)S(1)} %collective-permute-done.6.core_ref, bf16[48,144]{1,0:T(8,128)(2,1)S(1)} %get-tuple-element.46.fine_mix.refs_3_, f32[5,16,128]{2,1,0:T(8,128)S(1)} %get-tuple-element.68.cf_ref, f32[34,48,256]{2,1,0:T(8,128)S(1)} %get-tuple-element.69.u3, ...), custom_call_target="tpu_custom_call" | custom-call | tf_op jit(solution)/shard_map/pallas_call | solution.py:429
  35.1 7.2 %collective-permute-done.4.q3_ref = f32[392,128]{1,0:T(8,128)S(1)} collective-permute-done((f32[392,128]{1,0:T(8,128)S(1)}, f32[392,128]{1,0:T(8,128)S(1)}, u32[]{:S(2)}, u32[]{:S(2)}) %collective-permute-start.4) | collective-permute-done | bytes 200736 | tf_op jit(solution)/shard_map/ppermute | solution.py:382
  42.3 0.7 %shard_map.73.far = f32[16,48,256]{2,1,0:T(8,128)S(1)} custom-call(bf16[48,144]{1,0:T(8,128)(2,1)S(1)} %get-tuple-element.44.coarse_mix.refs_4_, f32[6,16,256]{2,1,0:T(8,128)S(1)} %get-tuple-element.65.cc_ref, f32[392,128]{1,0:T(8,128)S(1)} %collective-permute-done.4.q3_ref), custom_call_target="tpu_custom_call" | custom-call | tf_op jit(solution)/shard_map/pallas_call | solution.py:433
  43.0 0.8 %shard_map.75 = (f32[16,48,256]{2,1,0:T(8,128)S(1)}, f32[768,128]{1,0:T(8,128)S(1)}) custom-call(f32[600,128]{1,0:T(8,128)S(1)} %collective-permute-done.5.q1_ref, f32[768,128]{1,0:T(8,128)S(1)} %get-tuple-element.70.inner_ref, f32[6,16,256]{2,1,0:T(8,128)S(1)} %get-tuple-element.65.cc_ref, f32[32,128]{1,0:T(8,128)S(1)} %get-tuple-element.40.mk_ref.refs_1_), custom_call_target="tpu_custom_call" | custom-call | tf_op jit(solution)/shard_map/pallas_call | solution.py:432
  43.8 2.1 %shard_map.76 = (f32[768,128]{1,0:T(8,128)}, f32[768,128]{1,0:T(8,128)}) custom-call(f32[1]{0:T(128)} %bitcast.later_ref.refs_0_, f32[32,128]{1,0:T(8,128)S(1)} %get-tuple-element.40.mk_ref.refs_1_, bf16[48,144]{1,0:T(8,128)(2,1)S(1)} %get-tuple-element.44.coarse_mix.refs_4_, f32[6,16,256]{2,1,0:T(8,128)S(1)} %get-tuple-element.65.cc_ref, ...), custom_call_target="tpu_custom_call" | custom-call | tf_op jit(solution)/shard_map/pallas_call | solution.py:434
  (7 shorter events, 0.0 us)
Async XLA Ops:
  1.3 1.0 %copy-start = (f32[1,48,16,128]{3,2,1,0:T(8,128)S(1)}, f32[1,48,16,128]{3,2,1,0:T(8,128)}, u32[]{:S(2)}) copy-start(f32[1,48,16,128]{3,2,1,0:T(8,128)} %param.5) | copy-start | bytes 1179652
  2.6 10.1 %collective-permute-start = (f32[72,128]{1,0:T(8,128)S(1)}, f32[72,128]{1,0:T(8,128)S(1)}, u32[]{:S(2)}, u32[]{:S(2)}) collective-permute-start(f32[72,128]{1,0:T(8,128)S(1)} %get-tuple-element.42), channel_id=1, source_target_pairs={{0,1},{1,2},{2,3},{3,4},{4,5},{5,6},{6,7},{7,8},{8,9},{9,10},{10,1... | collective-permute-start | bytes 110600 | tf_op jit(solution)/shard_map/ppermute | solution.py:382
  2.6 10.1 %collective-permute-start.1 = (f32[72,128]{1,0:T(8,128)S(1)}, f32[72,128]{1,0:T(8,128)S(1)}, u32[]{:S(2)}, u32[]{:S(2)}) collective-permute-start(f32[72,128]{1,0:T(8,128)S(1)} %get-tuple-element.43), channel_id=1, source_target_pairs={{0,15},{1,0},{2,1},{3,2},{4,3},{5,4},{6,5},{7,6},{8,7},{9,8},{10,9... | collective-permute-start | bytes 110600 | tf_op jit(solution)/shard_map/ppermute | solution.py:382
  12.9 9.8 %collective-permute-start.3 = (f32[544,128]{1,0:T(8,128)S(1)}, f32[544,128]{1,0:T(8,128)S(1)}, u32[]{:S(2)}, u32[]{:S(2)}) collective-permute-start(f32[544,128]{1,0:T(8,128)S(1)} %get-tuple-element.48), channel_id=1, source_target_pairs={{0,16},{16,32},{32,48},{48,64},{64,80},{80,96},{96,112},{1,17},{17... | collective-permute-start | bytes 835592 | tf_op jit(solution)/shard_map/ppermute | solution.py:382
  17.6 9.7 %collective-permute-start.2 = (f32[544,128]{1,0:T(8,128)S(1)}, f32[544,128]{1,0:T(8,128)S(1)}, u32[]{:S(2)}, u32[]{:S(2)}) collective-permute-start(f32[544,128]{1,0:T(8,128)S(1)} %get-tuple-element.47), channel_id=1, source_target_pairs={{16,0},{32,16},{48,32},{64,48},{80,64},{96,80},{112,96},{17,1},{33... | collective-permute-start | bytes 835592 | tf_op jit(solution)/shard_map/ppermute | solution.py:382
  19.5 14.7 %collective-permute-start.6 = (f32[768,128]{1,0:T(8,128)S(1)}, f32[768,128]{1,0:T(8,128)S(1)}, u32[]{:S(2)}, u32[]{:S(2)}) collective-permute-start(f32[768,128]{1,0:T(8,128)S(1)} %get-tuple-element.49.core_ref), channel_id=1, source_target_pairs={{0,128},{128,256},{256,384},{1,129},{129,257},{257,385},{2,130},{1... | collective-permute-start | bytes 1179656 | tf_op jit(solution)/shard_map/ppermute | solution.py:382
  30.3 12.7 %collective-permute-start.5 = (f32[600,128]{1,0:T(8,128)S(1)}, f32[600,128]{1,0:T(8,128)S(1)}, u32[]{:S(2)}, u32[]{:S(2)}) collective-permute-start(f32[600,128]{1,0:T(8,128)S(1)} %get-tuple-element.67), channel_id=1, source_target_pairs={{0,128},{128,256},{256,384},{1,129},{129,257},{257,385},{2,130},{1... | collective-permute-start | bytes 921608 | tf_op jit(solution)/shard_map/ppermute | solution.py:382
  31.6 10.7 %collective-permute-start.4 = (f32[392,128]{1,0:T(8,128)S(1)}, f32[392,128]{1,0:T(8,128)S(1)}, u32[]{:S(2)}, u32[]{:S(2)}) collective-permute-start(f32[392,128]{1,0:T(8,128)S(1)} %get-tuple-element.66), channel_id=1, source_target_pairs={{0,384},{1,385},{2,386},{3,387},{4,388},{5,389},{6,390},{7,391},{8... | collective-permute-start | bytes 602120 | tf_op jit(solution)/shard_map/ppermute | solution.py:382
  32.9 10.9 %collective-permute-start.7 = (f32[336,128]{1,0:T(8,128)S(1)}, f32[336,128]{1,0:T(8,128)S(1)}, u32[]{:S(2)}, u32[]{:S(2)}) collective-permute-start(f32[336,128]{1,0:T(8,128)S(1)} %get-tuple-element.72), channel_id=1, source_target_pairs={{0,256},{128,384},{1,257},{129,385},{2,258},{130,386},{3,259},{131... | collective-permute-start | bytes 516104 | tf_op jit(solution)/shard_map/ppermute | solution.py:382
  34.2 9.6 %copy-start.1 = (f32[1,48,16,128]{3,2,1,0:T(8,128)S(1)}, f32[1,48,16,128]{3,2,1,0:T(8,128)}, u32[]{:S(2)}) copy-start(f32[1,48,16,128]{3,2,1,0:T(8,128)} %param.5) | copy-start | bytes 1179652

commit v6 on v5

--- a/solution.py
+++ b/solution.py
@@ -18,7 +18,7 @@
 REACH = 3
 RING = [*range(REACH), *range(R - REACH, R)]
 SIDE = range(2, 6)
-Q3, Q2, Q1, RG = 49 * 8, 42 * 8, 35 * 8, 40 * 8
+Q3, Q2, Q1, RG = 49 * 8, 39 * 8, 32 * 8, 40 * 8
 LAT = H * K + 8 * H + 2 * R + 8
 VMEM = pl.BlockSpec(memory_space=pltpu.VMEM)
 SMEM = pl.BlockSpec(memory_space=pltpu.SMEM)
@@ -185,22 +185,62 @@
         core_cf[i] = cf[i, :, :C]
 
 
-def put_q(q_ref, out_ref, first, count):
+PAIRS3 = [(i, i + 1) for i in range(1, 15, 2)]
+PAIRS2 = [(2, 13), *PAIRS3[1:6]]
+PAIRS1 = PAIRS3[1:6]
+
+
+def join(qs, pair):
     even = lanes((K, W)) % 2 == 0
-    for p in range(count // 2):
-        odd = by_tile(lambda t: shift(t, 1), q_ref[first + 2 * p + 1])
-        both = jnp.where(even, q_ref[first + 2 * p], odd)
+    return jnp.where(even, qs[pair[0]], by_tile(lambda t: shift(t, 1), qs[pair[1]]))
+
+
+def put_q3(qs, out_ref, indices):
+    for p in indices:
+        both = join(qs, PAIRS3[p])
         out_ref[pl.ds(p * K, K), :] = both[:, :C]
-        out_ref[pl.ds((count // 2) * K + 8 * p, 8), :] = pack_row(both[:, C:])
-
-
-def take_q(in_ref, count, write):
-    for p in range(count // 2):
-        core = in_ref[pl.ds(p * K, K), :]
-        side = unpack_row(in_ref[pl.ds((count // 2) * K + 8 * p, 8), :])
-        both = jnp.concatenate([core, side], axis=1)
-        write(2 * p, both)
-        write(2 * p + 1, by_tile(lambda t: shift(t, -1), both))
+        out_ref[pl.ds(7 * K + 8 * p, 8), :] = pack_row(both[:, C:])
+
+
+def ends3(q3_ref, p):
+    return q3_ref[pl.ds(7 * K + 8 * p, 8), :]
+
+
+def put_q2(qs, q3_ref, out_ref):
+    both = join(qs, PAIRS2[0])
+    out_ref[pl.ds(0, K), :] = both[:, :C]
+    out_ref[pl.ds(K, 5 * K), :] = q3_ref[pl.ds(K, 5 * K), :]
+    ends = [pack_row(both[:, C:])] + [ends3(q3_ref, p) for p in range(1, 6)]
+    low = lanes((8, C)) % SLOT < H
+    for j in range(3):
+        both = jnp.where(low, shift(ends[j], -5), shift(ends[j + 3], 4))
+        out_ref[pl.ds(6 * K + 8 * j, 8), :] = both
+
+
+def put_q1(q3_ref, out_ref):
+    out_ref[pl.ds(0, 5 * K), :] = q3_ref[pl.ds(K, 5 * K), :]
+    ends = [ends3(q3_ref, p) for p in range(1, 6)]
+    at = lanes((8, C)) % SLOT
+    both = shift(ends[3], 5)
+    for k in (2, 1, 0):
+        both = jnp.where(at < 4 * k + 4, shift(ends[k], 4 * k - 7), both)
+    out_ref[pl.ds(5 * K, 8), :] = both
+    out_ref[pl.ds(5 * K + 8, 8), :] = ends[4]
+
+
+def take_q(in_ref, pairs, write):
+    for p, (first, second) in enumerate(pairs):
+        n = len(pairs)
+        ends = lambda j: in_ref[pl.ds(n * K + 8 * j, 8), :]
+        if n == 7:
+            packed = ends(p)
+        elif n == 6:
+            packed = shift(ends(p % 3), 5 if p < 3 else -4)
+        else:
+            packed = shift(ends(0), 7 - 4 * p) if p < 4 else ends(1)
+        both = jnp.concatenate([in_ref[pl.ds(p * K, K), :], unpack_row(packed)], axis=1)
+        write(first, both)
+        write(second, by_tile(lambda t: shift(t, -1), both))
 
 
 def put_ring(src, out_ref):
@@ -267,18 +307,22 @@
 
 def upper_kernel(*refs):
     *ins, mk, cf, cc = refs
-    outer_rows(True, *ins[:6], ins[13:20], ins[20], mk, cf, cc)
+    states, cc_out, q3_ref = ins[13:20], ins[20], ins[21]
+    outer_rows(True, *ins[:6], states, cc_out, mk, cf, cc)
+    put_q3(states[6], q3_ref, range(4))
 
 
 def lower_kernel(*refs):
-    *ins, q3_ref, q2_ref, q1_ref, mk, cf, cc = refs
-    states = ins[14:21]
-    outer_rows(False, *ins[:6], states, ins[21], mk, cf, cc)
-    u3, qs = states[3], states[6]
-    put_q(qs, q3_ref, 1, 14)
-    put_q(qs, q2_ref, 2, 12)
-    put_q(qs, q1_ref, 3, 10)
-    put_ring(u3, q1_ref)
+    *ins, mk, cf, cc = refs
+    states, cc_out, q3_ref, q2_ref = ins[15:22], ins[22], ins[23], ins[24]
+    outer_rows(False, *ins[:6], states, cc_out, mk, cf, cc)
+    put_q3(states[6], q3_ref, range(4, 7))
+    put_q2(states[6], q3_ref, q2_ref)
+
+
+def near_message_kernel(u3, q3_ref, out_ref):
+    put_q1(q3_ref, out_ref)
+    put_ring(u3, out_ref)
 
 
 def before_kernel(core_ref, fine_mix, cf_ref, u3, cc_ref, mk_ref, inner_ref, rest_ref, ua, ub):
@@ -306,7 +350,7 @@
 
 
 def near_kernel(q1_ref, inner_ref, cc_ref, mk_ref, a, base_ref):
-    take_q(q1_ref, 10, lambda i, value: a.__setitem__(3 + i, value))
+    take_q(q1_ref, PAIRS1, lambda i, value: a.__setitem__(i, value))
     rows = take_ring(q1_ref, inner_ref)
     for i in range(R // 2):
         pair = rows[2 * i], rows[2 * i + 1]
@@ -315,8 +359,8 @@
             base_ref[pl.ds(r * K, K), :] = value - mk_ref[pl.ds(r, 1), :] * fc
 
 
-def far_kernel(coarse_mix, cc_ref, q3_ref, b, a):
-    take_q(q3_ref, 14, lambda i, value: a.__setitem__(1 + i, value))
+def far_kernel(coarse_mix, cc_ref, q3_ref, _, b, a):
+    take_q(q3_ref, PAIRS3, lambda i, value: a.__setitem__(i, value))
     for i in range(2, 14):
         b[i] = step_row(a, i, cc_ref, i, 2, coarse_mix[...])
 
@@ -325,7 +369,7 @@
     later_ref, mk_ref, coarse_mix, cc_ref, x_ref, far, near, q2_ref, qs, rest_ref, base_ref,
     out_hbm, next_hbm, a, b, out_ref, next_ref, sems,
 ):
-    take_q(q2_ref, 12, lambda i, value: b.__setitem__(2 + i, far[2 + i] + value))
+    take_q(q2_ref, PAIRS2, lambda i, value: b.__setitem__(i, far[i] + value))
     for i in range(3, 13):
         a[i] = near[i] + step_row(b, i, cc_ref, i, 2, coarse_mix[...])
     first = later_ref[0] == 0.0
@@ -414,23 +458,29 @@
     parts = [scratch(4, 48, C), scratch(5, 48, W), scratch(6, NC, W)]
     coefs = f32(6, NC, W)
     states = call(
-        upper_kernel, 13, shapes + (coefs,), parts, smem=1, aliases={6 + i: i for i in range(7)}
-    )(later, mk, side, fine_mix, coarse_mix, up, *states)
-    *states, cc, q3, q2, q1 = call(
-        lower_kernel,
-        14,
-        shapes + (coefs, f32(Q3, C), f32(Q2, C), f32(Q1 + RG, C)),
+        upper_kernel,
+        13,
+        shapes + (coefs, f32(Q3, C)),
         parts,
         smem=1,
-        aliases={6 + i: i for i in range(8)},
+        aliases={6 + i: i for i in range(7)},
+    )(later, mk, side, fine_mix, coarse_mix, up, *states)
+    *states, cc, q3, q2 = call(
+        lower_kernel,
+        15,
+        shapes + (coefs, f32(Q3, C), f32(Q2, C)),
+        parts,
+        smem=1,
+        aliases={6 + i: i for i in range(9)},
     )(later, mk, side, fine_mix, coarse_mix, down, *states)
     u3, qs = states[3], states[6]
+    q1 = call(near_message_kernel, 2, f32(Q1 + RG, C))(u3, q3)
     q3, q2, q1 = moved(q3, "tm", 3), moved(q2, "tm", 2), moved(q1, "tm", 1)
     inner, rest = call(
         before_kernel, 6, (f32(R * K, C), f32(R * K, C)), [scratch(R, K, C), scratch(R, K, C)]
     )(before, fine_mix, cf, u3, cc, mk)
     near, base = call(near_kernel, 4, (coarse, f32(R * K, C)))(q1, inner, cc, mk)
-    far = call(far_kernel, 3, coarse, [scratch(NC, K, W)])(coarse_mix, cc, q3)
+    far = call(far_kernel, 4, coarse, [scratch(NC, K, W)])(coarse_mix, cc, q3, near)
     out, following = call(
         last_kernel,
         11,

time: 46.2 us -> 44 us (0.952)
  the two profiles are of different devices: /device:TPU:30 before, /device:TPU:28 now
where the time goes in v6:
time: 44 us; the launch traced here: 43.5 us
  starting transfers between devices  23.3 us (53%)
  Pallas kernels  9.96 us (23%)
  waiting for transfers between devices  6.94 us (16%)
  other arithmetic  1.54 us (4%)
  local copies, waits for them, and re-layouts  1 us (2%)
  between operations  0.78 us (2%)
    ppermute x8, starting transfers between devices, moved(): return lax.ppermute(value, axis, pairs)  23.3 us
    ppermute x8, waiting for transfers between devices, moved(): return lax.ppermute(value, axis, pairs)  6.94 us
    pallas_call x1, Pallas kernels, body(): call(last_kernel, 11, (f32(K * R, C), f32(K * R, C)), [scratch(NC, K, W)]...  1.95 us
    pallas_call x1, Pallas kernels, body(): call(own_kernel, 6, shapes + (f32(5, R, C),), [scratch(4, R, C), scratch(...  1.82 us
    pallas_call x1, Pallas kernels, body(): call(lower_kernel, 15, shapes + (coefs, f32(Q3, C), f32(Q2, C)), parts, s...  1.65 us
    pallas_call x1, Pallas kernels, body(): call(upper_kernel, 13, shapes + (coefs, f32(Q3, C)), parts, smem=1, alias...  1.64 us
    unnamed x4, local copies, waits for them, and re-layouts  1 us
  transfers between devices with their start and end apart: 8, of which 4 were waited for; matrix products, arithmetic and copies ran while one was open for 2% of the time, Pallas kernels for 18%

profile of v6, /device:TPU:28, one launch (start us, length us, event | category | flops | bytes accessed | tf_op | source)
XLA Modules:
  0.0 43.5 jit_solution(17326791285459038478)
XLA Ops:
  0.6 0.7 %negate_select_fusion.signed_ref = f32[16,128]{1,0:T(8,128)S(1)} fusion(f32[16,128]{1,0:T(8,128)} %param.7, s32[16,128]{1,0:T(8,128)} %param.6), kind=kLoop, calls=%fused_computation.1 | loop fusion | flops 6144 | bytes 24576 | tf_op jit(solution)/shard_map/jit(_where)/select_n | solution.py:436
  1.4 1.0 %copy-done = f32[1,48,16,128]{3,2,1,0:T(8,128)S(1)} copy-done((f32[1,48,16,128]{3,2,1,0:T(8,128)S(1)}, f32[1,48,16,128]{3,2,1,0:T(8,128)}, u32[]{:S(2)}) %copy-start) | copy-done | bytes 393240
  2.3 0.3 shard_map.68
  2.6 8.5 %collective-permute-start.1 = (f32[72,128]{1,0:T(8,128)S(1)}, f32[72,128]{1,0:T(8,128)S(1)}, u32[]{:S(2)}, u32[]{:S(2)}) collective-permute-start(f32[72,128]{1,0:T(8,128)S(1)} %get-tuple-element.43), channel_id=1, source_target_pairs={{0,15},{1,0},{2,1},{3,2},{4,3},{5,4},{6,5},{7,6},{8,7},{9,8},{10,9... | collective-permute-start | bytes 110600 | tf_op jit(solution)/shard_map/ppermute | solution.py:426
  11.1 0.8 %broadcast_multiply_fusion.mix_ref = f32[2,48,48]{2,1,0:T(8,128)S(1)} fusion(f32[2]{0:T(128)} %constant.11.clone, f32[48,48]{1,0:T(8,128)} %param.8), kind=kLoop, calls=%fused_computation | loop fusion | flops 4608 | bytes 27656 | tf_op jit(solution)/shard_map/mul | solution.py:432
  12.0 0.8 %collective-permute-done.rl_ref = f32[72,128]{1,0:T(8,128)S(1)} collective-permute-done((f32[72,128]{1,0:T(8,128)S(1)}, f32[72,128]{1,0:T(8,128)S(1)}, u32[]{:S(2)}, u32[]{:S(2)}) %collective-permute-start) | collective-permute-done | bytes 36896 | tf_op jit(solution)/shard_map/ppermute | solution.py:426
  12.8 0.1 shard_map.69
  12.9 4.7 %collective-permute-start.3 = (f32[544,128]{1,0:T(8,128)S(1)}, f32[544,128]{1,0:T(8,128)S(1)}, u32[]{:S(2)}, u32[]{:S(2)}) collective-permute-start(f32[544,128]{1,0:T(8,128)S(1)} %get-tuple-element.48), channel_id=1, source_target_pairs={{0,16},{16,32},{32,48},{48,64},{64,80},{80,96},{96,112},{1,17},{17... | collective-permute-start | bytes 835592 | tf_op jit(solution)/shard_map/ppermute | solution.py:426
  17.6 1.9 %collective-permute-start.2 = (f32[544,128]{1,0:T(8,128)S(1)}, f32[544,128]{1,0:T(8,128)S(1)}, u32[]{:S(2)}, u32[]{:S(2)}) collective-permute-start(f32[544,128]{1,0:T(8,128)S(1)} %get-tuple-element.47), channel_id=1, source_target_pairs={{16,0},{32,16},{48,32},{64,48},{80,64},{96,80},{112,96},{17,1},{33... | collective-permute-start | bytes 835592 | tf_op jit(solution)/shard_map/ppermute | solution.py:426
  19.5 3.1 %collective-permute-start.6 = (f32[768,128]{1,0:T(8,128)S(1)}, f32[768,128]{1,0:T(8,128)S(1)}, u32[]{:S(2)}, u32[]{:S(2)}) collective-permute-start(f32[768,128]{1,0:T(8,128)S(1)} %get-tuple-element.49.core_ref), channel_id=1, source_target_pairs={{0,128},{128,256},{256,384},{1,129},{129,257},{257,385},{2,130},{1... | collective-permute-start | bytes 1179656 | tf_op jit(solution)/shard_map/ppermute | solution.py:426
  22.6 1.8 %shard_map.70 = (f32[34,48,256]{2,1,0:T(8,128)S(1)}, f32[34,48,256]{2,1,0:T(8,128)S(1)}, f32[34,48,256]{2,1,0:T(8,128)S(1)}, f32[34,48,256]{2,1,0:T(8,128)S(1)},...) custom-call(f32[1]{0:T(128)} %bitcast.later_ref.refs_0_, ...), custom_call_target="tpu_custom_call" | custom-call | tf_op jit(solution)/shard_map/pallas_call | solution.py:451
  24.5 1.6 %shard_map.71 = (f32[34,48,256]{2,1,0:T(8,128)S(1)}, f32[34,48,256]{2,1,0:T(8,128)S(1)}, f32[34,48,256]{2,1,0:T(8,128)S(1)}, f32[34,48,256]{2,1,0:T(8,128)S(1)},...) custom-call(f32[1]{0:T(128)} %bitcast.later_ref.refs_0_, ...), custom_call_target="tpu_custom_call", output_to_operand_aliasing={{0}: (6, {}), {1}: (7, {}), {2}: (8, {}), {3}: (9, {}), {4}... | custom-call | tf_op jit(solution)/shard_map/pallas_call | solution.py:460
  26.1 1.1 %collective-permute-done.2.refs_5_ = f32[544,128]{1,0:T(8,128)S(1)} collective-permute-done((f32[544,128]{1,0:T(8,128)S(1)}, f32[544,128]{1,0:T(8,128)S(1)}, u32[]{:S(2)}, u32[]{:S(2)}) %collective-permute-start.2) | collective-permute-done | bytes 278560 | tf_op jit(solution)/shard_map/ppermute | solution.py:426
  27.2 1.6 %shard_map.72 = (f32[34,48,256]{2,1,0:T(8,128)S(1)}, f32[34,48,256]{2,1,0:T(8,128)S(1)}, f32[34,48,256]{2,1,0:T(8,128)S(1)}, f32[34,48,256]{2,1,0:T(8,128)S(1)},...) custom-call(f32[1]{0:T(128)} %bitcast.later_ref.refs_0_, ...), custom_call_target="tpu_custom_call", output_to_operand_aliasing={{0}: (6, {}), {1}: (7, {}), {2}: (8, {}), {3}: (9, {}), {4}... | custom-call | tf_op jit(solution)/shard_map/pallas_call | solution.py:468
  28.9 0.2 shard_map.73
  29.1 3.1 %collective-permute-start.5 = (f32[576,128]{1,0:T(8,128)S(1)}, f32[576,128]{1,0:T(8,128)S(1)}, u32[]{:S(2)}, u32[]{:S(2)}) collective-permute-start(f32[576,128]{1,0:T(8,128)S(1)} %shard_map.73), channel_id=1, source_target_pairs={{0,128},{128,256},{256,384},{1,129},{129,257},{257,385},{2,130},{1... | collective-permute-start | bytes 884744 | tf_op jit(solution)/shard_map/ppermute | solution.py:426
  32.2 0.7 %collective-permute-start.4 = (f32[392,128]{1,0:T(8,128)S(1)}, f32[392,128]{1,0:T(8,128)S(1)}, u32[]{:S(2)}, u32[]{:S(2)}) collective-permute-start(f32[392,128]{1,0:T(8,128)S(1)} %get-tuple-element.67.q3_ref), channel_id=1, source_target_pairs={{0,384},{1,385},{2,386},{3,387},{4,388},{5,389},{6,390},{7,391},{8... | collective-permute-start | bytes 602120 | tf_op jit(solution)/shard_map/ppermute | solution.py:426
  32.9 1.3 %collective-permute-start.7 = (f32[312,128]{1,0:T(8,128)S(1)}, f32[312,128]{1,0:T(8,128)S(1)}, u32[]{:S(2)}, u32[]{:S(2)}) collective-permute-start(f32[312,128]{1,0:T(8,128)S(1)} %get-tuple-element.72), channel_id=1, source_target_pairs={{0,256},{128,384},{1,257},{129,385},{2,258},{130,386},{3,259},{131... | collective-permute-start | bytes 479240 | tf_op jit(solution)/shard_map/ppermute | solution.py:426
  34.2 0.9 %shard_map.74 = (f32[768,128]{1,0:T(8,128)S(1)}, f32[768,128]{1,0:T(8,128)S(1)}) custom-call(f32[768,128]{1,0:T(8,128)S(1)} %collective-permute-done.6.core_ref, bf16[48,144]{1,0:T(8,128)(2,1)S(1)} %get-tuple-element.46.fine_mix.refs_3_, f32[5,16,128]{2,1,0:T(8,128)S(1)} %get-tuple-element.69.cf_ref, f32[34,48,256]{2,1,0:T(8,128)S(1)} %get-tuple-element.68.u3, ...), custom_call_target="tpu_custom_call" | custom-call | tf_op jit(solution)/shard_map/pallas_call | solution.py:479
  35.1 2.7 %collective-permute-done.5.q1_ref = f32[576,128]{1,0:T(8,128)S(1)} collective-permute-done((f32[576,128]{1,0:T(8,128)S(1)}, f32[576,128]{1,0:T(8,128)S(1)}, u32[]{:S(2)}, u32[]{:S(2)}) %collective-permute-start.5) | collective-permute-done | bytes 294944 | tf_op jit(solution)/shard_map/ppermute | solution.py:426
  37.8 0.7 %shard_map.75 = (f32[16,48,256]{2,1,0:T(8,128)S(1)}, f32[768,128]{1,0:T(8,128)S(1)}) custom-call(f32[576,128]{1,0:T(8,128)S(1)} %collective-permute-done.5.q1_ref, f32[768,128]{1,0:T(8,128)S(1)} %get-tuple-element.70.inner_ref, f32[6,16,256]{2,1,0:T(8,128)S(1)} %get-tuple-element.66.cc_ref, f32[32,128]{1,0:T(8,128)S(1)} %get-tuple-element.40.mk_ref.refs_1_), custom_call_target="tpu_custom_call" | custom-call | tf_op jit(solution)/shard_map/pallas_call | solution.py:482
  38.5 0.7 %shard_map.76.far = f32[16,48,256]{2,1,0:T(8,128)S(1)} custom-call(bf16[48,144]{1,0:T(8,128)(2,1)S(1)} %get-tuple-element.44.coarse_mix.refs_4_, f32[6,16,256]{2,1,0:T(8,128)S(1)} %get-tuple-element.66.cc_ref, f32[392,128]{1,0:T(8,128)S(1)} %collective-permute-done.4.q3_ref, f32[16,48,256]{2,1,0:T(8,128)S(1)} %get-tuple-element.71._.near), custom_call_target="tpu_custom_call" | custom-call | tf_op jit(solution)/shard_map/pallas_call | solution.py:483
  39.2 2.3 %collective-permute-done.7.q2_ref = f32[312,128]{1,0:T(8,128)S(1)} collective-permute-done((f32[312,128]{1,0:T(8,128)S(1)}, f32[312,128]{1,0:T(8,128)S(1)}, u32[]{:S(2)}, u32[]{:S(2)}) %collective-permute-start.7) | collective-permute-done | bytes 159776 | tf_op jit(solution)/shard_map/ppermute | solution.py:426
  41.6 2.0 %shard_map.77 = (f32[768,128]{1,0:T(8,128)}, f32[768,128]{1,0:T(8,128)}) custom-call(f32[1]{0:T(128)} %bitcast.later_ref.refs_0_, f32[32,128]{1,0:T(8,128)S(1)} %get-tuple-element.40.mk_ref.refs_1_, bf16[48,144]{1,0:T(8,128)(2,1)S(1)} %get-tuple-element.44.coarse_mix.refs_4_, f32[6,16,256]{2,1,0:T(8,128)S(1)} %get-tuple-element.66.cc_ref, ...), custom_call_target="tpu_custom_call" | custom-call | tf_op jit(solution)/shard_map/pallas_call | solution.py:484
  (8 shorter events, 0.1 us)
Async XLA Ops:
  1.3 1.0 %copy-start = (f32[1,48,16,128]{3,2,1,0:T(8,128)S(1)}, f32[1,48,16,128]{3,2,1,0:T(8,128)}, u32[]{:S(2)}) copy-start(f32[1,48,16,128]{3,2,1,0:T(8,128)} %param.5) | copy-start | bytes 1179652
  2.6 10.1 %collective-permute-start = (f32[72,128]{1,0:T(8,128)S(1)}, f32[72,128]{1,0:T(8,128)S(1)}, u32[]{:S(2)}, u32[]{:S(2)}) collective-permute-start(f32[72,128]{1,0:T(8,128)S(1)} %get-tuple-element.42), channel_id=1, source_target_pairs={{0,1},{1,2},{2,3},{3,4},{4,5},{5,6},{6,7},{7,8},{8,9},{9,10},{10,1... | collective-permute-start | bytes 110600 | tf_op jit(solution)/shard_map/ppermute | solution.py:426
  2.6 10.1 %collective-permute-start.1 = (f32[72,128]{1,0:T(8,128)S(1)}, f32[72,128]{1,0:T(8,128)S(1)}, u32[]{:S(2)}, u32[]{:S(2)}) collective-permute-start(f32[72,128]{1,0:T(8,128)S(1)} %get-tuple-element.43), channel_id=1, source_target_pairs={{0,15},{1,0},{2,1},{3,2},{4,3},{5,4},{6,5},{7,6},{8,7},{9,8},{10,9... | collective-permute-start | bytes 110600 | tf_op jit(solution)/shard_map/ppermute | solution.py:426
  12.9 11.6 %collective-permute-start.3 = (f32[544,128]{1,0:T(8,128)S(1)}, f32[544,128]{1,0:T(8,128)S(1)}, u32[]{:S(2)}, u32[]{:S(2)}) collective-permute-start(f32[544,128]{1,0:T(8,128)S(1)} %get-tuple-element.48), channel_id=1, source_target_pairs={{0,16},{16,32},{32,48},{48,64},{64,80},{80,96},{96,112},{1,17},{17... | collective-permute-start | bytes 835592 | tf_op jit(solution)/shard_map/ppermute | solution.py:426
  17.6 9.7 %collective-permute-start.2 = (f32[544,128]{1,0:T(8,128)S(1)}, f32[544,128]{1,0:T(8,128)S(1)}, u32[]{:S(2)}, u32[]{:S(2)}) collective-permute-start(f32[544,128]{1,0:T(8,128)S(1)} %get-tuple-element.47), channel_id=1, source_target_pairs={{16,0},{32,16},{48,32},{64,48},{80,64},{96,80},{112,96},{17,1},{33... | collective-permute-start | bytes 835592 | tf_op jit(solution)/shard_map/ppermute | solution.py:426
  19.5 14.7 %collective-permute-start.6 = (f32[768,128]{1,0:T(8,128)S(1)}, f32[768,128]{1,0:T(8,128)S(1)}, u32[]{:S(2)}, u32[]{:S(2)}) collective-permute-start(f32[768,128]{1,0:T(8,128)S(1)} %get-tuple-element.49.core_ref), channel_id=1, source_target_pairs={{0,128},{128,256},{256,384},{1,129},{129,257},{257,385},{2,130},{1... | collective-permute-start | bytes 1179656 | tf_op jit(solution)/shard_map/ppermute | solution.py:426
  29.1 8.7 %collective-permute-start.5 = (f32[576,128]{1,0:T(8,128)S(1)}, f32[576,128]{1,0:T(8,128)S(1)}, u32[]{:S(2)}, u32[]{:S(2)}) collective-permute-start(f32[576,128]{1,0:T(8,128)S(1)} %shard_map.73), channel_id=1, source_target_pairs={{0,128},{128,256},{256,384},{1,129},{129,257},{257,385},{2,130},{1... | collective-permute-start | bytes 884744 | tf_op jit(solution)/shard_map/ppermute | solution.py:426
  32.2 6.3 %collective-permute-start.4 = (f32[392,128]{1,0:T(8,128)S(1)}, f32[392,128]{1,0:T(8,128)S(1)}, u32[]{:S(2)}, u32[]{:S(2)}) collective-permute-start(f32[392,128]{1,0:T(8,128)S(1)} %get-tuple-element.67.q3_ref), channel_id=1, source_target_pairs={{0,384},{1,385},{2,386},{3,387},{4,388},{5,389},{6,390},{7,391},{8... | collective-permute-start | bytes 602120 | tf_op jit(solution)/shard_map/ppermute | solution.py:426
  32.9 8.7 %collective-permute-start.7 = (f32[312,128]{1,0:T(8,128)S(1)}, f32[312,128]{1,0:T(8,128)S(1)}, u32[]{:S(2)}, u32[]{:S(2)}) collective-permute-start(f32[312,128]{1,0:T(8,128)S(1)} %get-tuple-element.72), channel_id=1, source_target_pairs={{0,256},{128,384},{1,257},{129,385},{2,258},{130,386},{3,259},{131... | collective-permute-start | bytes 479240 | tf_op jit(solution)/shard_map/ppermute | solution.py:426
  35.1 6.5 %copy-start.1 = (f32[1,48,16,128]{3,2,1,0:T(8,128)S(1)}, f32[1,48,16,128]{3,2,1,0:T(8,128)}, u32[]{:S(2)}) copy-start(f32[1,48,16,128]{3,2,1,0:T(8,128)} %param.5) | copy-start | bytes 1179652

commit v7 on v6

--- a/solution.py
+++ b/solution.py
@@ -18,8 +18,9 @@
 REACH = 3
 RING = [*range(REACH), *range(R - REACH, R)]
 SIDE = range(2, 6)
-Q3, Q2, Q1, RG = 49 * 8, 39 * 8, 32 * 8, 40 * 8
-LAT = H * K + 8 * H + 2 * R + 8
+Q3, Q2, Q1, RG = 49 * 8, 39 * 8, 21 * 8, 40 * 8
+HALF = (H - 1) // 2
+LAT = H * K + 8 * HALF + 2 * R + 8
 VMEM = pl.BlockSpec(memory_space=pltpu.VMEM)
 SMEM = pl.BlockSpec(memory_space=pltpu.SMEM)
 ANY = pl.BlockSpec(memory_space=pl.ANY)
@@ -77,6 +78,23 @@
         right_ref[pl.ds(8 * p, 8), :] = jnp.where(low, shift(a, -H), b)
 
 
+def corner_rows(j, first_rows):
+    d = j + 1
+    place = (lambda k: k - 1) if first_rows else (lambda k: H - k)
+    return d, place(d), place(H - d)
+
+
+def corner_ends(halo_ref, first_rows):
+    low = lanes((8, C)) % SLOT < H
+    ends = [None] * H
+    for j in range(HALF):
+        d, near, far = corner_rows(j, first_rows)
+        both = halo_ref[pl.ds(H * K + 8 * j, 8), :]
+        ends[near] = both
+        ends[far] = jnp.where(low, shift(both, H - d), shift(both, d - H))
+    return ends
+
+
 def halo_kernel(
     core_in, mk_ref, rl_ref, rr_ref, mix_ref,
     core_ref, top_ref, bot_ref, side_ref, fine_ref, coarse_ref,
@@ -89,11 +107,17 @@
         a, b = rl_ref[pl.ds(8 * p, 8), :], rr_ref[pl.ds(8 * p, 8), :]
         side_ref[pl.ds(8 * p, 8), :] = jnp.where(low, a, shift(b, H))
         side_ref[pl.ds(8 * (p + half), 8), :] = jnp.where(low, shift(a, -H), b)
+    at = lanes((8, C)) % SLOT
     for ref, first in ((top_ref, 0), (bot_ref, R - H)):
         ref[pl.ds(0, H * K), :] = core_in[pl.ds(first * K, H * K), :]
-        ref[pl.ds(H * K, 8 * H), :] = side_ref[pl.ds(8 * first, 8 * H), :]
-        ref[pl.ds(H * K + 8 * H, 2 * R), :] = mk_ref[...]
-        ref[pl.ds(H * K + 8 * H + 2 * R, 8), :] = side_ref[pl.ds(8 * R, 8), :]
+        for j in range(HALF):
+            d, near, far = corner_rows(j, first == 0)
+            a, b = (side_ref[pl.ds(8 * (first + i), 8), :] for i in (near, far))
+            both = jnp.where(at < d, shift(b, d - H), a)
+            both = jnp.where(at >= SLOT - d, shift(b, H - d), both)
+            ref[pl.ds(H * K + 8 * j, 8), :] = both
+        ref[pl.ds(H * K + 8 * HALF, 2 * R), :] = mk_ref[...]
+        ref[pl.ds(H * K + 8 * HALF + 2 * R, 8), :] = side_ref[pl.ds(8 * R, 8), :]
 
 
 def split(x):
@@ -159,7 +183,7 @@
 
 
 def own_kernel(
-    later_ref, core_ref, side_ref, mk_ref, fine_mix, coarse_mix, u0, u1, u2, u3, rs, gs, qs, core_cf, mk, cf, cc
+    slot_ref, core_ref, side_ref, mk_ref, fine_mix, coarse_mix, u0, u1, u2, u3, rs, gs, qs, core_cf, mk, cf, cc
 ):
     for r in range(R):
         u0[H + r, :, :C] = core_ref[pl.ds(r * K, K), :]
@@ -180,7 +204,7 @@
     for i in range(5, 11):
         gs[i] = step_row(rs, i, cc, i - 4, 2, coarse_mix[...])
     for i in range(6, 10):
-        qs[i] = restrict(u3, i, cc, i - 4) - later_ref[0] * gs[i]
+        qs[i] = restrict(u3, i, cc, i - 4) - jnp.minimum(slot_ref[0], 1.0) * gs[i]
     for i in range(5):
         core_cf[i] = cf[i, :, :C]
 
@@ -217,27 +241,45 @@
         out_ref[pl.ds(6 * K + 8 * j, 8), :] = both
 
 
-def put_q1(q3_ref, out_ref):
-    out_ref[pl.ds(0, 5 * K), :] = q3_ref[pl.ds(K, 5 * K), :]
+def put_q1(qs, q3_ref, out_ref):
+    for p, core in enumerate((q3_ref[pl.ds(K, K), :], join(qs, (5, 10))[:, :C], q3_ref[pl.ds(5 * K, K), :])):
+        out_ref[pl.ds(p * K, K), :] = core
     ends = [ends3(q3_ref, p) for p in range(1, 6)]
     at = lanes((8, C)) % SLOT
     both = shift(ends[3], 5)
     for k in (2, 1, 0):
         both = jnp.where(at < 4 * k + 4, shift(ends[k], 4 * k - 7), both)
-    out_ref[pl.ds(5 * K, 8), :] = both
-    out_ref[pl.ds(5 * K + 8, 8), :] = ends[4]
+    out_ref[pl.ds(3 * K, 8), :] = both
+    out_ref[pl.ds(3 * K + 8, 8), :] = ends[4]
+    inner = [pack_row(q3_ref[pl.ds(3 * K, K), :]), pack_row(join(qs, (6, 9))[:, :C])]
+    out_ref[pl.ds(3 * K + 16, 8), :] = jnp.where(at < H, shift(inner[0], -5), shift(inner[1], 4))
+
+
+def take_q1(in_ref, inner_ref, a):
+    def put(pair, at, value):
+        a[pair[0], :, at] = value
+        a[pair[1], :, at] = shift(value, -1)
+
+    core, side = pl.ds(0, C), pl.ds(C, C)
+    for p, pair in enumerate(PAIRS1):
+        packed = in_ref[pl.ds(3 * K + (8 if p == 4 else 0), 8), :]
+        put(pair, side, unpack_row(packed if p == 4 else shift(packed, 7 - 4 * p)))
+    for p, pair in enumerate(((3, 4), (5, 10), (11, 12))):
+        put(pair, core, in_ref[pl.ds(p * K, K), :])
+    lane = lanes((K, C))
+    inside = (lane >= 4) & (lane < C - 4)
+    packed = in_ref[pl.ds(3 * K + 16, 8), :]
+    for pair, by in (((7, 8), 5), ((6, 9), -4)):
+        ends = unpack_row(shift(packed, by))
+        for i, value in zip(pair, (ends, shift(ends, -1))):
+            a[i, :, core] = jnp.where(inside, inner_ref[i - 6], value)
 
 
 def take_q(in_ref, pairs, write):
     for p, (first, second) in enumerate(pairs):
         n = len(pairs)
         ends = lambda j: in_ref[pl.ds(n * K + 8 * j, 8), :]
-        if n == 7:
-            packed = ends(p)
-        elif n == 6:
-            packed = shift(ends(p % 3), 5 if p < 3 else -4)
-        else:
-            packed = shift(ends(0), 7 - 4 * p) if p < 4 else ends(1)
+        packed = ends(p) if n == 7 else shift(ends(p % 3), 5 if p < 3 else -4)
         both = jnp.concatenate([in_ref[pl.ds(p * K, K), :], unpack_row(packed)], axis=1)
         write(first, both)
         write(second, by_tile(lambda t: shift(t, -1), both))
@@ -268,15 +310,15 @@
 
 
 def outer_rows(
-    upper, later_ref, mk_ref, side_ref, fine_mix, coarse_mix, halo_ref, states, cc_out, mk, cf, cc
+    upper, slot_ref, mk_ref, side_ref, fine_mix, coarse_mix, halo_ref, states, cc_out, mk, cf, cc
 ):
     u0, u1, u2, u3, rs, gs, qs = states
     mk[...] = jnp.zeros_like(mk)
     first = 0 if upper else H + R
-    for i in range(H):
+    for i, ends in enumerate(corner_ends(halo_ref, not upper)):
         u0[first + i, :, :C] = halo_ref[pl.ds(i * K, K), :]
-        u0[first + i, :, C:] = unpack_row(halo_ref[pl.ds(H * K + 8 * i, 8), :])
-    at = H * K + 8 * H
+        u0[first + i, :, C:] = jnp.zeros((K, C), jnp.float32) if ends is None else unpack_row(ends)
+    at = H * K + 8 * HALF
     for j, ref, at, side, side_at in (
         (0 if upper else 2, halo_ref, at, halo_ref, at + 2 * R),
         (1, mk_ref, 0, side_ref, 8 * R),
@@ -299,35 +341,45 @@
     for i in mirror([1, 2, 3, 4]):
         gs[i] = step_row(rs, i, cc, i, 2, coarse_mix[...])
     for i in mirror([1, 2, 3, 4, 5]):
-        qs[i] = restrict(u3, i, cc, i) - later_ref[0] * gs[i]
+        qs[i] = restrict(u3, i, cc, i) - jnp.minimum(slot_ref[0], 1.0) * gs[i]
     half = pl.ds(0 if upper else NC // 2, NC // 2)
     for i in range(6):
         cc_out[i, half, :] = cc[i, half, :]
 
 
-def upper_kernel(*refs):
+FIRST_UPPER = False
+
+
+def first_side_kernel(*refs):
     *ins, mk, cf, cc = refs
     states, cc_out, q3_ref = ins[13:20], ins[20], ins[21]
-    outer_rows(True, *ins[:6], states, cc_out, mk, cf, cc)
-    put_q3(states[6], q3_ref, range(4))
-
-
-def lower_kernel(*refs):
+    outer_rows(FIRST_UPPER, *ins[:6], states, cc_out, mk, cf, cc)
+    put_q3(states[6], q3_ref, range(4) if FIRST_UPPER else range(3, 7))
+
+
+def second_side_kernel(*refs):
     *ins, mk, cf, cc = refs
     states, cc_out, q3_ref, q2_ref = ins[15:22], ins[22], ins[23], ins[24]
-    outer_rows(False, *ins[:6], states, cc_out, mk, cf, cc)
-    put_q3(states[6], q3_ref, range(4, 7))
+    outer_rows(not FIRST_UPPER, *ins[:6], states, cc_out, mk, cf, cc)
+    put_q3(states[6], q3_ref, range(4, 7) if FIRST_UPPER else range(3))
     put_q2(states[6], q3_ref, q2_ref)
 
 
-def near_message_kernel(u3, q3_ref, out_ref):
-    put_q1(q3_ref, out_ref)
+def near_message_kernel(u3, qs, q3_ref, out_ref):
+    put_q1(qs, q3_ref, out_ref)
     put_ring(u3, out_ref)
 
 
-def before_kernel(core_ref, fine_mix, cf_ref, u3, cc_ref, mk_ref, inner_ref, rest_ref, ua, ub):
+def before_kernel(
+    slot_ref, core_ref, fine_mix, coarse_mix, cf_ref, u3, cc_ref, mk_ref,
+    inner_ref, rest_ref, qi_ref, ua, ub, rs, cc,
+):
     for r in range(R):
         ua[r] = core_ref[pl.ds(r * K, K), :]
+    for i in range(6):
+        cc[i] = cc_ref[i, :, :C]
+    for i in range(R // 2):
+        rs[i] = block_mean((ua[2 * i], ua[2 * i + 1]), cc_ref, i)
     for margin, src, dst in ((1, ua, ub), (2, ub, ua), (3, ua, None)):
         for r in range(margin, R - margin):
             value = step_row(src, r, cf_ref, r, 1, fine_mix[...])
@@ -337,6 +389,10 @@
                 dst[r] = value
     for r in RING:
         inner_ref[pl.ds(r * K, K), :] = jnp.zeros((K, C), jnp.float32)
+    for i in range(2, 6):
+        pair = [inner_ref[pl.ds(r * K, K), :] for r in (2 * i, 2 * i + 1)]
+        g = step_row(rs, i, cc, 4 + i, 2, coarse_mix[...])
+        qi_ref[i - 2] = block_mean(pair, cc_ref, i) - jnp.clip(slot_ref[0] - 1.0, 0.0, 1.0) * g
     for i in range(R // 2):
         pair = [u3[H + r, :, :C] for r in (2 * i, 2 * i + 1)]
         fc = spread(block_mean(pair, cc_ref, i))
@@ -349,8 +405,8 @@
     return (total + shift(total, -1)) * cc_ref[5, 4 + i : 5 + i, :C]
 
 
-def near_kernel(q1_ref, inner_ref, cc_ref, mk_ref, a, base_ref):
-    take_q(q1_ref, PAIRS1, lambda i, value: a.__setitem__(i, value))
+def near_kernel(q1_ref, inner_ref, qi_ref, cc_ref, mk_ref, _, a, base_ref):
+    take_q1(q1_ref, qi_ref, a)
     rows = take_ring(q1_ref, inner_ref)
     for i in range(R // 2):
         pair = rows[2 * i], rows[2 * i + 1]
@@ -359,20 +415,20 @@
             base_ref[pl.ds(r * K, K), :] = value - mk_ref[pl.ds(r, 1), :] * fc
 
 
-def far_kernel(coarse_mix, cc_ref, q3_ref, _, b, a):
+def far_kernel(coarse_mix, cc_ref, q3_ref, b, a):
     take_q(q3_ref, PAIRS3, lambda i, value: a.__setitem__(i, value))
     for i in range(2, 14):
         b[i] = step_row(a, i, cc_ref, i, 2, coarse_mix[...])
 
 
 def last_kernel(
-    later_ref, mk_ref, coarse_mix, cc_ref, x_ref, far, near, q2_ref, qs, rest_ref, base_ref,
+    slot_ref, mk_ref, coarse_mix, cc_ref, x_ref, far, near, q2_ref, qs, rest_ref, base_ref,
     out_hbm, next_hbm, a, b, out_ref, next_ref, sems,
 ):
     take_q(q2_ref, PAIRS2, lambda i, value: b.__setitem__(i, far[i] + value))
     for i in range(3, 13):
         a[i] = near[i] + step_row(b, i, cc_ref, i, 2, coarse_mix[...])
-    first = later_ref[0] == 0.0
+    first = slot_ref[0] == 0.0
 
     def put(ref, from_ref, i, value):
         value = spread(value)
@@ -391,13 +447,22 @@
 
     next_copy = pltpu.make_async_copy(next_ref, next_hbm, sems.at[0])
     next_copy.start()
+    halves = []
     for i in range(R // 2):
         z = qs[4 + i] + step_row(a, 4 + i, cc_ref, 4 + i, 2, coarse_mix[...])
         put(out_ref, rest_ref, i, z[:, :C])
-    out_copy = pltpu.make_async_copy(out_ref, out_hbm, sems.at[1])
-    out_copy.start()
-    next_copy.wait()
-    out_copy.wait()
+        if i % 4 == 3:
+            rows = pl.ds(i // 4 * 8, 8)
+            halves.append(
+                pltpu.make_async_copy(
+                    out_ref.reshape(K, R, C).at[:, rows, :],
+                    out_hbm.reshape(K, R, C).at[:, rows, :],
+                    sems.at[1 + i // 4],
+                )
+            )
+            halves[-1].start()
+    for copy in (next_copy, *halves):
+        copy.wait()
 
 
 def f32(*shape):
@@ -408,7 +473,7 @@
     return pltpu.VMEM(shape, jnp.float32)
 
 
-def call(kernel, n_in, outs, scratches=(), smem=0, aliases=None, out_spec=VMEM):
+def call(kernel, n_in, outs, scratches=(), smem=0, aliases=None, out_spec=VMEM, cost=None):
     return pl.pallas_call(
         kernel,
         out_shape=outs,
@@ -416,6 +481,7 @@
         out_specs=jax.tree.map(lambda _: out_spec, outs),
         scratch_shapes=list(scratches),
         input_output_aliases=aliases or {},
+        cost_estimate=cost,
         compiler_params=pltpu.CompilerParams(vmem_limit_bytes=40 * 1024 * 1024),
     )
 
@@ -428,7 +494,7 @@
 
 def body(start, wet, kappa, mixing):
     x = start.reshape(K * R, C)
-    later = (lax.axis_index("tm") > 0).astype(jnp.float32).reshape(1)
+    slot = lax.axis_index("tm").astype(jnp.float32).reshape(1)
     mixing = mixing[None] * jnp.array([1.0, 3.0], jnp.float32)[:, None, None]
     lon = (R + 2) * 4
     left, right, core, mk = call(
@@ -454,41 +520,58 @@
         shapes + (f32(5, R, C),),
         [scratch(4, R, C), scratch(5, R, W), scratch(6, R // 2, W)],
         smem=1,
-    )(later, core, side, mk, fine_mix, coarse_mix)
+    )(slot, core, side, mk, fine_mix, coarse_mix)
     parts = [scratch(4, 48, C), scratch(5, 48, W), scratch(6, NC, W)]
     coefs = f32(6, NC, W)
     states = call(
-        upper_kernel,
+        first_side_kernel,
         13,
         shapes + (coefs, f32(Q3, C)),
         parts,
         smem=1,
         aliases={6 + i: i for i in range(7)},
-    )(later, mk, side, fine_mix, coarse_mix, up, *states)
+    )(slot, mk, side, fine_mix, coarse_mix, up if FIRST_UPPER else down, *states)
     *states, cc, q3, q2 = call(
-        lower_kernel,
+        second_side_kernel,
         15,
         shapes + (coefs, f32(Q3, C), f32(Q2, C)),
         parts,
         smem=1,
         aliases={6 + i: i for i in range(9)},
-    )(later, mk, side, fine_mix, coarse_mix, down, *states)
+    )(slot, mk, side, fine_mix, coarse_mix, down if FIRST_UPPER else up, *states)
     u3, qs = states[3], states[6]
-    q1 = call(near_message_kernel, 2, f32(Q1 + RG, C))(u3, q3)
+    q1 = call(
+        near_message_kernel,
+        3,
+        f32(Q1 + RG, C),
+        cost=pl.CostEstimate(flops=300 * 10**8, bytes_accessed=0, transcendentals=0),
+    )(u3, qs, q3)
     q3, q2, q1 = moved(q3, "tm", 3), moved(q2, "tm", 2), moved(q1, "tm", 1)
-    inner, rest = call(
-        before_kernel, 6, (f32(R * K, C), f32(R * K, C)), [scratch(R, K, C), scratch(R, K, C)]
-    )(before, fine_mix, cf, u3, cc, mk)
-    near, base = call(near_kernel, 4, (coarse, f32(R * K, C)))(q1, inner, cc, mk)
-    far = call(far_kernel, 4, coarse, [scratch(NC, K, W)])(coarse_mix, cc, q3, near)
+    inner, rest, inner_q = call(
+        before_kernel,
+        8,
+        (f32(R * K, C), f32(R * K, C), f32(4, K, C)),
+        [scratch(R, K, C), scratch(R, K, C), scratch(R // 2, K, C), scratch(6, NC, C)],
+        smem=1,
+    )(slot, before, fine_mix, coarse_mix, cf, u3, cc, mk)
+    far = call(
+        far_kernel,
+        3,
+        coarse,
+        [scratch(NC, K, W)],
+        cost=pl.CostEstimate(flops=20 * 10**8, bytes_accessed=0, transcendentals=0),
+    )(coarse_mix, cc, q3)
+    near, base = call(near_kernel, 6, (coarse, f32(R * K, C)))(
+        q1, inner, inner_q, cc, mk, far
+    )
     out, following = call(
         last_kernel,
         11,
         (f32(K * R, C), f32(K * R, C)),
-        [scratch(NC, K, W)] * 2 + [scratch(K * R, C)] * 2 + [pltpu.SemaphoreType.DMA((2,))],
+        [scratch(NC, K, W)] * 2 + [scratch(K * R, C)] * 2 + [pltpu.SemaphoreType.DMA((3,))],
         smem=1,
         out_spec=ANY,
-    )(later, mk, coarse_mix, cc, x, far, near, q2, qs, rest, base)
+    )(slot, mk, coarse_mix, cc, x, far, near, q2, qs, rest, base)
     return out.reshape(1, K, R, C), following.reshape(1, K, R, C)
 
 

time: 44 us -> 42.1 us (0.957)
  waiting for transfers between devices: 6.94 us -> 5.67 us
  starting transfers between devices: 23.3 us -> 22.5 us
    ppermute x8, waiting for transfers between devices: 6.94 us -> 5.67 us  [moved(): return lax.ppermute(value, axis, pairs)]
    ppermute x8, starting transfers between devices: 23.3 us -> 22.5 us  [moved(): return lax.ppermute(value, axis, pairs)]
  transfers between devices with their start and end apart: 8 -> 8, of which waited for: 4 -> 3; matrix products, arithmetic and copies ran while one was open for 2% -> 2% of each run, Pallas kernels for 18% -> 19%
where the time goes in v7:
time: 42.1 us; the launch traced here: 41.7 us
  starting transfers between devices  22.5 us (53%)
  Pallas kernels  10.2 us (24%)
  waiting for transfers between devices  5.67 us (13%)
  other arithmetic  1.54 us (4%)
  local copies, waits for them, and re-layouts  1 us (2%)
  between operations  0.78 us (2%)
    ppermute x8, starting transfers between devices, moved(): return lax.ppermute(value, axis, pairs)  22.5 us
    ppermute x8, waiting for transfers between devices, moved(): return lax.ppermute(value, axis, pairs)  5.67 us
    pallas_call x1, Pallas kernels, body(): call(last_kernel, 11, (f32(K * R, C), f32(K * R, C)), [scratch(NC, K, W)]...  1.9 us
    pallas_call x1, Pallas kernels, body(): call(own_kernel, 6, shapes + (f32(5, R, C),), [scratch(4, R, C), scratch(...  1.84 us
    pallas_call x1, Pallas kernels, body(): call(second_side_kernel, 15, shapes + (coefs, f32(Q3, C), f32(Q2, C)), pa...  1.65 us
    pallas_call x1, Pallas kernels, body(): call(first_side_kernel, 13, shapes + (coefs, f32(Q3, C)), parts, smem=1,...  1.64 us
    unnamed x4, local copies, waits for them, and re-layouts  1 us
    pallas_call x1, Pallas kernels, body(): call(before_kernel, 8, (f32(R * K, C), f32(R * K, C), f32(4, K, C)), [scr...  0.97 us
  transfers between devices with their start and end apart: 8, of which 3 were waited for; matrix products, arithmetic and copies ran while one was open for 2% of the time, Pallas kernels for 19%

profile of v7, /device:TPU:28, one launch (start us, length us, event | category | flops | bytes accessed | tf_op | source)
XLA Modules:
  0.0 41.7 jit_solution(13039561912621758393)
XLA Ops:
  0.6 0.7 %negate_select_fusion.signed_ref = f32[16,128]{1,0:T(8,128)S(1)} fusion(f32[16,128]{1,0:T(8,128)} %param.7, s32[16,128]{1,0:T(8,128)} %param.6), kind=kLoop, calls=%fused_computation.1 | loop fusion | flops 6144 | bytes 24576 | tf_op jit(solution)/shard_map/jit(_where)/select_n | solution.py:502
  1.4 1.0 %copy-done = f32[1,48,16,128]{3,2,1,0:T(8,128)S(1)} copy-done((f32[1,48,16,128]{3,2,1,0:T(8,128)S(1)}, f32[1,48,16,128]{3,2,1,0:T(8,128)}, u32[]{:S(2)}) %copy-start) | copy-done | bytes 393240
  2.3 0.3 shard_map.68
  2.6 8.5 %collective-permute-start.1 = (f32[72,128]{1,0:T(8,128)S(1)}, f32[72,128]{1,0:T(8,128)S(1)}, u32[]{:S(2)}, u32[]{:S(2)}) collective-permute-start(f32[72,128]{1,0:T(8,128)S(1)} %get-tuple-element.44), channel_id=1, source_target_pairs={{0,15},{1,0},{2,1},{3,2},{4,3},{5,4},{6,5},{7,6},{8,7},{9,8},{10,9... | collective-permute-start | bytes 110600 | tf_op jit(solution)/shard_map/ppermute | solution.py:492
  11.1 0.8 %broadcast_multiply_fusion.mix_ref = f32[2,48,48]{2,1,0:T(8,128)S(1)} fusion(f32[2]{0:T(128)} %constant.10.clone, f32[48,48]{1,0:T(8,128)} %param.8), kind=kLoop, calls=%fused_computation | loop fusion | flops 4608 | bytes 27656 | tf_op jit(solution)/shard_map/mul | solution.py:498
  12.0 0.8 %collective-permute-done.rl_ref = f32[72,128]{1,0:T(8,128)S(1)} collective-permute-done((f32[72,128]{1,0:T(8,128)S(1)}, f32[72,128]{1,0:T(8,128)S(1)}, u32[]{:S(2)}, u32[]{:S(2)}) %collective-permute-start) | collective-permute-done | bytes 36896 | tf_op jit(solution)/shard_map/ppermute | solution.py:492
  12.8 0.0 collective-permute-done.1.rr_ref
  12.8 0.2 shard_map.69
  12.9 2.4 %collective-permute-start.3 = (f32[504,128]{1,0:T(8,128)S(1)}, f32[504,128]{1,0:T(8,128)S(1)}, u32[]{:S(2)}, u32[]{:S(2)}) collective-permute-start(f32[504,128]{1,0:T(8,128)S(1)} %get-tuple-element.49), channel_id=1, source_target_pairs={{16,0},{32,16},{48,32},{64,48},{80,64},{96,80},{112,96},{17,1},{33... | collective-permute-start | bytes 774152 | tf_op jit(solution)/shard_map/ppermute | solution.py:492
  15.3 4.7 %collective-permute-start.2 = (f32[504,128]{1,0:T(8,128)S(1)}, f32[504,128]{1,0:T(8,128)S(1)}, u32[]{:S(2)}, u32[]{:S(2)}) collective-permute-start(f32[504,128]{1,0:T(8,128)S(1)} %get-tuple-element.48), channel_id=1, source_target_pairs={{0,16},{16,32},{32,48},{48,64},{64,80},{80,96},{96,112},{1,17},{17... | collective-permute-start | bytes 774152 | tf_op jit(solution)/shard_map/ppermute | solution.py:492
  20.0 3.1 %collective-permute-start.6 = (f32[768,128]{1,0:T(8,128)S(1)}, f32[768,128]{1,0:T(8,128)S(1)}, u32[]{:S(2)}, u32[]{:S(2)}) collective-permute-start(f32[768,128]{1,0:T(8,128)S(1)} %get-tuple-element.50.core_ref), channel_id=1, source_target_pairs={{0,128},{128,256},{256,384},{1,129},{129,257},{257,385},{2,130},{1... | collective-permute-start | bytes 1179656 | tf_op jit(solution)/shard_map/ppermute | solution.py:492
  23.1 1.8 %shard_map.70 = (f32[34,48,256]{2,1,0:T(8,128)S(1)}, f32[34,48,256]{2,1,0:T(8,128)S(1)}, f32[34,48,256]{2,1,0:T(8,128)S(1)}, f32[34,48,256]{2,1,0:T(8,128)S(1)},...) custom-call(f32[1]{0:T(128)} %bitcast.slot_ref.refs_0_, ...), custom_call_target="tpu_custom_call" | custom-call | tf_op jit(solution)/shard_map/pallas_call | solution.py:517
  25.0 1.6 %shard_map.71 = (f32[34,48,256]{2,1,0:T(8,128)S(1)}, f32[34,48,256]{2,1,0:T(8,128)S(1)}, f32[34,48,256]{2,1,0:T(8,128)S(1)}, f32[34,48,256]{2,1,0:T(8,128)S(1)},...) custom-call(f32[1]{0:T(128)} %bitcast.slot_ref.refs_0_, ...), custom_call_target="tpu_custom_call", output_to_operand_aliasing={{0}: (6, {}), {1}: (7, {}), {2}: (8, {}), {3}: (9, {}), {4}... | custom-call | tf_op jit(solution)/shard_map/pallas_call | solution.py:526
  26.6 1.6 %shard_map.72 = (f32[34,48,256]{2,1,0:T(8,128)S(1)}, f32[34,48,256]{2,1,0:T(8,128)S(1)}, f32[34,48,256]{2,1,0:T(8,128)S(1)}, f32[34,48,256]{2,1,0:T(8,128)S(1)},...) custom-call(f32[1]{0:T(128)} %bitcast.slot_ref.refs_0_, ...), custom_call_target="tpu_custom_call", output_to_operand_aliasing={{0}: (6, {}), {1}: (7, {}), {2}: (8, {}), {3}: (9, {}), {4}... | custom-call | tf_op jit(solution)/shard_map/pallas_call | solution.py:534
  28.3 0.7 %collective-permute-start.4 = (f32[392,128]{1,0:T(8,128)S(1)}, f32[392,128]{1,0:T(8,128)S(1)}, u32[]{:S(2)}, u32[]{:S(2)}) collective-permute-start(f32[392,128]{1,0:T(8,128)S(1)} %get-tuple-element.68.q3_ref), channel_id=1, source_target_pairs={{0,384},{1,385},{2,386},{3,387},{4,388},{5,389},{6,390},{7,391},{8... | collective-permute-start | bytes 602120 | tf_op jit(solution)/shard_map/ppermute | solution.py:492
  29.0 0.3 shard_map.74
  29.2 1.9 %collective-permute-start.5 = (f32[488,128]{1,0:T(8,128)S(1)}, f32[488,128]{1,0:T(8,128)S(1)}, u32[]{:S(2)}, u32[]{:S(2)}) collective-permute-start(f32[488,128]{1,0:T(8,128)S(1)} %shard_map.74), channel_id=1, source_target_pairs={{0,128},{128,256},{256,384},{1,129},{129,257},{257,385},{2,130},{1... | collective-permute-start | bytes 749576 | tf_op jit(solution)/shard_map/ppermute | solution.py:492
  31.1 1.3 %collective-permute-start.7 = (f32[312,128]{1,0:T(8,128)S(1)}, f32[312,128]{1,0:T(8,128)S(1)}, u32[]{:S(2)}, u32[]{:S(2)}) collective-permute-start(f32[312,128]{1,0:T(8,128)S(1)} %get-tuple-element.75), channel_id=1, source_target_pairs={{0,256},{128,384},{1,257},{129,385},{2,258},{130,386},{3,259},{131... | collective-permute-start | bytes 479240 | tf_op jit(solution)/shard_map/ppermute | solution.py:492
  32.5 1.0 %shard_map.75 = (f32[768,128]{1,0:T(8,128)S(1)}, f32[768,128]{1,0:T(8,128)S(1)}, f32[4,48,128]{2,1,0:T(8,128)S(1)}) custom-call(f32[1]{0:T(128)} %bitcast.slot_ref.refs_0_, f32[768,128]{1,0:T(8,128)S(1)} %collective-permute-done.6.core_ref, bf16[48,144]{1,0:T(8,128)(2,1)S(1)} %get-tuple-element.47.fine_mix.refs_3_, ...), custom_call_target="tpu_custom_call" | custom-call | tf_op jit(solution)/shard_map/pallas_call | solution.py:550
  33.4 0.7 %shard_map.73._.far = f32[16,48,256]{2,1,0:T(8,128)S(1)} custom-call(bf16[48,144]{1,0:T(8,128)(2,1)S(1)} %get-tuple-element.45.coarse_mix.refs_4_, f32[6,16,256]{2,1,0:T(8,128)S(1)} %get-tuple-element.67.cc_ref, f32[392,128]{1,0:T(8,128)S(1)} %collective-permute-done.4.q3_ref), custom_call_target="tpu_custom_call" | custom-call | flops 2000000000 | tf_op jit(solution)/shard_map/pallas_call | solution.py:557
  34.2 3.1 %collective-permute-done.5.q1_ref = f32[488,128]{1,0:T(8,128)S(1)} collective-permute-done((f32[488,128]{1,0:T(8,128)S(1)}, f32[488,128]{1,0:T(8,128)S(1)}, u32[]{:S(2)}, u32[]{:S(2)}) %collective-permute-start.5) | collective-permute-done | bytes 249888 | tf_op jit(solution)/shard_map/ppermute | solution.py:492
  37.4 0.7 %shard_map.76 = (f32[16,48,256]{2,1,0:T(8,128)S(1)}, f32[768,128]{1,0:T(8,128)S(1)}) custom-call(f32[488,128]{1,0:T(8,128)S(1)} %collective-permute-done.5.q1_ref, f32[768,128]{1,0:T(8,128)S(1)} %get-tuple-element.72.inner_ref, f32[4,48,128]{2,1,0:T(8,128)S(1)} %get-tuple-element.73.qi_ref, f32[6,16,256]{2,1,0:T(8,128)S(1)} %get-tuple-element.67.cc_ref, ...), custom_call_target="tpu_custom_call" | custom-call | tf_op jit(solution)/shard_map/pallas_call | solution.py:564
  38.1 1.7 %collective-permute-done.7.q2_ref = f32[312,128]{1,0:T(8,128)S(1)} collective-permute-done((f32[312,128]{1,0:T(8,128)S(1)}, f32[312,128]{1,0:T(8,128)S(1)}, u32[]{:S(2)}, u32[]{:S(2)}) %collective-permute-start.7) | collective-permute-done | bytes 159776 | tf_op jit(solution)/shard_map/ppermute | solution.py:492
  39.8 1.9 %shard_map.77 = (f32[768,128]{1,0:T(8,128)}, f32[768,128]{1,0:T(8,128)}) custom-call(f32[1]{0:T(128)} %bitcast.slot_ref.refs_0_, f32[32,128]{1,0:T(8,128)S(1)} %get-tuple-element.41.mk_ref.refs_1_, bf16[48,144]{1,0:T(8,128)(2,1)S(1)} %get-tuple-element.45.coarse_mix.refs_4_, f32[6,16,256]{2,1,0:T(8,128)S(1)} %get-tuple-element.67.cc_ref, ...), custom_call_target="tpu_custom_call" | custom-call | tf_op jit(solution)/shard_map/pallas_call | solution.py:567
  (8 shorter events, 0.0 us)
Async XLA Ops:
  1.3 1.0 %copy-start = (f32[1,48,16,128]{3,2,1,0:T(8,128)S(1)}, f32[1,48,16,128]{3,2,1,0:T(8,128)}, u32[]{:S(2)}) copy-start(f32[1,48,16,128]{3,2,1,0:T(8,128)} %param.5) | copy-start | bytes 1179652
  2.6 10.1 %collective-permute-start = (f32[72,128]{1,0:T(8,128)S(1)}, f32[72,128]{1,0:T(8,128)S(1)}, u32[]{:S(2)}, u32[]{:S(2)}) collective-permute-start(f32[72,128]{1,0:T(8,128)S(1)} %get-tuple-element.43), channel_id=1, source_target_pairs={{0,1},{1,2},{2,3},{3,4},{4,5},{5,6},{6,7},{7,8},{8,9},{9,10},{10,1... | collective-permute-start | bytes 110600 | tf_op jit(solution)/shard_map/ppermute | solution.py:492
  2.6 10.1 %collective-permute-start.1 = (f32[72,128]{1,0:T(8,128)S(1)}, f32[72,128]{1,0:T(8,128)S(1)}, u32[]{:S(2)}, u32[]{:S(2)}) collective-permute-start(f32[72,128]{1,0:T(8,128)S(1)} %get-tuple-element.44), channel_id=1, source_target_pairs={{0,15},{1,0},{2,1},{3,2},{4,3},{5,4},{6,5},{7,6},{8,7},{9,8},{10,9... | collective-permute-start | bytes 110600 | tf_op jit(solution)/shard_map/ppermute | solution.py:492
  12.9 12.0 %collective-permute-start.3 = (f32[504,128]{1,0:T(8,128)S(1)}, f32[504,128]{1,0:T(8,128)S(1)}, u32[]{:S(2)}, u32[]{:S(2)}) collective-permute-start(f32[504,128]{1,0:T(8,128)S(1)} %get-tuple-element.49), channel_id=1, source_target_pairs={{16,0},{32,16},{48,32},{64,48},{80,64},{96,80},{112,96},{17,1},{33... | collective-permute-start | bytes 774152 | tf_op jit(solution)/shard_map/ppermute | solution.py:492
  15.3 11.3 %collective-permute-start.2 = (f32[504,128]{1,0:T(8,128)S(1)}, f32[504,128]{1,0:T(8,128)S(1)}, u32[]{:S(2)}, u32[]{:S(2)}) collective-permute-start(f32[504,128]{1,0:T(8,128)S(1)} %get-tuple-element.48), channel_id=1, source_target_pairs={{0,16},{16,32},{32,48},{48,64},{64,80},{80,96},{96,112},{1,17},{17... | collective-permute-start | bytes 774152 | tf_op jit(solution)/shard_map/ppermute | solution.py:492
  20.0 12.4 %collective-permute-start.6 = (f32[768,128]{1,0:T(8,128)S(1)}, f32[768,128]{1,0:T(8,128)S(1)}, u32[]{:S(2)}, u32[]{:S(2)}) collective-permute-start(f32[768,128]{1,0:T(8,128)S(1)} %get-tuple-element.50.core_ref), channel_id=1, source_target_pairs={{0,128},{128,256},{256,384},{1,129},{129,257},{257,385},{2,130},{1... | collective-permute-start | bytes 1179656 | tf_op jit(solution)/shard_map/ppermute | solution.py:492
  28.3 5.2 %collective-permute-start.4 = (f32[392,128]{1,0:T(8,128)S(1)}, f32[392,128]{1,0:T(8,128)S(1)}, u32[]{:S(2)}, u32[]{:S(2)}) collective-permute-start(f32[392,128]{1,0:T(8,128)S(1)} %get-tuple-element.68.q3_ref), channel_id=1, source_target_pairs={{0,384},{1,385},{2,386},{3,387},{4,388},{5,389},{6,390},{7,391},{8... | collective-permute-start | bytes 602120 | tf_op jit(solution)/shard_map/ppermute | solution.py:492
  29.2 8.1 %collective-permute-start.5 = (f32[488,128]{1,0:T(8,128)S(1)}, f32[488,128]{1,0:T(8,128)S(1)}, u32[]{:S(2)}, u32[]{:S(2)}) collective-permute-start(f32[488,128]{1,0:T(8,128)S(1)} %shard_map.74), channel_id=1, source_target_pairs={{0,128},{128,256},{256,384},{1,129},{129,257},{257,385},{2,130},{1... | collective-permute-start | bytes 749576 | tf_op jit(solution)/shard_map/ppermute | solution.py:492
  31.1 8.7 %collective-permute-start.7 = (f32[312,128]{1,0:T(8,128)S(1)}, f32[312,128]{1,0:T(8,128)S(1)}, u32[]{:S(2)}, u32[]{:S(2)}) collective-permute-start(f32[312,128]{1,0:T(8,128)S(1)} %get-tuple-element.75), channel_id=1, source_target_pairs={{0,256},{128,384},{1,257},{129,385},{2,258},{130,386},{3,259},{131... | collective-permute-start | bytes 479240 | tf_op jit(solution)/shard_map/ppermute | solution.py:492
  34.2 5.6 %copy-start.1 = (f32[1,48,16,128]{3,2,1,0:T(8,128)S(1)}, f32[1,48,16,128]{3,2,1,0:T(8,128)}, u32[]{:S(2)}) copy-start(f32[1,48,16,128]{3,2,1,0:T(8,128)} %param.5) | copy-start | bytes 1179652

commit v8 on v7

--- a/solution.py
+++ b/solution.py
@@ -199,12 +199,20 @@
         def _(r):
             dst[H + r] = step_row(src, H + r, cf, r, 1, fine_mix[...])
 
-    for i in range(4, 12):
-        rs[i] = restrict(u0, i, cc, i - 4)
-    for i in range(5, 11):
-        gs[i] = step_row(rs, i, cc, i - 4, 2, coarse_mix[...])
-    for i in range(6, 10):
-        qs[i] = restrict(u3, i, cc, i - 4) - jnp.minimum(slot_ref[0], 1.0) * gs[i]
+    @pl.when(slot_ref[0] == 0.0)
+    def _():
+        for i in range(6, 10):
+            qs[i] = restrict(u3, i, cc, i - 4)
+
+    @pl.when(slot_ref[0] > 0.0)
+    def _():
+        for i in range(4, 12):
+            rs[i] = restrict(u0, i, cc, i - 4)
+        for i in range(5, 11):
+            gs[i] = step_row(rs, i, cc, i - 4, 2, coarse_mix[...])
+        for i in range(6, 10):
+            qs[i] = restrict(u3, i, cc, i - 4) - gs[i]
+
     for i in range(5):
         core_cf[i] = cf[i, :, :C]
 
@@ -328,20 +336,31 @@
             mk[2 * i, pl.ds(j * R, R), :] = ref[pl.ds(at + i * R, R), :]
             mk[2 * i + 1, pl.ds(j * R, R), :] = coefs[i * R : i * R + R]
     fine_coarse_coefficients(mk, R - 8, NC, cf, cc)
-    for margin, src, dst in ((1, u0, u1), (2, u1, u2), (3, u2, u3)):
-
-        @pl.loop(0, H, unroll=H)
-        def _(i):
-            r = margin + i if upper else E - 1 - margin - i
-            dst[r] = step_row(src, r, cf, r + BASE, 1, fine_mix[...])
-
     mirror = lambda rows: rows if upper else [NC - 1 - i for i in rows]
-    for i in mirror([0, 1, 2, 3]):
-        rs[i] = restrict(u0, i, cc, i)
-    for i in mirror([1, 2, 3, 4]):
-        gs[i] = step_row(rs, i, cc, i, 2, coarse_mix[...])
-    for i in mirror([1, 2, 3, 4, 5]):
-        qs[i] = restrict(u3, i, cc, i) - jnp.minimum(slot_ref[0], 1.0) * gs[i]
+
+    def rows_of(steps, wide, narrow, lowered):
+        for margin, src, dst in ((1, u0, u1), (2, u1, u2), (3, u2, u3)):
+
+            @pl.loop(*steps, unroll=steps[1] - steps[0])
+            def _(i):
+                r = margin + i if upper else E - 1 - margin - i
+                dst[r] = step_row(src, r, cf, r + BASE, 1, fine_mix[...])
+
+        for i in mirror(wide):
+            rs[i] = restrict(u0, i, cc, i)
+        for i in mirror(narrow):
+            gs[i] = step_row(rs, i, cc, i, 2, coarse_mix[...])
+        for i in mirror(lowered):
+            fc = restrict(u3, i, cc, i)
+            qs[i] = fc - gs[i] if narrow else fc
+
+    for k in range(4):
+
+        @pl.when(slot_ref[0] == float(k))
+        def _():
+            wide, narrow = ([*range(k - 1, 4)], [*range(k, 4)]) if k else ([], [])
+            rows_of((2 * k, H), wide, [i + 1 for i in narrow], [*range(k + 1, 6)])
+
     half = pl.ds(0 if upper else NC // 2, NC // 2)
     for i in range(6):
         cc_out[i, half, :] = cc[i, half, :]

time: 42.1 us -> 41.5 us (0.986)
  Pallas kernels: 10.2 us -> 9.55 us
  transfers between devices with their start and end apart: 8 -> 8, of which waited for: 3 -> 3; matrix products, arithmetic and copies ran while one was open for 2% -> 2% of each run, Pallas kernels for 19% -> 18%
where the time goes in v8:
time: 41.5 us; the launch traced here: 41.1 us
  starting transfers between devices  22.5 us (54%)
  Pallas kernels  9.55 us (23%)
  waiting for transfers between devices  5.67 us (14%)
  other arithmetic  1.54 us (4%)
  local copies, waits for them, and re-layouts  1 us (2%)
  between operations  0.78 us (2%)
    ppermute x8, starting transfers between devices, moved(): return lax.ppermute(value, axis, pairs)  22.5 us
    ppermute x8, waiting for transfers between devices, moved(): return lax.ppermute(value, axis, pairs)  5.67 us
    pallas_call x1, Pallas kernels, body(): call(own_kernel, 6, shapes + (f32(5, R, C),), [scratch(4, R, C), scratch(...  1.9 us
    pallas_call x1, Pallas kernels, body(): call(last_kernel, 11, (f32(K * R, C), f32(K * R, C)), [scratch(NC, K, W)]...  1.9 us
    pallas_call x1, Pallas kernels, body(): call(second_side_kernel, 15, shapes + (coefs, f32(Q3, C), f32(Q2, C)), pa...  1.31 us
    pallas_call x1, Pallas kernels, body(): call(first_side_kernel, 13, shapes + (coefs, f32(Q3, C)), parts, smem=1,...  1.28 us
    unnamed x4, local copies, waits for them, and re-layouts  1 us
    pallas_call x1, Pallas kernels, body(): call(before_kernel, 8, (f32(R * K, C), f32(R * K, C), f32(4, K, C)), [scr...  0.98 us
  transfers between devices with their start and end apart: 8, of which 3 were waited for; matrix products, arithmetic and copies ran while one was open for 2% of the time, Pallas kernels for 18%

profile of v8, /device:TPU:28, one launch (start us, length us, event | category | flops | bytes accessed | tf_op | source)
XLA Modules:
  0.0 41.1 jit_solution(10497447199113784335)
XLA Ops:
  0.6 0.7 %negate_select_fusion.signed_ref = f32[16,128]{1,0:T(8,128)S(1)} fusion(f32[16,128]{1,0:T(8,128)} %param.7, s32[16,128]{1,0:T(8,128)} %param.6), kind=kLoop, calls=%fused_computation.1 | loop fusion | flops 6144 | bytes 24576 | tf_op jit(solution)/shard_map/jit(_where)/select_n | solution.py:521
  1.4 1.0 %copy-done = f32[1,48,16,128]{3,2,1,0:T(8,128)S(1)} copy-done((f32[1,48,16,128]{3,2,1,0:T(8,128)S(1)}, f32[1,48,16,128]{3,2,1,0:T(8,128)}, u32[]{:S(2)}) %copy-start) | copy-done | bytes 393240
  2.3 0.3 shard_map.68
  2.6 8.5 %collective-permute-start.1 = (f32[72,128]{1,0:T(8,128)S(1)}, f32[72,128]{1,0:T(8,128)S(1)}, u32[]{:S(2)}, u32[]{:S(2)}) collective-permute-start(f32[72,128]{1,0:T(8,128)S(1)} %get-tuple-element.44), channel_id=1, source_target_pairs={{0,15},{1,0},{2,1},{3,2},{4,3},{5,4},{6,5},{7,6},{8,7},{9,8},{10,9... | collective-permute-start | bytes 110600 | tf_op jit(solution)/shard_map/ppermute | solution.py:511
  11.1 0.8 %broadcast_multiply_fusion.mix_ref = f32[2,48,48]{2,1,0:T(8,128)S(1)} fusion(f32[2]{0:T(128)} %constant.10.clone, f32[48,48]{1,0:T(8,128)} %param.8), kind=kLoop, calls=%fused_computation | loop fusion | flops 4608 | bytes 27656 | tf_op jit(solution)/shard_map/mul | solution.py:517
  12.0 0.8 %collective-permute-done.rl_ref = f32[72,128]{1,0:T(8,128)S(1)} collective-permute-done((f32[72,128]{1,0:T(8,128)S(1)}, f32[72,128]{1,0:T(8,128)S(1)}, u32[]{:S(2)}, u32[]{:S(2)}) %collective-permute-start) | collective-permute-done | bytes 36896 | tf_op jit(solution)/shard_map/ppermute | solution.py:511
  12.8 0.0 collective-permute-done.1.rr_ref
  12.8 0.2 shard_map.69
  12.9 2.4 %collective-permute-start.3 = (f32[504,128]{1,0:T(8,128)S(1)}, f32[504,128]{1,0:T(8,128)S(1)}, u32[]{:S(2)}, u32[]{:S(2)}) collective-permute-start(f32[504,128]{1,0:T(8,128)S(1)} %get-tuple-element.49), channel_id=1, source_target_pairs={{16,0},{32,16},{48,32},{64,48},{80,64},{96,80},{112,96},{17,1},{33... | collective-permute-start | bytes 774152 | tf_op jit(solution)/shard_map/ppermute | solution.py:511
  15.3 4.7 %collective-permute-start.2 = (f32[504,128]{1,0:T(8,128)S(1)}, f32[504,128]{1,0:T(8,128)S(1)}, u32[]{:S(2)}, u32[]{:S(2)}) collective-permute-start(f32[504,128]{1,0:T(8,128)S(1)} %get-tuple-element.48), channel_id=1, source_target_pairs={{0,16},{16,32},{32,48},{48,64},{64,80},{80,96},{96,112},{1,17},{17... | collective-permute-start | bytes 774152 | tf_op jit(solution)/shard_map/ppermute | solution.py:511
  20.0 3.1 %collective-permute-start.6 = (f32[768,128]{1,0:T(8,128)S(1)}, f32[768,128]{1,0:T(8,128)S(1)}, u32[]{:S(2)}, u32[]{:S(2)}) collective-permute-start(f32[768,128]{1,0:T(8,128)S(1)} %get-tuple-element.50.core_ref), channel_id=1, source_target_pairs={{0,128},{128,256},{256,384},{1,129},{129,257},{257,385},{2,130},{1... | collective-permute-start | bytes 1179656 | tf_op jit(solution)/shard_map/ppermute | solution.py:511
  23.1 1.9 %shard_map.70 = (f32[34,48,256]{2,1,0:T(8,128)S(1)}, f32[34,48,256]{2,1,0:T(8,128)S(1)}, f32[34,48,256]{2,1,0:T(8,128)S(1)}, f32[34,48,256]{2,1,0:T(8,128)S(1)},...) custom-call(f32[1]{0:T(128)} %bitcast.slot_ref.refs_0_, ...), custom_call_target="tpu_custom_call" | custom-call | tf_op jit(solution)/shard_map/pallas_call | solution.py:536
  25.0 1.3 %shard_map.71 = (f32[34,48,256]{2,1,0:T(8,128)S(1)}, f32[34,48,256]{2,1,0:T(8,128)S(1)}, f32[34,48,256]{2,1,0:T(8,128)S(1)}, f32[34,48,256]{2,1,0:T(8,128)S(1)},...) custom-call(f32[1]{0:T(128)} %bitcast.slot_ref.refs_0_, ...), custom_call_target="tpu_custom_call", output_to_operand_aliasing={{0}: (6, {}), {1}: (7, {}), {2}: (8, {}), {3}: (9, {}), {4}... | custom-call | tf_op jit(solution)/shard_map/pallas_call | solution.py:545
  26.3 1.3 %shard_map.72 = (f32[34,48,256]{2,1,0:T(8,128)S(1)}, f32[34,48,256]{2,1,0:T(8,128)S(1)}, f32[34,48,256]{2,1,0:T(8,128)S(1)}, f32[34,48,256]{2,1,0:T(8,128)S(1)},...) custom-call(f32[1]{0:T(128)} %bitcast.slot_ref.refs_0_, ...), custom_call_target="tpu_custom_call", output_to_operand_aliasing={{0}: (6, {}), {1}: (7, {}), {2}: (8, {}), {3}: (9, {}), {4}... | custom-call | tf_op jit(solution)/shard_map/pallas_call | solution.py:553
  27.7 0.7 %collective-permute-start.4 = (f32[392,128]{1,0:T(8,128)S(1)}, f32[392,128]{1,0:T(8,128)S(1)}, u32[]{:S(2)}, u32[]{:S(2)}) collective-permute-start(f32[392,128]{1,0:T(8,128)S(1)} %get-tuple-element.68.q3_ref), channel_id=1, source_target_pairs={{0,384},{1,385},{2,386},{3,387},{4,388},{5,389},{6,390},{7,391},{8... | collective-permute-start | bytes 602120 | tf_op jit(solution)/shard_map/ppermute | solution.py:511
  28.3 0.3 shard_map.74
  28.6 1.9 %collective-permute-start.5 = (f32[488,128]{1,0:T(8,128)S(1)}, f32[488,128]{1,0:T(8,128)S(1)}, u32[]{:S(2)}, u32[]{:S(2)}) collective-permute-start(f32[488,128]{1,0:T(8,128)S(1)} %shard_map.74), channel_id=1, source_target_pairs={{0,128},{128,256},{256,384},{1,129},{129,257},{257,385},{2,130},{1... | collective-permute-start | bytes 749576 | tf_op jit(solution)/shard_map/ppermute | solution.py:511
  30.5 1.3 %collective-permute-start.7 = (f32[312,128]{1,0:T(8,128)S(1)}, f32[312,128]{1,0:T(8,128)S(1)}, u32[]{:S(2)}, u32[]{:S(2)}) collective-permute-start(f32[312,128]{1,0:T(8,128)S(1)} %get-tuple-element.75), channel_id=1, source_target_pairs={{0,256},{128,384},{1,257},{129,385},{2,258},{130,386},{3,259},{131... | collective-permute-start | bytes 479240 | tf_op jit(solution)/shard_map/ppermute | solution.py:511
  31.8 1.0 %shard_map.75 = (f32[768,128]{1,0:T(8,128)S(1)}, f32[768,128]{1,0:T(8,128)S(1)}, f32[4,48,128]{2,1,0:T(8,128)S(1)}) custom-call(f32[1]{0:T(128)} %bitcast.slot_ref.refs_0_, f32[768,128]{1,0:T(8,128)S(1)} %collective-permute-done.6.core_ref, bf16[48,144]{1,0:T(8,128)(2,1)S(1)} %get-tuple-element.47.fine_mix.refs_3_, ...), custom_call_target="tpu_custom_call" | custom-call | tf_op jit(solution)/shard_map/pallas_call | solution.py:569
  32.8 0.7 %shard_map.73._.far = f32[16,48,256]{2,1,0:T(8,128)S(1)} custom-call(bf16[48,144]{1,0:T(8,128)(2,1)S(1)} %get-tuple-element.45.coarse_mix.refs_4_, f32[6,16,256]{2,1,0:T(8,128)S(1)} %get-tuple-element.67.cc_ref, f32[392,128]{1,0:T(8,128)S(1)} %collective-permute-done.4.q3_ref), custom_call_target="tpu_custom_call" | custom-call | flops 2000000000 | tf_op jit(solution)/shard_map/pallas_call | solution.py:576
  33.6 3.2 %collective-permute-done.5.q1_ref = f32[488,128]{1,0:T(8,128)S(1)} collective-permute-done((f32[488,128]{1,0:T(8,128)S(1)}, f32[488,128]{1,0:T(8,128)S(1)}, u32[]{:S(2)}, u32[]{:S(2)}) %collective-permute-start.5) | collective-permute-done | bytes 249888 | tf_op jit(solution)/shard_map/ppermute | solution.py:511
  36.7 0.7 %shard_map.76 = (f32[16,48,256]{2,1,0:T(8,128)S(1)}, f32[768,128]{1,0:T(8,128)S(1)}) custom-call(f32[488,128]{1,0:T(8,128)S(1)} %collective-permute-done.5.q1_ref, f32[768,128]{1,0:T(8,128)S(1)} %get-tuple-element.72.inner_ref, f32[4,48,128]{2,1,0:T(8,128)S(1)} %get-tuple-element.73.qi_ref, f32[6,16,256]{2,1,0:T(8,128)S(1)} %get-tuple-element.67.cc_ref, ...), custom_call_target="tpu_custom_call" | custom-call | tf_op jit(solution)/shard_map/pallas_call | solution.py:583
  37.5 1.7 %collective-permute-done.7.q2_ref = f32[312,128]{1,0:T(8,128)S(1)} collective-permute-done((f32[312,128]{1,0:T(8,128)S(1)}, f32[312,128]{1,0:T(8,128)S(1)}, u32[]{:S(2)}, u32[]{:S(2)}) %collective-permute-start.7) | collective-permute-done | bytes 159776 | tf_op jit(solution)/shard_map/ppermute | solution.py:511
  39.2 1.9 %shard_map.77 = (f32[768,128]{1,0:T(8,128)}, f32[768,128]{1,0:T(8,128)}) custom-call(f32[1]{0:T(128)} %bitcast.slot_ref.refs_0_, f32[32,128]{1,0:T(8,128)S(1)} %get-tuple-element.41.mk_ref.refs_1_, bf16[48,144]{1,0:T(8,128)(2,1)S(1)} %get-tuple-element.45.coarse_mix.refs_4_, f32[6,16,256]{2,1,0:T(8,128)S(1)} %get-tuple-element.67.cc_ref, ...), custom_call_target="tpu_custom_call" | custom-call | tf_op jit(solution)/shard_map/pallas_call | solution.py:586
  (8 shorter events, 0.0 us)
Async XLA Ops:
  1.3 1.0 %copy-start = (f32[1,48,16,128]{3,2,1,0:T(8,128)S(1)}, f32[1,48,16,128]{3,2,1,0:T(8,128)}, u32[]{:S(2)}) copy-start(f32[1,48,16,128]{3,2,1,0:T(8,128)} %param.5) | copy-start | bytes 1179652
  2.6 10.1 %collective-permute-start = (f32[72,128]{1,0:T(8,128)S(1)}, f32[72,128]{1,0:T(8,128)S(1)}, u32[]{:S(2)}, u32[]{:S(2)}) collective-permute-start(f32[72,128]{1,0:T(8,128)S(1)} %get-tuple-element.43), channel_id=1, source_target_pairs={{0,1},{1,2},{2,3},{3,4},{4,5},{5,6},{6,7},{7,8},{8,9},{9,10},{10,1... | collective-permute-start | bytes 110600 | tf_op jit(solution)/shard_map/ppermute | solution.py:511
  2.6 10.1 %collective-permute-start.1 = (f32[72,128]{1,0:T(8,128)S(1)}, f32[72,128]{1,0:T(8,128)S(1)}, u32[]{:S(2)}, u32[]{:S(2)}) collective-permute-start(f32[72,128]{1,0:T(8,128)S(1)} %get-tuple-element.44), channel_id=1, source_target_pairs={{0,15},{1,0},{2,1},{3,2},{4,3},{5,4},{6,5},{7,6},{8,7},{9,8},{10,9... | collective-permute-start | bytes 110600 | tf_op jit(solution)/shard_map/ppermute | solution.py:511
  12.9 12.1 %collective-permute-start.3 = (f32[504,128]{1,0:T(8,128)S(1)}, f32[504,128]{1,0:T(8,128)S(1)}, u32[]{:S(2)}, u32[]{:S(2)}) collective-permute-start(f32[504,128]{1,0:T(8,128)S(1)} %get-tuple-element.49), channel_id=1, source_target_pairs={{16,0},{32,16},{48,32},{64,48},{80,64},{96,80},{112,96},{17,1},{33... | collective-permute-start | bytes 774152 | tf_op jit(solution)/shard_map/ppermute | solution.py:511
  15.3 11.0 %collective-permute-start.2 = (f32[504,128]{1,0:T(8,128)S(1)}, f32[504,128]{1,0:T(8,128)S(1)}, u32[]{:S(2)}, u32[]{:S(2)}) collective-permute-start(f32[504,128]{1,0:T(8,128)S(1)} %get-tuple-element.48), channel_id=1, source_target_pairs={{0,16},{16,32},{32,48},{48,64},{64,80},{80,96},{96,112},{1,17},{17... | collective-permute-start | bytes 774152 | tf_op jit(solution)/shard_map/ppermute | solution.py:511
  20.0 11.8 %collective-permute-start.6 = (f32[768,128]{1,0:T(8,128)S(1)}, f32[768,128]{1,0:T(8,128)S(1)}, u32[]{:S(2)}, u32[]{:S(2)}) collective-permute-start(f32[768,128]{1,0:T(8,128)S(1)} %get-tuple-element.50.core_ref), channel_id=1, source_target_pairs={{0,128},{128,256},{256,384},{1,129},{129,257},{257,385},{2,130},{1... | collective-permute-start | bytes 1179656 | tf_op jit(solution)/shard_map/ppermute | solution.py:511
  27.7 5.1 %collective-permute-start.4 = (f32[392,128]{1,0:T(8,128)S(1)}, f32[392,128]{1,0:T(8,128)S(1)}, u32[]{:S(2)}, u32[]{:S(2)}) collective-permute-start(f32[392,128]{1,0:T(8,128)S(1)} %get-tuple-element.68.q3_ref), channel_id=1, source_target_pairs={{0,384},{1,385},{2,386},{3,387},{4,388},{5,389},{6,390},{7,391},{8... | collective-permute-start | bytes 602120 | tf_op jit(solution)/shard_map/ppermute | solution.py:511
  28.6 8.2 %collective-permute-start.5 = (f32[488,128]{1,0:T(8,128)S(1)}, f32[488,128]{1,0:T(8,128)S(1)}, u32[]{:S(2)}, u32[]{:S(2)}) collective-permute-start(f32[488,128]{1,0:T(8,128)S(1)} %shard_map.74), channel_id=1, source_target_pairs={{0,128},{128,256},{256,384},{1,129},{129,257},{257,385},{2,130},{1... | collective-permute-start | bytes 749576 | tf_op jit(solution)/shard_map/ppermute | solution.py:511
  30.5 8.7 %collective-permute-start.7 = (f32[312,128]{1,0:T(8,128)S(1)}, f32[312,128]{1,0:T(8,128)S(1)}, u32[]{:S(2)}, u32[]{:S(2)}) collective-permute-start(f32[312,128]{1,0:T(8,128)S(1)} %get-tuple-element.75), channel_id=1, source_target_pairs={{0,256},{128,384},{1,257},{129,385},{2,258},{130,386},{3,259},{131... | collective-permute-start | bytes 479240 | tf_op jit(solution)/shard_map/ppermute | solution.py:511
  33.6 5.6 %copy-start.1 = (f32[1,48,16,128]{3,2,1,0:T(8,128)S(1)}, f32[1,48,16,128]{3,2,1,0:T(8,128)}, u32[]{:S(2)}) copy-start(f32[1,48,16,128]{3,2,1,0:T(8,128)} %param.5) | copy-start | bytes 1179652

commit v9 on v8

--- a/solution.py
+++ b/solution.py
@@ -373,20 +373,28 @@
     *ins, mk, cf, cc = refs
     states, cc_out, q3_ref = ins[13:20], ins[20], ins[21]
     outer_rows(FIRST_UPPER, *ins[:6], states, cc_out, mk, cf, cc)
-    put_q3(states[6], q3_ref, range(4) if FIRST_UPPER else range(3, 7))
+
+    @pl.when(ins[0][0] < 3.0)
+    def _():
+        put_q3(states[6], q3_ref, range(4) if FIRST_UPPER else range(3, 7))
 
 
 def second_side_kernel(*refs):
     *ins, mk, cf, cc = refs
     states, cc_out, q3_ref, q2_ref = ins[15:22], ins[22], ins[23], ins[24]
     outer_rows(not FIRST_UPPER, *ins[:6], states, cc_out, mk, cf, cc)
-    put_q3(states[6], q3_ref, range(4, 7) if FIRST_UPPER else range(3))
-    put_q2(states[6], q3_ref, q2_ref)
-
-
-def near_message_kernel(u3, qs, q3_ref, out_ref):
-    put_q1(qs, q3_ref, out_ref)
-    put_ring(u3, out_ref)
+
+    @pl.when(ins[0][0] < 3.0)
+    def _():
+        put_q3(states[6], q3_ref, range(4, 7) if FIRST_UPPER else range(3))
+        put_q2(states[6], q3_ref, q2_ref)
+
+
+def near_message_kernel(slot_ref, u3, qs, q3_ref, out_ref):
+    @pl.when(slot_ref[0] < 3.0)
+    def _():
+        put_q1(qs, q3_ref, out_ref)
+        put_ring(u3, out_ref)
 
 
 def before_kernel(
@@ -561,10 +569,11 @@
     u3, qs = states[3], states[6]
     q1 = call(
         near_message_kernel,
-        3,
+        4,
         f32(Q1 + RG, C),
+        smem=1,
         cost=pl.CostEstimate(flops=300 * 10**8, bytes_accessed=0, transcendentals=0),
-    )(u3, qs, q3)
+    )(slot, u3, qs, q3)
     q3, q2, q1 = moved(q3, "tm", 3), moved(q2, "tm", 2), moved(q1, "tm", 1)
     inner, rest, inner_q = call(
         before_kernel,

time: 41.5 us -> 41.5 us (level)
  no operation moved by 1% of the time
where the time goes in v9:
time: 41.5 us; the launch traced here: 41.1 us
  starting transfers between devices  22.5 us (54%)
  Pallas kernels  9.57 us (23%)
  waiting for transfers between devices  5.65 us (14%)
  other arithmetic  1.54 us (4%)
  local copies, waits for them, and re-layouts  1 us (2%)
  between operations  0.78 us (2%)
    ppermute x8, starting transfers between devices, moved(): return lax.ppermute(value, axis, pairs)  22.5 us
    ppermute x8, waiting for transfers between devices, moved(): return lax.ppermute(value, axis, pairs)  5.65 us
    pallas_call x1, Pallas kernels, body(): call(own_kernel, 6, shapes + (f32(5, R, C),), [scratch(4, R, C), scratch(...  1.9 us
    pallas_call x1, Pallas kernels, body(): call(last_kernel, 11, (f32(K * R, C), f32(K * R, C)), [scratch(NC, K, W)]...  1.9 us
    pallas_call x1, Pallas kernels, body(): call(second_side_kernel, 15, shapes + (coefs, f32(Q3, C), f32(Q2, C)), pa...  1.32 us
    pallas_call x1, Pallas kernels, body(): call(first_side_kernel, 13, shapes + (coefs, f32(Q3, C)), parts, smem=1,...  1.28 us
    unnamed x4, local copies, waits for them, and re-layouts  1 us
    pallas_call x1, Pallas kernels, body(): call(before_kernel, 8, (f32(R * K, C), f32(R * K, C), f32(4, K, C)), [scr...  0.99 us
  transfers between devices with their start and end apart: 8, of which 3 were waited for; matrix products, arithmetic and copies ran while one was open for 2% of the time, Pallas kernels for 18%

profile of v9, /device:TPU:28, one launch (start us, length us, event | category | flops | bytes accessed | tf_op | source)
XLA Modules:
  0.0 41.1 jit_solution(7849336795155418098)
XLA Ops:
  0.6 0.7 %negate_select_fusion.signed_ref = f32[16,128]{1,0:T(8,128)S(1)} fusion(f32[16,128]{1,0:T(8,128)} %param.7, s32[16,128]{1,0:T(8,128)} %param.6), kind=kLoop, calls=%fused_computation.1 | loop fusion | flops 6144 | bytes 24576 | tf_op jit(solution)/shard_map/jit(_where)/select_n | solution.py:529
  1.4 1.0 %copy-done = f32[1,48,16,128]{3,2,1,0:T(8,128)S(1)} copy-done((f32[1,48,16,128]{3,2,1,0:T(8,128)S(1)}, f32[1,48,16,128]{3,2,1,0:T(8,128)}, u32[]{:S(2)}) %copy-start) | copy-done | bytes 393240
  2.3 0.3 shard_map.68
  2.6 8.5 %collective-permute-start.1 = (f32[72,128]{1,0:T(8,128)S(1)}, f32[72,128]{1,0:T(8,128)S(1)}, u32[]{:S(2)}, u32[]{:S(2)}) collective-permute-start(f32[72,128]{1,0:T(8,128)S(1)} %get-tuple-element.44), channel_id=1, source_target_pairs={{0,15},{1,0},{2,1},{3,2},{4,3},{5,4},{6,5},{7,6},{8,7},{9,8},{10,9... | collective-permute-start | bytes 110600 | tf_op jit(solution)/shard_map/ppermute | solution.py:519
  11.1 0.8 %broadcast_multiply_fusion.mix_ref = f32[2,48,48]{2,1,0:T(8,128)S(1)} fusion(f32[2]{0:T(128)} %constant.10.clone, f32[48,48]{1,0:T(8,128)} %param.8), kind=kLoop, calls=%fused_computation | loop fusion | flops 4608 | bytes 27656 | tf_op jit(solution)/shard_map/mul | solution.py:525
  12.0 0.8 %collective-permute-done.rl_ref = f32[72,128]{1,0:T(8,128)S(1)} collective-permute-done((f32[72,128]{1,0:T(8,128)S(1)}, f32[72,128]{1,0:T(8,128)S(1)}, u32[]{:S(2)}, u32[]{:S(2)}) %collective-permute-start) | collective-permute-done | bytes 36896 | tf_op jit(solution)/shard_map/ppermute | solution.py:519
  12.8 0.0 collective-permute-done.1.rr_ref
  12.8 0.2 shard_map.69
  12.9 2.4 %collective-permute-start.3 = (f32[504,128]{1,0:T(8,128)S(1)}, f32[504,128]{1,0:T(8,128)S(1)}, u32[]{:S(2)}, u32[]{:S(2)}) collective-permute-start(f32[504,128]{1,0:T(8,128)S(1)} %get-tuple-element.49), channel_id=1, source_target_pairs={{16,0},{32,16},{48,32},{64,48},{80,64},{96,80},{112,96},{17,1},{33... | collective-permute-start | bytes 774152 | tf_op jit(solution)/shard_map/ppermute | solution.py:519
  15.3 4.7 %collective-permute-start.2 = (f32[504,128]{1,0:T(8,128)S(1)}, f32[504,128]{1,0:T(8,128)S(1)}, u32[]{:S(2)}, u32[]{:S(2)}) collective-permute-start(f32[504,128]{1,0:T(8,128)S(1)} %get-tuple-element.48), channel_id=1, source_target_pairs={{0,16},{16,32},{32,48},{48,64},{64,80},{80,96},{96,112},{1,17},{17... | collective-permute-start | bytes 774152 | tf_op jit(solution)/shard_map/ppermute | solution.py:519
  20.0 3.1 %collective-permute-start.6 = (f32[768,128]{1,0:T(8,128)S(1)}, f32[768,128]{1,0:T(8,128)S(1)}, u32[]{:S(2)}, u32[]{:S(2)}) collective-permute-start(f32[768,128]{1,0:T(8,128)S(1)} %get-tuple-element.50.core_ref), channel_id=1, source_target_pairs={{0,128},{128,256},{256,384},{1,129},{129,257},{257,385},{2,130},{1... | collective-permute-start | bytes 1179656 | tf_op jit(solution)/shard_map/ppermute | solution.py:519
  23.1 1.9 %shard_map.70 = (f32[34,48,256]{2,1,0:T(8,128)S(1)}, f32[34,48,256]{2,1,0:T(8,128)S(1)}, f32[34,48,256]{2,1,0:T(8,128)S(1)}, f32[34,48,256]{2,1,0:T(8,128)S(1)},...) custom-call(f32[1]{0:T(128)} %bitcast.slot_ref.refs_0_, ...), custom_call_target="tpu_custom_call" | custom-call | tf_op jit(solution)/shard_map/pallas_call | solution.py:544
  25.0 1.3 %shard_map.71 = (f32[34,48,256]{2,1,0:T(8,128)S(1)}, f32[34,48,256]{2,1,0:T(8,128)S(1)}, f32[34,48,256]{2,1,0:T(8,128)S(1)}, f32[34,48,256]{2,1,0:T(8,128)S(1)},...) custom-call(f32[1]{0:T(128)} %bitcast.slot_ref.refs_0_, ...), custom_call_target="tpu_custom_call", output_to_operand_aliasing={{0}: (6, {}), {1}: (7, {}), {2}: (8, {}), {3}: (9, {}), {4}... | custom-call | tf_op jit(solution)/shard_map/pallas_call | solution.py:553
  26.3 1.3 %shard_map.72 = (f32[34,48,256]{2,1,0:T(8,128)S(1)}, f32[34,48,256]{2,1,0:T(8,128)S(1)}, f32[34,48,256]{2,1,0:T(8,128)S(1)}, f32[34,48,256]{2,1,0:T(8,128)S(1)},...) custom-call(f32[1]{0:T(128)} %bitcast.slot_ref.refs_0_, ...), custom_call_target="tpu_custom_call", output_to_operand_aliasing={{0}: (6, {}), {1}: (7, {}), {2}: (8, {}), {3}: (9, {}), {4}... | custom-call | tf_op jit(solution)/shard_map/pallas_call | solution.py:561
  27.7 0.7 %collective-permute-start.4 = (f32[392,128]{1,0:T(8,128)S(1)}, f32[392,128]{1,0:T(8,128)S(1)}, u32[]{:S(2)}, u32[]{:S(2)}) collective-permute-start(f32[392,128]{1,0:T(8,128)S(1)} %get-tuple-element.68.q3_ref), channel_id=1, source_target_pairs={{0,384},{1,385},{2,386},{3,387},{4,388},{5,389},{6,390},{7,391},{8... | collective-permute-start | bytes 602120 | tf_op jit(solution)/shard_map/ppermute | solution.py:519
  28.3 0.2 shard_map.74
  28.6 1.9 %collective-permute-start.5 = (f32[488,128]{1,0:T(8,128)S(1)}, f32[488,128]{1,0:T(8,128)S(1)}, u32[]{:S(2)}, u32[]{:S(2)}) collective-permute-start(f32[488,128]{1,0:T(8,128)S(1)} %shard_map.74), channel_id=1, source_target_pairs={{0,128},{128,256},{256,384},{1,129},{129,257},{257,385},{2,130},{1... | collective-permute-start | bytes 749576 | tf_op jit(solution)/shard_map/ppermute | solution.py:519
  30.5 1.3 %collective-permute-start.7 = (f32[312,128]{1,0:T(8,128)S(1)}, f32[312,128]{1,0:T(8,128)S(1)}, u32[]{:S(2)}, u32[]{:S(2)}) collective-permute-start(f32[312,128]{1,0:T(8,128)S(1)} %get-tuple-element.75), channel_id=1, source_target_pairs={{0,256},{128,384},{1,257},{129,385},{2,258},{130,386},{3,259},{131... | collective-permute-start | bytes 479240 | tf_op jit(solution)/shard_map/ppermute | solution.py:519
  31.8 1.0 %shard_map.75 = (f32[768,128]{1,0:T(8,128)S(1)}, f32[768,128]{1,0:T(8,128)S(1)}, f32[4,48,128]{2,1,0:T(8,128)S(1)}) custom-call(f32[1]{0:T(128)} %bitcast.slot_ref.refs_0_, f32[768,128]{1,0:T(8,128)S(1)} %collective-permute-done.6.core_ref, bf16[48,144]{1,0:T(8,128)(2,1)S(1)} %get-tuple-element.47.fine_mix.refs_3_, ...), custom_call_target="tpu_custom_call" | custom-call | tf_op jit(solution)/shard_map/pallas_call | solution.py:578
  32.8 0.7 %shard_map.73._.far = f32[16,48,256]{2,1,0:T(8,128)S(1)} custom-call(bf16[48,144]{1,0:T(8,128)(2,1)S(1)} %get-tuple-element.45.coarse_mix.refs_4_, f32[6,16,256]{2,1,0:T(8,128)S(1)} %get-tuple-element.67.cc_ref, f32[392,128]{1,0:T(8,128)S(1)} %collective-permute-done.4.q3_ref), custom_call_target="tpu_custom_call" | custom-call | flops 2000000000 | tf_op jit(solution)/shard_map/pallas_call | solution.py:585
  33.6 3.1 %collective-permute-done.5.q1_ref = f32[488,128]{1,0:T(8,128)S(1)} collective-permute-done((f32[488,128]{1,0:T(8,128)S(1)}, f32[488,128]{1,0:T(8,128)S(1)}, u32[]{:S(2)}, u32[]{:S(2)}) %collective-permute-start.5) | collective-permute-done | bytes 249888 | tf_op jit(solution)/shard_map/ppermute | solution.py:519
  36.7 0.7 %shard_map.76 = (f32[16,48,256]{2,1,0:T(8,128)S(1)}, f32[768,128]{1,0:T(8,128)S(1)}) custom-call(f32[488,128]{1,0:T(8,128)S(1)} %collective-permute-done.5.q1_ref, f32[768,128]{1,0:T(8,128)S(1)} %get-tuple-element.72.inner_ref, f32[4,48,128]{2,1,0:T(8,128)S(1)} %get-tuple-element.73.qi_ref, f32[6,16,256]{2,1,0:T(8,128)S(1)} %get-tuple-element.67.cc_ref, ...), custom_call_target="tpu_custom_call" | custom-call | tf_op jit(solution)/shard_map/pallas_call | solution.py:592
  37.5 1.7 %collective-permute-done.7.q2_ref = f32[312,128]{1,0:T(8,128)S(1)} collective-permute-done((f32[312,128]{1,0:T(8,128)S(1)}, f32[312,128]{1,0:T(8,128)S(1)}, u32[]{:S(2)}, u32[]{:S(2)}) %collective-permute-start.7) | collective-permute-done | bytes 159776 | tf_op jit(solution)/shard_map/ppermute | solution.py:519
  39.2 1.9 %shard_map.77 = (f32[768,128]{1,0:T(8,128)}, f32[768,128]{1,0:T(8,128)}) custom-call(f32[1]{0:T(128)} %bitcast.slot_ref.refs_0_, f32[32,128]{1,0:T(8,128)S(1)} %get-tuple-element.41.mk_ref.refs_1_, bf16[48,144]{1,0:T(8,128)(2,1)S(1)} %get-tuple-element.45.coarse_mix.refs_4_, f32[6,16,256]{2,1,0:T(8,128)S(1)} %get-tuple-element.67.cc_ref, ...), custom_call_target="tpu_custom_call" | custom-call | tf_op jit(solution)/shard_map/pallas_call | solution.py:595
  (8 shorter events, 0.0 us)
Async XLA Ops:
  1.3 1.0 %copy-start = (f32[1,48,16,128]{3,2,1,0:T(8,128)S(1)}, f32[1,48,16,128]{3,2,1,0:T(8,128)}, u32[]{:S(2)}) copy-start(f32[1,48,16,128]{3,2,1,0:T(8,128)} %param.5) | copy-start | bytes 1179652
  2.6 10.1 %collective-permute-start = (f32[72,128]{1,0:T(8,128)S(1)}, f32[72,128]{1,0:T(8,128)S(1)}, u32[]{:S(2)}, u32[]{:S(2)}) collective-permute-start(f32[72,128]{1,0:T(8,128)S(1)} %get-tuple-element.43), channel_id=1, source_target_pairs={{0,1},{1,2},{2,3},{3,4},{4,5},{5,6},{6,7},{7,8},{8,9},{9,10},{10,1... | collective-permute-start | bytes 110600 | tf_op jit(solution)/shard_map/ppermute | solution.py:519
  2.6 10.1 %collective-permute-start.1 = (f32[72,128]{1,0:T(8,128)S(1)}, f32[72,128]{1,0:T(8,128)S(1)}, u32[]{:S(2)}, u32[]{:S(2)}) collective-permute-start(f32[72,128]{1,0:T(8,128)S(1)} %get-tuple-element.44), channel_id=1, source_target_pairs={{0,15},{1,0},{2,1},{3,2},{4,3},{5,4},{6,5},{7,6},{8,7},{9,8},{10,9... | collective-permute-start | bytes 110600 | tf_op jit(solution)/shard_map/ppermute | solution.py:519
  12.9 12.1 %collective-permute-start.3 = (f32[504,128]{1,0:T(8,128)S(1)}, f32[504,128]{1,0:T(8,128)S(1)}, u32[]{:S(2)}, u32[]{:S(2)}) collective-permute-start(f32[504,128]{1,0:T(8,128)S(1)} %get-tuple-element.49), channel_id=1, source_target_pairs={{16,0},{32,16},{48,32},{64,48},{80,64},{96,80},{112,96},{17,1},{33... | collective-permute-start | bytes 774152 | tf_op jit(solution)/shard_map/ppermute | solution.py:519
  15.3 11.0 %collective-permute-start.2 = (f32[504,128]{1,0:T(8,128)S(1)}, f32[504,128]{1,0:T(8,128)S(1)}, u32[]{:S(2)}, u32[]{:S(2)}) collective-permute-start(f32[504,128]{1,0:T(8,128)S(1)} %get-tuple-element.48), channel_id=1, source_target_pairs={{0,16},{16,32},{32,48},{48,64},{64,80},{80,96},{96,112},{1,17},{17... | collective-permute-start | bytes 774152 | tf_op jit(solution)/shard_map/ppermute | solution.py:519
  20.0 11.8 %collective-permute-start.6 = (f32[768,128]{1,0:T(8,128)S(1)}, f32[768,128]{1,0:T(8,128)S(1)}, u32[]{:S(2)}, u32[]{:S(2)}) collective-permute-start(f32[768,128]{1,0:T(8,128)S(1)} %get-tuple-element.50.core_ref), channel_id=1, source_target_pairs={{0,128},{128,256},{256,384},{1,129},{129,257},{257,385},{2,130},{1... | collective-permute-start | bytes 1179656 | tf_op jit(solution)/shard_map/ppermute | solution.py:519
  27.7 5.2 %collective-permute-start.4 = (f32[392,128]{1,0:T(8,128)S(1)}, f32[392,128]{1,0:T(8,128)S(1)}, u32[]{:S(2)}, u32[]{:S(2)}) collective-permute-start(f32[392,128]{1,0:T(8,128)S(1)} %get-tuple-element.68.q3_ref), channel_id=1, source_target_pairs={{0,384},{1,385},{2,386},{3,387},{4,388},{5,389},{6,390},{7,391},{8... | collective-permute-start | bytes 602120 | tf_op jit(solution)/shard_map/ppermute | solution.py:519
  28.6 8.2 %collective-permute-start.5 = (f32[488,128]{1,0:T(8,128)S(1)}, f32[488,128]{1,0:T(8,128)S(1)}, u32[]{:S(2)}, u32[]{:S(2)}) collective-permute-start(f32[488,128]{1,0:T(8,128)S(1)} %shard_map.74), channel_id=1, source_target_pairs={{0,128},{128,256},{256,384},{1,129},{129,257},{257,385},{2,130},{1... | collective-permute-start | bytes 749576 | tf_op jit(solution)/shard_map/ppermute | solution.py:519
  30.5 8.7 %collective-permute-start.7 = (f32[312,128]{1,0:T(8,128)S(1)}, f32[312,128]{1,0:T(8,128)S(1)}, u32[]{:S(2)}, u32[]{:S(2)}) collective-permute-start(f32[312,128]{1,0:T(8,128)S(1)} %get-tuple-element.75), channel_id=1, source_target_pairs={{0,256},{128,384},{1,257},{129,385},{2,258},{130,386},{3,259},{131... | collective-permute-start | bytes 479240 | tf_op jit(solution)/shard_map/ppermute | solution.py:519
  33.6 5.6 %copy-start.1 = (f32[1,48,16,128]{3,2,1,0:T(8,128)S(1)}, f32[1,48,16,128]{3,2,1,0:T(8,128)}, u32[]{:S(2)}) copy-start(f32[1,48,16,128]{3,2,1,0:T(8,128)} %param.5) | copy-start | bytes 1179652
